TPU v7x, 128 devices: a whole 4x4x4 slice. The times are simulated.
128 devices in a mesh: layer: 2 (over x_lo), row: 8 (over x_hi, z), col: 8 (over y, core).
Axes of the slice: x: 4 (x_hi: 2, x_lo: 2; x = x_hi * 2 + x_lo), y: 4, z: 4, core: 2. Of those that a mesh axis runs over, the one named last changes fastest.
Arguments:
- grids: bfloat16 [4, 8192, 16384], P('layer', 'row', 'col'), may hold values from -6 to 6
- taper: float32 [8192], replicated, may hold values from 0.5 to 2
- w_steps: int32 [4], P('layer'), may hold values from -40 to 40
Outputs:
- image: float32 [8192, 8192], P(('layer', 'col'), 'row')
All inputs are finite; a program needn't handle non-finite values.
Results may differ from a plain program's by a relative error of at most 0.01.
Values may be sent and summed in bfloat16 or wider, within the bound.
No kernel may reach another device: no remote copies, remote signals or barrier semaphores. Data moves between devices by JAX's collectives and lax.ppermute only.
A program may use at most 192 MiB of HBM per device.

v0:
```python
import math

import jax
import jax.numpy as jnp
from jax import lax
from jax.sharding import PartitionSpec as P

RADIX = 128
INNER = 64


W_STEP = 1.0
TWO_PI = 2.0 * math.pi


def circle(product, count):
    angle = TWO_PI / count * (product % count).astype(jnp.float32)
    return (jnp.cos(angle), jnp.sin(angle))


def complex_table(cosine, sine):
    upper = jnp.stack([cosine, -sine])
    lower = jnp.stack([sine, cosine])
    return jnp.stack([upper, lower]).astype(jnp.bfloat16)


def on_device(grids, taper, w_steps):
    row_count = lax.axis_size("row")
    col_count = lax.axis_size("col")
    lay_count = lax.axis_size("layer")
    width = RADIX * INNER
    slab = width // (row_count * col_count)
    local = grids.shape[0]
    steps_a = jnp.arange(RADIX, dtype=jnp.int32)
    steps_b = jnp.arange(INNER, dtype=jnp.int32)
    turned = lax.all_to_all(grids, "col", split_axis=1, concat_axis=2, tiled=True)
    blocks = turned.reshape(local, slab, RADIX, 2 * INNER)
    cos_a, sin_a = circle(steps_a[:, None] * steps_a[None, :], RADIX)
    table_a = jnp.stack([cos_a, sin_a]).astype(jnp.bfloat16)
    both = jnp.einsum("xrak,sac->sxrck", blocks, table_a, preferred_element_type=jnp.float32)
    signs = jnp.concatenate([-jnp.ones((INNER,), jnp.float32), jnp.ones((INNER,), jnp.float32)])
    spun = both[0] + jnp.roll(both[1], INNER, axis=-1) * signs
    inner_pos = jnp.arange(2 * INNER, dtype=jnp.int32) % INNER
    tw_cos, tw_sin = circle(steps_a[:, None] * inner_pos[None, :], width)
    mixed = (spun * tw_cos + jnp.roll(spun, INNER, axis=-1) * signs * tw_sin).astype(jnp.bfloat16)
    cos_b, sin_b = circle(steps_b[:, None] * steps_b[None, :], INNER)
    top_half = jnp.concatenate([cos_b, sin_b], axis=1)
    low_half = jnp.concatenate([-sin_b, cos_b], axis=1)
    block_b = jnp.concatenate([top_half, low_half], axis=0).astype(jnp.bfloat16)
    half = jnp.einsum("xrck,kj->xrjc", mixed, block_b, preferred_element_type=jnp.float32)
    half = half.reshape(local, slab, 2, width).astype(jnp.bfloat16)
    spectra = lax.all_to_all(
        lax.all_to_all(half, "row", split_axis=3, concat_axis=1, tiled=True),
        "col",
        split_axis=3,
        concat_axis=1,
        tiled=True,
    )
    per_dev = RADIX // (row_count * col_count)
    low_part = steps_a % per_dev
    row_part = steps_a // per_dev % row_count
    col_part = steps_a // (per_dev * row_count)
    source_a = row_part * (col_count * per_dev) + col_part * per_dev + low_part
    spectra = spectra.reshape(local, RADIX, INNER, 2, slab)
    cos_u, sin_u = circle(source_a[:, None] * steps_a[None, :], RADIX)
    table_u = complex_table(cos_u, sin_u)
    turned_u = jnp.einsum("xabsm,tsac->xcbtm", spectra, table_u, preferred_element_type=jnp.float32)
    twc, tws = circle(steps_a[:, None] * steps_b[None, :], width)
    twc = twc[:, :, None]
    tws = tws[:, :, None]
    real_u = turned_u[:, :, :, 0]
    imag_u = turned_u[:, :, :, 1]
    mixed_u = jnp.stack([real_u * twc - imag_u * tws, real_u * tws + imag_u * twc], axis=3).astype(
        jnp.bfloat16
    )
    col_share = INNER // col_count
    lay_share = INNER // (lay_count * col_count)
    col_part = steps_b // col_share
    lay_part = steps_b // lay_share % lay_count
    low_part = steps_b % lay_share
    source_d = lay_part * (INNER // lay_count) + col_part * lay_share + low_part
    taper_rows = taper.reshape(lay_count, col_count, width // (lay_count * col_count))
    taper_rows = jnp.transpose(taper_rows, (1, 0, 2)).reshape(width)
    cos_d, sin_d = circle(steps_b[:, None] * source_d[None, :], INNER)
    table_d = complex_table(cos_d, sin_d)
    final = jnp.einsum("xcbsm,tsbd->xdctm", mixed_u, table_d, preferred_element_type=jnp.float32)
    final = final.reshape(local, width, 2, slab)
    row_index = (source_d[:, None] * RADIX + steps_a[None, :]).reshape(width)
    col_start = lax.axis_index("row") * (width // row_count) + lax.axis_index("col") * slab
    col_index = col_start + jnp.arange(slab, dtype=jnp.int32)
    across = (row_index.astype(jnp.float32) - width / 2) / width
    down = (col_index.astype(jnp.float32) - width / 2) / width
    height = jnp.sqrt(1.0 - across[:, None] * across[:, None] - down[None, :] * down[None, :])
    w_values = w_steps.astype(jnp.float32) * W_STEP
    phase = TWO_PI * w_values[:, None, None] * (height - 1.0)[None]
    summed = jnp.sum(jnp.cos(phase) * final[:, :, 0] - jnp.sin(phase) * final[:, :, 1], axis=0)
    taper_cols = lax.dynamic_slice_in_dim(taper, col_start, slab)
    summed = summed * (taper_rows[:, None] * taper_cols[None, :]) / width
    spread = lax.all_to_all(
        summed.astype(jnp.bfloat16), "col", split_axis=0, concat_axis=1, tiled=True
    ).astype(summed.dtype)
    result = lax.psum_scatter(
        spread.astype(jnp.bfloat16), "layer", scatter_dimension=0, tiled=True
    ).astype(jnp.float32)
    return result


def solution(mesh):
    placed = (P("layer", "row", "col"), P(), P("layer"))
    return jax.shard_map(
        on_device, mesh=mesh, in_specs=placed, out_specs=P(("layer", "col"), "row"), check_vma=False
    )
```

profile of v0, /device:TPU:0, one launch (start us, length us, event | category | flops | bytes accessed | tf_op | source)
XLA Modules:
  0.0 684.4 jit_solution(7480933078789368160)
XLA Ops:
  6.5 16.4 %copy.44 = bf16[2,1024,2048]{2,0,1:T(2,128)(2,1)} copy(bf16[2,1024,2048]{2,1,0:T(8,128)(2,1)} %param.3) | data formatting | bytes 16777216 | tf_op args[0]
  22.9 5.0 all-to-all-start
  28.8 93.7 %all-to-all-done = bf16[2,1024,2048]{2,0,1:T(2,128)(2,1)} async-done(((bf16[2,1024,2048]{2,0,1:T(2,128)(2,1)}), bf16[2,1024,2048]{2,0,1:T(2,128)(2,1)}, u32[]{:S(2)}, u32[]{:S(2)}) %all-to-all-start) | async-done | bytes 8388640 | tf_op jit(solution)/shard_map/all_to_all | solution.py:36
  122.5 10.5 %copy.45 = bf16[2,1024,2048]{2,1,0:T(8,128)(2,1)} copy(bf16[2,1024,2048]{2,0,1:T(2,128)(2,1)} %all-to-all-done) | data formatting | bytes 16777216 | tf_op jit(solution)/shard_map/all_to_all | solution.py:36
  133.0 11.8 %copy.46 = bf16[2,128,8,2048]{1,3,2,0:T(8,128)(2,1)} copy(bf16[2,128,8,2048]{3,1,2,0:T(8,128)(2,1)} %bitcast.96) | data formatting | bytes 16777216 | tf_op jit(solution)/shard_map/all_to_all | solution.py:36
  144.8 13.5 %copy.47 = bf16[2,128,128,128]{2,3,1,0:T(8,128)(2,1)} copy(bf16[2,128,128,128]{1,3,2,0:T(8,128)(2,1)} %bitcast.97) | data formatting | bytes 16777216 | tf_op jit(solution)/shard_map/reshape | solution.py:37
  158.3 18.9 %convolution_bitcast_fusion = f32[2,2,128,128,128]{3,4,2,1,0:T(8,128)} fusion(bf16[2,128,128,128]{2,3,1,0:T(8,128)(2,1)} %copy.47, bf16[1,128,128]{2,1,0:T(8,128)(2,1)S(1)} %get-tuple-element.23, bf16[1,128,128]{2,1,0:T(8,128)(2,1)S(1)} %get-tuple-element.24), kind=kOutput, calls=%fused_computation.8 | convolution fusion | flops 2147614720 | bytes 42008576 | tf_op jit(solution)/shard_map/xrak,sac->sxrck/dot_general | solution.py:40
  177.2 6.6 slice_bitcast_fusion
  183.8 6.6 fusion.102
  190.4 11.9 %fusion = f32[2,128,128,128]{2,3,1,0:T(8,128)S(1)} fusion(f32[2,2,128,128,128]{3,4,2,1,0:T(8,128)} %convolution_bitcast_fusion, f32[2,128,128,64]{2,3,1,0:T(8,128)} %get-tuple-element.10, f32[2,128,128,64]{2,3,1,0:T(8,128)} %get-tuple-element.9, f32[128]{0:T(128)S(1)} %copy-done.3), kind=kLoop, calls=%fused_computation.2 | loop fusion | flops 12582912 | bytes 50332160 | tf_op jit(solution)/shard_map/add | solution.py:42
  202.3 7.0 %fusion.101 = (f32[2,128,128,64]{2,3,1,0:T(8,128)}, f32[2,128,128,64]{2,3,1,0:T(8,128)}) fusion(f32[2,128,128,128]{2,3,1,0:T(8,128)S(1)} %fusion), kind=kLoop, calls=%fused_computation.170 | loop fusion | bytes 33554432 | tf_op jit(solution)/shard_map/jit(_roll_static)/slice | solution.py:45
  209.4 4.3 copy-done
  213.7 15.7 %convert_bitcast_fusion = bf16[2,128,128,128]{3,2,1,0:T(8,128)(2,1)} fusion(f32[2,128,128,64]{2,3,1,0:T(8,128)} %get-tuple-element.8, f32[2,128,128,64]{2,3,1,0:T(8,128)} %get-tuple-element.7, f32[2,128,128,128]{2,3,1,0:T(8,128)} %copy-done, f32[128,128]{0,1:T(8,128)S(1)} %get-tuple-element.22, f32[128,128]{0,1:T(8,128)S(1)} %get-tuple-element.21, ...), kind=kOutput, calls=%fused_computation.28 | convolution fusion | flops 1103233024 | bytes 42099200 | tf_op jit(solution)/shard_map/xrck,kj->xrjc/dot_general | solution.py:50
  229.4 12.5 %convert_element_type.156 = bf16[2,128,2,8192]{3,2,1,0:T(2,128)(2,1)} reshape(bf16[2,128,128,128]{3,2,1,0:T(8,128)(2,1)} %convert_bitcast_fusion) | data formatting | bytes 16777216 | tf_op jit(solution)/shard_map/convert_element_type | solution.py:51
  242.0 28.6 %copy.49 = bf16[2,128,2,8192]{1,2,0,3:T(2,128)(2,1)} copy(bf16[2,128,2,8192]{3,2,1,0:T(2,128)(2,1)} %convert_element_type.156) | data formatting | bytes 16777216 | tf_op jit(solution)/shard_map/convert_element_type | solution.py:51
  270.6 103.6 %all_to_all.64 = bf16[2,128,2,8192]{1,2,0,3:T(2,128)(2,1)} all-to-all(bf16[2,128,2,8192]{1,2,0,3:T(2,128)(2,1)} %copy.49), channel_id=1, replica_groups=mesh['layer'=2,'row'=8,'col'=8] {'row'}, dimensions={3} | all-to-all | bytes 16777216 | tf_op jit(solution)/shard_map/all_to_all | solution.py:53
  374.1 7.7 %copy.50 = bf16[2,128,2,8192]{1,3,2,0:T(8,128)(2,1)} copy(bf16[2,128,2,8192]{1,2,0,3:T(2,128)(2,1)} %all_to_all.64) | data formatting | bytes 16777216 | tf_op jit(solution)/shard_map/all_to_all | solution.py:53
  381.8 11.4 %copy.51 = bf16[2,8,128,2,1024]{4,2,1,3,0:T(8,128)(2,1)} copy(bf16[2,8,128,2,1024]{2,4,1,3,0:T(8,128)(2,1)} %bitcast.98) | data formatting | bytes 16777216 | tf_op jit(solution)/shard_map/all_to_all | solution.py:53
  393.2 21.4 %copy.52 = bf16[2,1024,2,1024]{1,2,0,3:T(2,128)(2,1)} copy(bf16[2,1024,2,1024]{3,1,2,0:T(8,128)(2,1)} %bitcast.99) | data formatting | bytes 16777216 | tf_op jit(solution)/shard_map/all_to_all | solution.py:53
  414.7 5.1 all-to-all-start.2
  420.8 4.9 sqrt_add_fusion
  425.7 88.7 %all-to-all-done.2 = bf16[2,1024,2,1024]{1,2,0,3:T(2,128)(2,1)} async-done(((bf16[2,1024,2,1024]{1,2,0,3:T(2,128)(2,1)}), bf16[2,1024,2,1024]{1,2,0,3:T(2,128)(2,1)}, u32[]{:S(2)}, u32[]{:S(2)}) %all-to-all-start.2) | async-done | bytes 8388640 | tf_op jit(solution)/shard_map/all_to_all | solution.py:52
  514.4 9.5 %copy.53 = bf16[2,1024,2,1024]{1,3,2,0:T(8,128)(2,1)} copy(bf16[2,1024,2,1024]{1,2,0,3:T(2,128)(2,1)} %all-to-all-done.2) | data formatting | bytes 16777216 | tf_op jit(solution)/shard_map/all_to_all | solution.py:52
  523.9 11.4 %copy.54 = bf16[2,8,1024,2,128]{4,2,1,3,0:T(8,128)(2,1)} copy(bf16[2,8,1024,2,128]{2,4,1,3,0:T(8,128)(2,1)} %bitcast.100) | data formatting | bytes 16777216 | tf_op jit(solution)/shard_map/all_to_all | solution.py:52
  535.2 9.4 %fusion.20 = f32[2,128,64,2,128]{4,1,2,0,3:T(8,128)S(1)} fusion(bf16[2,128,64,2,128]{4,2,1,3,0:T(8,128)(2,1)} %bitcast.95, bf16[1,2,128,128]{3,2,1,0:T(8,128)(2,1)S(1)} %get-tuple-element.12, bf16[1,2,128,128]{3,2,1,0:T(8,128)(2,1)S(1)} %get-tuple-element.11), kind=kOutput, calls=%fused_computation.32 | convolution fusion | flops 2147745792 | bytes 25296896 | tf_op jit(solution)/shard_map/xabsm,tsac->xcbtm/dot_general | solution.py:67
  544.7 4.7 subtract_convert_fusion
  549.4 6.2 pad_maximum_fusion
  555.6 9.7 %fusion.23 = f32[2,64,128,2,128]{4,1,2,0,3:T(8,128)S(1)} fusion(bf16[2,128,64,2,128]{4,1,2,0,3:T(8,128)(2,1)} %pad_maximum_fusion, bf16[1,2,64,64]{2,3,1,0:T(8,128)(2,1)S(1)} %get-tuple-element.14, bf16[1,2,64,64]{2,3,1,0:T(8,128)(2,1)S(1)} %get-tuple-element.13), kind=kOutput, calls=%fused_computation.33 | convolution fusion | flops 1073807360 | bytes 25198592 | tf_op jit(solution)/shard_map/xcbsm,tsbd->xdctm/dot_general | solution.py:86
  565.3 11.7 %copy.58 = f32[2,64,128,2,128]{4,2,1,3,0:T(8,128)} copy(f32[2,64,128,2,128]{4,1,2,0,3:T(8,128)S(1)} %fusion.23) | data formatting | bytes 33554432 | tf_op jit(solution)/shard_map/xcbsm,tsbd->xdctm/transpose | solution.py:86
  577.0 33.7 %fusion.6 = f32[8192,128]{1,0:T(8,128)S(1)} fusion(f32[2,8192,2,128]{3,1,2,0:T(8,128)} %bitcast.94, f32[8192,128]{1,0:T(8,128)S(1)} %copy-done.1, f32[2]{0:T(128)S(1)} %convert_multiply_fusion), kind=kLoop, calls=%fused_computation.13 | loop fusion | flops 9437184 | bytes 25165832 | tf_op jit(solution)/shard_map/reduce_sum | solution.py:96
  612.2 30.0 %all_to_all.65 = bf16[8,1024,128]{2,1,0:T(8,128)(2,1)S(1)} all-to-all(bf16[8,1024,128]{2,1,0:T(8,128)(2,1)S(1)} %multiply_convert_fusion), channel_id=1, replica_groups=mesh['layer'=2,'row'=8,'col'=8] {'col'}, dimensions={0} | all-to-all | bytes 4194304 | tf_op jit(solution)/shard_map/all_to_all | solution.py:99
  644.7 29.8 %reduce-scatter.2.cloned.1.call-done = bf16[512,1024]{0,1:T(8,128)(2,1)} async-done(((bf16[1024,1024]{0,1:T(8,128)(2,1)}), bf16[512,1024]{0,1:T(8,128)(2,1)}) %reduce-scatter.2.cloned.1.call-update) | async-done | bytes 1048592 | tf_op jit(solution)/shard_map/reduce_scatter | solution.py:102
  (32 shorter events, 8.5 us)
Async XLA Ops:
  22.9 99.6 %all-to-all-start = ((bf16[2,1024,2048]{2,0,1:T(2,128)(2,1)}), bf16[2,1024,2048]{2,0,1:T(2,128)(2,1)}, u32[]{:S(2)}, u32[]{:S(2)}) async-start(bf16[2,1024,2048]{2,0,1:T(2,128)(2,1)} %copy.44), calls=%async_computation | async-start | bytes 16777216 | tf_op jit(solution)/shard_map/all_to_all | solution.py:36
  183.8 6.6 copy-start.3
  202.3 11.4 %copy-start = (f32[2,128,128,128]{2,3,1,0:T(8,128)}, f32[2,128,128,128]{2,3,1,0:T(8,128)S(1)}, u32[]{:S(2)}) copy-start(f32[2,128,128,128]{2,3,1,0:T(8,128)S(1)} %fusion) | copy-start | bytes 50331652
  414.7 5.2 copy-start.2
  414.7 6.1 copy-start.4
  414.7 99.7 %all-to-all-start.2 = ((bf16[2,1024,2,1024]{1,2,0,3:T(2,128)(2,1)}), bf16[2,1024,2,1024]{1,2,0,3:T(2,128)(2,1)}, u32[]{:S(2)}, u32[]{:S(2)}) async-start(bf16[2,1024,2,1024]{1,2,0,3:T(2,128)(2,1)} %copy.52), calls=%async_computation.2 | async-start | bytes 16777216 | tf_op jit(solution)/shard_map/all_to_all | solution.py:52
  419.8 254.8 %reduce-scatter.2.cloned.1.call-start = ((), (), s32[]{:S(2)}) async-start(), calls=%async_computation.5 | async-start | bytes 3145728 | tf_op jit(solution)/shard_map/reduce_scatter | solution.py:102
  565.3 11.7 %copy-start.1 = (f32[8192,128]{1,0:T(8,128)S(1)}, f32[8192,128]{1,0:T(8,128)}, u32[]{:S(2)}) copy-start(f32[8192,128]{1,0:T(8,128)} %sqrt_add_fusion) | copy-start | bytes 12582916
Sparse Core Ops, SparseCore 0:
  644.9 29.6 reduce-scatter.1
where the time goes:
time: 697 us; the launch traced here: 684 us
  waiting for transfers between devices  212 us (30%)
  local copies, waits for them, and re-layouts  196 us (28%)
  blocking collectives  134 us (19%)
  other arithmetic  64.6 us (9%)
  matrix products  53.7 us (8%)
  between operations  14.1 us (2%)
  starting transfers between devices  10.1 us (1%)
    all_to_all x1, blocking collectives, on_device(): lax.all_to_all(half, 'row', split_axis=3, concat_axis=1, tiled=True)  104 us
    all_to_all x1, waiting for transfers between devices, on_device(): lax.all_to_all(grids, 'col', split_axis=1, concat_axis=2, tiled=True)  93.7 us
    all_to_all x1, waiting for transfers between devices, on_device(): lax.all_to_all(lax.all_to_all(half, 'row', split_axis=3, concat_axis=1, t...  88.7 us
    convert_element_type x2, local copies, waits for them, and re-layouts, on_device(): half = half.reshape(local, slab, 2, width).astype(jnp.bfloat16)  41.1 us
    all_to_all x3, local copies, waits for them, and re-layouts, on_device(): lax.all_to_all(half, 'row', split_axis=3, concat_axis=1, tiled=True)  40.5 us
    reduce_sum x1, other arithmetic, on_device(): jnp.sum(jnp.cos(phase) * final[:, :, 0] - jnp.sin(phase) * final[:, :, 1]...  33.7 us
    all_to_all x1, blocking collectives, on_device(): lax.all_to_all(summed.astype(jnp.bfloat16), 'col', split_axis=0, concat_a...  30 us
    reduce_scatter x1, waiting for transfers between devices, on_device(): lax.psum_scatter(spread.astype(jnp.bfloat16), 'layer', scatter_dimension=...  29.8 us
  transfers between devices with their start and end apart: 3, of which 3 were waited for; matrix products, arithmetic and copies ran while one was open for 1% of the time, Pallas kernels for 0%

commit v1 on v0

v1 whole, which is shorter than its diff:
```python
import functools
import math

import jax
import jax.numpy as jnp
import numpy as np
from jax import lax
from jax.experimental import pallas as pl
from jax.experimental.pallas import tpu as pltpu
from jax.sharding import PartitionSpec as P

INNER = 64
NPIX = 8192
LANES = 128
GROUP = 8
LAYERS_AXIS = 2
BLOCK = NPIX // GROUP
ROWS = BLOCK // GROUP
CELLS = NPIX // ROWS
HALF_ROOT = math.sqrt(0.5)
VMEM_LIMIT = 60 * 1024 * 1024

SIN_TERMS = tuple((-1.0) ** n * math.pi ** (2 * n + 1) / math.factorial(2 * n + 1) for n in range(7))
COS_TERMS = tuple((-1.0) ** n * math.pi ** (2 * n) / math.factorial(2 * n) for n in range(7))


def unit(product, count):
    angle = 2.0 * np.pi / count * (product % count).astype(np.float64)
    return np.cos(angle), np.sin(angle)


def spread_tables():
    cell = np.arange(BLOCK).reshape(BLOCK // INNER, 1, INNER)
    cell = np.broadcast_to(cell, (BLOCK // INNER, 2, INNER)).reshape(1, 2 * BLOCK)
    cosine, sine = unit(np.arange(GROUP)[:, None] * cell, NPIX)
    return cosine.astype(np.float32), sine.astype(np.float32)


def wide_table():
    cell = np.arange(BLOCK).reshape(BLOCK // INNER, INNER, 1, 1)
    freq = np.arange(BLOCK).reshape(1, 1, GROUP, LANES)
    cosine, sine = unit(cell * freq, BLOCK)
    upper = np.stack([cosine, sine], axis=3)
    lower = np.stack([-sine, cosine], axis=3)
    return np.stack([upper, lower], axis=1).reshape(2 * BLOCK, 2 * BLOCK).astype(jnp.bfloat16)


def short_table():
    steps = np.arange(ROWS)
    cosine, sine = unit(steps[:, None] * steps[None, :], ROWS)
    upper = np.concatenate([cosine, -sine], axis=1)
    lower = np.concatenate([sine, cosine], axis=1)
    return np.concatenate([upper, lower], axis=0).astype(jnp.bfloat16)


def row_tables():
    cosine, sine = unit(np.arange(ROWS)[:, None] * np.arange(CELLS)[None, :], NPIX)
    return cosine.astype(np.float32), sine.astype(np.float32)


def along_v_kernel(cells_ref, cos_ref, sin_ref, table_ref, out_ref, spun):
    @pl.when(pl.program_id(0) == 0)
    def _():
        lane = lax.broadcasted_iota(jnp.int32, (16, LANES), 1)
        sign = jnp.where(lane < INNER, -1.0, 1.0)

        def turn(z):
            return pltpu.roll(z, INNER, 1) * sign

        def one_tile(tile, carry):
            rows = pl.ds(pl.multiple_of(tile * 16, 16), 16)
            for a in range(2 * BLOCK // LANES):
                lanes = pl.ds(a * LANES, LANES)
                x = [cells_ref[c, rows, lanes].astype(jnp.float32) for c in range(GROUP)]
                e = [x[c] + x[c + 4] for c in range(4)]
                d = [x[c] - x[c + 4] for c in range(4)]
                even, odd = e[0] + e[2], e[1] + e[3]
                near, far = (d[1] - d[3]) * HALF_ROOT, (d[1] + d[3]) * HALF_ROOT

                def put(j, z):
                    spun[j, rows, lanes] = z.astype(jnp.bfloat16)

                put(0, even + odd)
                z = even - odd
                put(4, z * cos_ref[4:5, lanes] + turn(z) * sin_ref[4:5, lanes])
                for j, p, q in ((2, e[0] - e[2], e[1] - e[3]), (1, d[0] + near, d[2] + far), (3, d[0] - near, far - d[2])):
                    jp, jq = turn(p), turn(q)
                    put(j, (p + jq) * cos_ref[j : j + 1, lanes] + (jp - q) * sin_ref[j : j + 1, lanes])
                    o = GROUP - j
                    put(o, (p - jq) * cos_ref[o : o + 1, lanes] + (jp + q) * sin_ref[o : o + 1, lanes])
            return carry

        lax.fori_loop(0, ROWS // 16, one_tile, 0)

    for j in range(GROUP):
        res = jnp.dot(spun[j], table_ref[...], preferred_element_type=jnp.float32)
        out_ref[0, j, 0] = res[:, :LANES].astype(jnp.bfloat16)
        out_ref[0, j, 1] = res[:, LANES:].astype(jnp.bfloat16)


def along_v(cells):
    tw_cos, tw_sin = spread_tables()
    whole = lambda *shape: pl.BlockSpec(shape, lambda s: (0,) * len(shape))
    return pl.pallas_call(
        along_v_kernel,
        grid=(GROUP,),
        out_shape=jax.ShapeDtypeStruct((GROUP, GROUP, 2, ROWS, LANES), jnp.bfloat16),
        in_specs=[
            whole(GROUP, ROWS, 2 * BLOCK),
            whole(GROUP, 2 * BLOCK),
            whole(GROUP, 2 * BLOCK),
            pl.BlockSpec((2 * BLOCK, 2 * LANES), lambda s: (0, s)),
        ],
        out_specs=pl.BlockSpec((1, GROUP, 2, ROWS, LANES), lambda s: (s, 0, 0, 0, 0)),
        scratch_shapes=[pltpu.VMEM((GROUP, ROWS, 2 * BLOCK), jnp.bfloat16)],
        compiler_params=pltpu.CompilerParams(vmem_limit_bytes=VMEM_LIMIT),
        cost_estimate=pl.CostEstimate(flops=2 * 1024 * 2048 * 2048, bytes_accessed=16 << 20, transcendentals=0),
        name="along_v",
    )(cells, jnp.asarray(tw_cos), jnp.asarray(tw_sin), jnp.asarray(wide_table()))


def eight(xr, xi):
    er = [xr[c] + xr[c + 4] for c in range(4)]
    ei = [xi[c] + xi[c + 4] for c in range(4)]
    dr = [xr[c] - xr[c + 4] for c in range(4)]
    di = [xi[c] - xi[c + 4] for c in range(4)]
    evr, evi, odr, odi = er[0] + er[2], ei[0] + ei[2], er[1] + er[3], ei[1] + ei[3]
    nr, ni = (dr[1] - dr[3]) * HALF_ROOT, (di[1] - di[3]) * HALF_ROOT
    fr, fi = (dr[1] + dr[3]) * HALF_ROOT, (di[1] + di[3]) * HALF_ROOT
    outr, outi = [None] * 8, [None] * 8
    outr[0], outi[0] = evr + odr, evi + odi
    outr[4], outi[4] = evr - odr, evi - odi
    pairs = (
        (2, er[0] - er[2], ei[0] - ei[2], er[1] - er[3], ei[1] - ei[3]),
        (1, dr[0] + nr, di[0] + ni, dr[2] + fr, di[2] + fi),
        (3, dr[0] - nr, di[0] - ni, fr - dr[2], fi - di[2]),
    )
    for j, pr, pi, qr, qi in pairs:
        outr[j], outi[j] = pr - qi, pi + qr
        outr[8 - j], outi[8 - j] = pr + qi, pi - qr
    return outr, outi


def along_u_kernel(first, last, place_ref, w_ref, cells_ref, cos_ref, sin_ref, table_ref, *rest):
    if first:
        out_ref, mid, spun = rest
    else:
        sofar_ref, out_ref, mid, spun = rest
    step = pl.program_id(0)
    tiles = ROWS // 16

    @pl.when(step < tiles)
    def _():
        for c in range(GROUP):
            xr = [cells_ref[GROUP * r + c, 0].astype(jnp.float32) for r in range(GROUP)]
            xi = [cells_ref[GROUP * r + c, 1].astype(jnp.float32) for r in range(GROUP)]
            yr, yi = eight(xr, xi)
            for i in range(GROUP):
                wr, wi = math.cos(2 * math.pi * c * i / CELLS), math.sin(2 * math.pi * c * i / CELLS)
                if c * i == 0:
                    mid[i, c, 0], mid[i, c, 1] = yr[i], yi[i]
                else:
                    mid[i, c, 0] = yr[i] * wr - yi[i] * wi
                    mid[i, c, 1] = yr[i] * wi + yi[i] * wr
        rows = pl.ds(pl.multiple_of(step * 16, 16), 16)
        lower = pl.ds(pl.multiple_of(ROWS + step * 16, 16), 16)
        for i1 in range(GROUP):
            yr, yi = eight([mid[i1, c, 0] for c in range(GROUP)], [mid[i1, c, 1] for c in range(GROUP)])
            for i2 in range(GROUP):
                i = i1 + GROUP * i2
                tc, ts = cos_ref[:, i : i + 1], sin_ref[:, i : i + 1]
                lanes = slice(i * LANES, (i + 1) * LANES)
                spun[rows, lanes] = (yr[i2] * tc - yi[i2] * ts).astype(jnp.bfloat16)
                spun[lower, lanes] = (yr[i2] * ts + yi[i2] * tc).astype(jnp.bfloat16)

    @pl.when(step >= tiles)
    def _():
        block = step - tiles
        lanes = pl.ds(pl.multiple_of(block * GROUP * LANES, LANES), GROUP * LANES)
        full = jnp.dot(table_ref[...], spun[:, lanes], preferred_element_type=jnp.float32)
        shape = (ROWS, LANES)
        g = lax.broadcasted_iota(jnp.int32, shape, 0)
        q = lax.broadcasted_iota(jnp.int32, shape, 1)
        m = place_ref[0] + GROUP * q
        down = (m.astype(jnp.float32) - NPIX / 2) / NPIX
        rest_down = 1.0 - down * down
        w_value = w_ref[0].astype(jnp.float32)
        images = []
        for n in range(GROUP):
            l = CELLS * g + (block * GROUP + n)
            across = (l.astype(jnp.float32) - NPIX / 2) / NPIX
            turns = w_value * (jnp.sqrt(rest_down - across * across) - 1.0)
            t = turns - jnp.floor(turns + 0.5)
            t2 = t * t
            sine, cosine = SIN_TERMS[-1], COS_TERMS[-1]
            for a, b in zip(SIN_TERMS[-2::-1], COS_TERMS[-2::-1]):
                sine, cosine = sine * t2 + a, cosine * t2 + b
            sine = sine * t
            real = full[:ROWS, n * LANES : (n + 1) * LANES]
            imag = full[ROWS:, n * LANES : (n + 1) * LANES]
            image = real - 2.0 * sine * (sine * real + cosine * imag)
            if not first:
                image = image + sofar_ref[:, n * LANES : (n + 1) * LANES]
            images.append(image)
        if not last:
            for n in range(GROUP):
                out_ref[:, n * LANES : (n + 1) * LANES] = images[n]
        else:
            for n in range(0, GROUP, 2):
                pair = [z.reshape(ROWS // 8, 8, LANES) for z in images[n : n + 2]]
                both = jnp.concatenate(pair, axis=1).astype(jnp.bfloat16)
                out_ref[:, 8 * n : 8 * n + 16, :] = both


def along_u(cells, place, w_value, sofar, last):
    first = sofar is None
    tiles = ROWS // 16
    tw_cos, tw_sin = row_tables()
    late = lambda s: jnp.maximum(s - tiles, 0)
    early = lambda s: jnp.minimum(s, tiles - 1)
    smem = pl.BlockSpec(memory_space=pltpu.SMEM)
    in_specs = [
        smem,
        smem,
        pl.BlockSpec((CELLS, 2, 16, LANES), lambda s: (0, 0, early(s), 0)),
        pl.BlockSpec((16, CELLS), lambda s: (early(s), 0)),
        pl.BlockSpec((16, CELLS), lambda s: (early(s), 0)),
        pl.BlockSpec((2 * ROWS, 2 * ROWS), lambda s: (0, 0)),
    ]
    args = [place, w_value, cells, jnp.asarray(tw_cos), jnp.asarray(tw_sin), jnp.asarray(short_table())]
    if not first:
        in_specs.append(pl.BlockSpec((ROWS, GROUP * LANES), lambda s: (0, late(s))))
        args.append(sofar)
    if last:
        out_shape = jax.ShapeDtypeStruct((ROWS // 8, 8 * CELLS, LANES), jnp.bfloat16)
        out_spec = pl.BlockSpec((ROWS // 8, 8 * GROUP, LANES), lambda s: (0, late(s), 0))
    else:
        out_shape = jax.ShapeDtypeStruct((ROWS, CELLS * LANES), jnp.float32)
        out_spec = pl.BlockSpec((ROWS, GROUP * LANES), lambda s: (0, late(s)))
    return pl.pallas_call(
        functools.partial(along_u_kernel, first, last),
        grid=(tiles + CELLS // GROUP,),
        out_shape=out_shape,
        in_specs=in_specs,
        out_specs=out_spec,
        scratch_shapes=[
            pltpu.VMEM((GROUP, GROUP, 2, 16, LANES), jnp.float32),
            pltpu.VMEM((2 * ROWS, CELLS * LANES), jnp.bfloat16),
        ],
        compiler_params=pltpu.CompilerParams(vmem_limit_bytes=VMEM_LIMIT),
        cost_estimate=pl.CostEstimate(flops=2 * 256 * 256 * 8192, bytes_accessed=8 << 20, transcendentals=0),
        name="along_u",
    )(*args)


def arrange_kernel(cells_ref, rows_ref, cols_ref, out_ref):
    count = 8 * CELLS
    total = None
    q = lax.broadcasted_iota(jnp.int32, (LANES, BLOCK), 0)
    m = lax.broadcasted_iota(jnp.int32, (LANES, BLOCK), 1)
    for j in range(GROUP):
        pick = jnp.where(m == GROUP * q + j, 1.0, 0.0).astype(jnp.bfloat16)
        part = jnp.dot(cells_ref[j], pick, preferred_element_type=jnp.float32)
        total = part if total is None else total + part
    l = lax.broadcasted_iota(jnp.int32, (count, count), 0)
    held = lax.broadcasted_iota(jnp.int32, (count, count), 1)
    pick = jnp.where(held == 8 * (l % CELLS) + l // CELLS, 1.0, 0.0).astype(jnp.bfloat16)
    total = jnp.dot(pick, total.astype(jnp.bfloat16), preferred_element_type=jnp.float32)
    out_ref[...] = total * (rows_ref[...] * cols_ref[...]) / NPIX


def arrange(cells, taper_rows, taper_cols):
    vmem = pl.BlockSpec(memory_space=pltpu.VMEM)
    return pl.pallas_call(
        arrange_kernel,
        out_shape=jax.ShapeDtypeStruct((8 * CELLS, BLOCK), jnp.float32),
        in_specs=[vmem] * 3,
        out_specs=vmem,
        compiler_params=pltpu.CompilerParams(vmem_limit_bytes=VMEM_LIMIT),
        name="arrange",
    )(cells, taper_rows, taper_cols)


def on_device(grids, taper, w_steps):
    lay, row, col = lax.axis_index("layer"), lax.axis_index("row"), lax.axis_index("col")
    local = grids.shape[0]
    place = (BLOCK * row + col).astype(jnp.int32).reshape(1)
    taper_cols = lax.dynamic_slice_in_dim(taper, BLOCK * row, BLOCK).reshape(1, BLOCK)
    taper_rows = lax.dynamic_slice_in_dim(taper, 8 * CELLS * (GROUP * lay + col), 8 * CELLS).reshape(8 * CELLS, 1)
    image = None
    for k in range(local):
        cells = lax.all_to_all(
            grids[k].reshape(GROUP, ROWS, 2 * BLOCK), "col", split_axis=0, concat_axis=0, tiled=True
        )
        half = along_v(cells).reshape(GROUP * GROUP, 2, ROWS, LANES)
        half = lax.all_to_all(half, ("row", "col"), split_axis=0, concat_axis=0, tiled=True)
        image = along_u(half, place, w_steps[k : k + 1], image, k == local - 1)
    image = image.reshape(LAYERS_AXIS, GROUP, 8 * CELLS, LANES)
    keep = lax.dynamic_index_in_dim(image, lay, 0, keepdims=False)
    send = lax.dynamic_index_in_dim(image, 1 - lay, 0, keepdims=False)
    other = lax.ppermute(send, "layer", [(0, 1), (1, 0)])
    summed = (keep.astype(jnp.float32) + other.astype(jnp.float32)).astype(jnp.bfloat16)
    tiles = lax.all_to_all(summed, "col", split_axis=0, concat_axis=0, tiled=True)
    return arrange(tiles, taper_rows, taper_cols)


def solution(mesh):
    placed = (P("layer", "row", "col"), P(), P("layer"))
    return jax.shard_map(
        on_device, mesh=mesh, in_specs=placed, out_specs=P(("layer", "col"), "row"), check_vma=False
    )
```

time: 697 us -> 324 us (0.46); the launches traced: 684 us -> 320 us
  local copies, waits for them, and re-layouts: 196 us -> 11.1 us
  blocking collectives: 134 us -> 54.8 us
  waiting for transfers between devices: 212 us -> 136 us
  Pallas kernels: 0 us -> 74.4 us
  other arithmetic: 64.6 us -> 2.47 us
  matrix products: 53.7 us -> 0 us
  starting transfers between devices: 10.1 us -> 40.7 us
  between operations: 14.1 us -> 0.06 us
    all_to_all x8 -> x0, local copies, waits for them, and re-layouts: 86.3 us -> none  [the longest x3 40.5 us: on_device(): lax.all_to_all(half, 'row', split_axis=3, concat_axis=1, tiled=True)]
    all_to_all x2 -> x1, blocking collectives: 134 us -> 54.8 us  [on_device(): lax.all_to_all(grids[k].reshape(GROUP, ROWS, 2 * BLOCK), 'col', split_axi...]
    pallas_call x0 -> x5, Pallas kernels: none -> 74.4 us  [the longest x2 34.7 us: along_u(): pl.pallas_call(functools.partial(along_u_kernel, first, last), grid=(tile...]
    all_to_all x2 -> x4, waiting for transfers between devices: 182 us -> 113 us  [the longest x2 67.4 us: on_device(): lax.all_to_all(half, ('row', 'col'), split_axis=0, concat_axis=0, tiled=T...]
    dot_general x4 -> x0, matrix products: 53.7 us -> none  [the longest x1 18.9 us: on_device(): jnp.einsum('xrak,sac->sxrck', blocks, table_a, preferred_element_type=jnp...]
    convert_element_type x3 -> x0, local copies, waits for them, and re-layouts: 43.7 us -> none  [the longest x2 41.1 us: on_device(): half = half.reshape(local, slab, 2, width).astype(jnp.bfloat16)]
    reduce_sum x1 -> x0, other arithmetic: 33.7 us -> none  [on_device(): jnp.sum(jnp.cos(phase) * final[:, :, 0] - jnp.sin(phase) * final[:, :, 1]...]
    reduce_scatter x1 -> x0, waiting for transfers between devices: 29.8 us -> none  [on_device(): lax.psum_scatter(spread.astype(jnp.bfloat16), 'layer', scatter_dimension=...]
  transfers between devices with their start and end apart: 3 -> 5, of which waited for: 3 -> 5; matrix products, arithmetic and copies ran while one was open for 1% -> 1% of each run, Pallas kernels for 0% -> 16%
where the time goes in v1:
time: 324 us; the launch traced here: 320 us
  waiting for transfers between devices  136 us (42%)
  Pallas kernels  74.4 us (23%)
  blocking collectives  54.8 us (17%)
  starting transfers between devices  40.7 us (13%)
  local copies, waits for them, and re-layouts  11.1 us (3%)
    all_to_all x2, waiting for transfers between devices, on_device(): lax.all_to_all(half, ('row', 'col'), split_axis=0, concat_axis=0, tiled=T...  67.4 us
    all_to_all x1, blocking collectives, on_device(): lax.all_to_all(grids[k].reshape(GROUP, ROWS, 2 * BLOCK), 'col', split_axi...  54.8 us
    pallas_call x2, Pallas kernels, along_u(): pl.pallas_call(functools.partial(along_u_kernel, first, last), grid=(tile...  34.7 us
    pallas_call x2, Pallas kernels, along_v(): pl.pallas_call(along_v_kernel, grid=(GROUP,), out_shape=jax.ShapeDtypeStr...  34.2 us
    all_to_all x1, waiting for transfers between devices, on_device(): lax.all_to_all(grids[k].reshape(GROUP, ROWS, 2 * BLOCK), 'col', split_axi...  32.6 us
    ppermute x1, waiting for transfers between devices, on_device(): other = lax.ppermute(send, 'layer', [(0, 1), (1, 0)])  23.1 us
    all_to_all x2, starting transfers between devices, on_device(): lax.all_to_all(half, ('row', 'col'), split_axis=0, concat_axis=0, tiled=T...  22.8 us
    all_to_all x1, waiting for transfers between devices, on_device(): lax.all_to_all(summed, 'col', split_axis=0, concat_axis=0, tiled=True)  13.1 us
  transfers between devices with their start and end apart: 5, of which 5 were waited for; matrix products, arithmetic and copies ran while one was open for 1% of the time, Pallas kernels for 16%

profile of v1, /device:TPU:0, one launch (start us, length us, event | category | flops | bytes accessed | tf_op | source)
XLA Modules:
  0.0 319.7 jit_solution(17402952314354001939)
XLA Ops:
  0.0 5.3 %fusion.1 = (bf16[1,1024,2048]{2,1,0:T(8,128)(2,1)S(1)}, bf16[1,1024,2048]{2,1,0:T(8,128)(2,1)}) fusion(bf16[2,1024,2048]{2,1,0:T(8,128)(2,1)} %param.15), kind=kLoop, calls=%fused_computation.3 | loop fusion | bytes 16777216 | tf_op jit(solution)/shard_map/slice | solution.py:293
  5.3 54.8 %all_to_all.25.cells_ref = bf16[8,128,2048]{2,1,0:T(8,128)(2,1)} all-to-all(bf16[8,128,2048]{2,1,0:T(8,128)(2,1)S(1)} %bitcast.14), channel_id=1, replica_groups=mesh['layer'=2,'row'=8,'col'=8] {'col'}, dimensions={0} | all-to-all | bytes 8388608 | tf_op jit(solution)/shard_map/all_to_all | solution.py:292
  60.1 4.6 %all-to-all-start = ((bf16[8,128,2048]{2,1,0:T(8,128)(2,1)}), bf16[8,128,2048]{2,1,0:T(8,128)(2,1)}, u32[]{:S(2)}, u32[]{:S(2)}) async-start(bf16[8,128,2048]{2,1,0:T(8,128)(2,1)} %bitcast.13), calls=%async_computation | async-start | bytes 8388608 | tf_op jit(solution)/shard_map/all_to_all | solution.py:292
  64.7 17.1 %along_v.3 = bf16[8,8,2,128,128]{4,3,2,1,0:T(8,128)(2,1)} custom-call(bf16[8,128,2048]{2,1,0:T(8,128)(2,1)} %all_to_all.25.cells_ref, f32[8,2048]{1,0:T(8,128)} %constant.46.clone.cos_ref, f32[8,2048]{1,0:T(8,128)} %constant.47.clone.sin_ref, bf16[2048,2048]{1,0:T(8,128)(2,1)} %constant.48.clone.table_ref), custom_call_target="tpu_custom_call" | custom-call | flops 8589934592 | bytes 16777216 | tf_op jit(solution)/shard_map/along_v/pallas_call | solution.py:104
  81.8 32.6 %all-to-all-done.cells_ref = bf16[8,128,2048]{2,1,0:T(8,128)(2,1)} async-done(((bf16[8,128,2048]{2,1,0:T(8,128)(2,1)}), bf16[8,128,2048]{2,1,0:T(8,128)(2,1)}, u32[]{:S(2)}, u32[]{:S(2)}) %all-to-all-start) | async-done | bytes 4194336 | tf_op jit(solution)/shard_map/all_to_all | solution.py:292
  114.4 9.6 %all-to-all-start.3 = ((bf16[64,2,128,128]{3,2,1,0:T(8,128)(2,1)}), bf16[64,2,128,128]{3,2,1,0:T(8,128)(2,1)}, u32[]{:S(2)}, u32[]{:S(2)}) async-start(bf16[64,2,128,128]{3,2,1,0:T(8,128)(2,1)} %bitcast.18), calls=%async_computation.3 | async-start | bytes 8388608 | tf_op jit(solution)/shard_map/all_to_all | solution.py:296
  124.0 17.1 %along_v.2 = bf16[8,8,2,128,128]{4,3,2,1,0:T(8,128)(2,1)} custom-call(bf16[8,128,2048]{2,1,0:T(8,128)(2,1)} %all-to-all-done.cells_ref, f32[8,2048]{1,0:T(8,128)} %constant.46.clone.cos_ref, f32[8,2048]{1,0:T(8,128)} %constant.47.clone.sin_ref, bf16[2048,2048]{1,0:T(8,128)(2,1)} %constant.48.clone.table_ref), custom_call_target="tpu_custom_call" | custom-call | flops 8589934592 | bytes 16777216 | tf_op jit(solution)/shard_map/along_v/pallas_call | solution.py:104
  141.1 34.0 %all-to-all-done.3.cells_ref = bf16[64,2,128,128]{3,2,1,0:T(8,128)(2,1)} async-done(((bf16[64,2,128,128]{3,2,1,0:T(8,128)(2,1)}), bf16[64,2,128,128]{3,2,1,0:T(8,128)(2,1)}, u32[]{:S(2)}, u32[]{:S(2)}) %all-to-all-start.3) | async-done | bytes 4194336 | tf_op jit(solution)/shard_map/all_to_all | solution.py:296
  175.1 0.0 copy-start.1
  175.1 13.2 %all-to-all-start.1 = ((bf16[64,2,128,128]{3,2,1,0:T(8,128)(2,1)}), bf16[64,2,128,128]{3,2,1,0:T(8,128)(2,1)}, u32[]{:S(2)}, u32[]{:S(2)}) async-start(bf16[64,2,128,128]{3,2,1,0:T(8,128)(2,1)} %bitcast.17), calls=%async_computation.1 | async-start | bytes 8388608 | tf_op jit(solution)/shard_map/all_to_all | solution.py:296
  188.3 0.0 copy-done.1
  188.3 0.6 fusion.2
  189.0 17.1 %along_u.2.rest_0_ = f32[128,8192]{1,0:T(8,128)} custom-call(s32[1]{0:T(128)} %bitcast.place_ref, s32[1]{0:T(128)} %get-tuple-element.7.w_ref, bf16[64,2,128,128]{3,2,1,0:T(8,128)(2,1)} %all-to-all-done.3.cells_ref, f32[128,64]{1,0:T(8,128)} %constant.49.clone.cos_ref, f32[128,64]{1,0:T(8,128)} %constant.50.clone.sin_ref, ...), custom_call_target="tpu_custom_call" | custom-call | flops 1073741824 | bytes 8388608 | tf_op jit(solution)/shard_map/along_u/pallas_call | solution.py:240
  206.0 33.4 %all-to-all-done.1.cells_ref = bf16[64,2,128,128]{3,2,1,0:T(8,128)(2,1)} async-done(((bf16[64,2,128,128]{3,2,1,0:T(8,128)(2,1)}), bf16[64,2,128,128]{3,2,1,0:T(8,128)(2,1)}, u32[]{:S(2)}, u32[]{:S(2)}) %all-to-all-start.1) | async-done | bytes 4194336 | tf_op jit(solution)/shard_map/all_to_all | solution.py:296
  239.5 17.6 %along_u.3 = bf16[16,512,128]{2,1,0:T(8,128)(2,1)} custom-call(s32[1]{0:T(128)} %bitcast.place_ref, s32[1]{0:T(128)} %get-tuple-element.8.w_ref, bf16[64,2,128,128]{3,2,1,0:T(8,128)(2,1)} %all-to-all-done.1.cells_ref, f32[128,64]{1,0:T(8,128)} %constant.49.clone.cos_ref, f32[128,64]{1,0:T(8,128)} %constant.50.clone.sin_ref, ...), custom_call_target="tpu_custom_call" | custom-call | flops 1073741824 | bytes 8388608 | tf_op jit(solution)/shard_map/along_u/pallas_call | solution.py:240
  257.1 1.3 dynamic-slice_bitcast_fusion
  258.4 5.1 %collective-permute-start = (bf16[8,512,128]{2,1,0:T(8,128)(2,1)S(1)}, bf16[8,512,128]{2,1,0:T(8,128)(2,1)S(1)}, u32[]{:S(2)}, u32[]{:S(2)}) collective-permute-start(bf16[8,512,128]{2,1,0:T(8,128)(2,1)S(1)} %dynamic-slice_bitcast_fusion), channel_id=1, source_target_pairs={{0,64},{64,0},{1,65},{65,1},{2,66},{66,2},{3,67},{67,3},{4,68},{68... | collective-permute-start | bytes 3145736 | tf_op jit(solution)/shard_map/ppermute | solution.py:301
  263.5 23.1 %collective-permute-done = bf16[8,512,128]{2,1,0:T(8,128)(2,1)S(1)} collective-permute-done((bf16[8,512,128]{2,1,0:T(8,128)(2,1)S(1)}, bf16[8,512,128]{2,1,0:T(8,128)(2,1)S(1)}, u32[]{:S(2)}, u32[]{:S(2)}) %collective-permute-start) | collective-permute-done | bytes 1048608 | tf_op jit(solution)/shard_map/ppermute | solution.py:301
  286.7 2.5 fusion
  289.1 8.2 %all-to-all-start.4 = ((bf16[8,512,128]{2,1,0:T(8,128)(2,1)}), bf16[8,512,128]{2,1,0:T(8,128)(2,1)S(1)}, u32[]{:S(2)}, u32[]{:S(2)}) async-start(bf16[8,512,128]{2,1,0:T(8,128)(2,1)} %fusion), calls=%async_computation.4 | async-start | bytes 2097152 | tf_op jit(solution)/shard_map/all_to_all | solution.py:303
  297.3 0.8 dynamic_slice.15
  298.1 0.9 copy.16.rows_ref
  298.9 1.3 dynamic_slice.16
  300.2 13.1 %all-to-all-done.4.cells_ref = bf16[8,512,128]{2,1,0:T(8,128)(2,1)S(1)} async-done(((bf16[8,512,128]{2,1,0:T(8,128)(2,1)}), bf16[8,512,128]{2,1,0:T(8,128)(2,1)S(1)}, u32[]{:S(2)}, u32[]{:S(2)}) %all-to-all-start.4) | async-done | bytes 1048608 | tf_op jit(solution)/shard_map/all_to_all | solution.py:303
  313.3 0.0 copy-start
  313.3 1.0 copy-done
  314.2 5.5 %arrange.1 = f32[512,1024]{1,0:T(8,128)} custom-call(bf16[8,512,128]{2,1,0:T(8,128)(2,1)} %copy-done, f32[512,1]{1,0:T(8,128)} %copy.16.rows_ref, f32[1,1024]{1,0:T(1,128)} %bitcast.19), custom_call_target="tpu_custom_call" | custom-call | tf_op jit(solution)/shard_map/arrange/pallas_call | solution.py:274
Async XLA Ops:
  60.1 54.3 %all-to-all-start = ((bf16[8,128,2048]{2,1,0:T(8,128)(2,1)}), bf16[8,128,2048]{2,1,0:T(8,128)(2,1)}, u32[]{:S(2)}, u32[]{:S(2)}) async-start(bf16[8,128,2048]{2,1,0:T(8,128)(2,1)} %bitcast.13), calls=%async_computation | async-start | bytes 8388608 | tf_op jit(solution)/shard_map/all_to_all | solution.py:292
  114.4 60.8 %all-to-all-start.3 = ((bf16[64,2,128,128]{3,2,1,0:T(8,128)(2,1)}), bf16[64,2,128,128]{3,2,1,0:T(8,128)(2,1)}, u32[]{:S(2)}, u32[]{:S(2)}) async-start(bf16[64,2,128,128]{3,2,1,0:T(8,128)(2,1)} %bitcast.18), calls=%async_computation.3 | async-start | bytes 8388608 | tf_op jit(solution)/shard_map/all_to_all | solution.py:296
  175.1 13.2 %copy-start.1 = (s32[2]{0:T(128)S(1)}, s32[2]{0:T(128)}, u32[]{:S(2)}) copy-start(s32[2]{0:T(128)} %param.17) | copy-start | bytes 28
  175.1 64.3 %all-to-all-start.1 = ((bf16[64,2,128,128]{3,2,1,0:T(8,128)(2,1)}), bf16[64,2,128,128]{3,2,1,0:T(8,128)(2,1)}, u32[]{:S(2)}, u32[]{:S(2)}) async-start(bf16[64,2,128,128]{3,2,1,0:T(8,128)(2,1)} %bitcast.17), calls=%async_computation.1 | async-start | bytes 8388608 | tf_op jit(solution)/shard_map/all_to_all | solution.py:296
  258.4 28.3 %collective-permute-start = (bf16[8,512,128]{2,1,0:T(8,128)(2,1)S(1)}, bf16[8,512,128]{2,1,0:T(8,128)(2,1)S(1)}, u32[]{:S(2)}, u32[]{:S(2)}) collective-permute-start(bf16[8,512,128]{2,1,0:T(8,128)(2,1)S(1)} %dynamic-slice_bitcast_fusion), channel_id=1, source_target_pairs={{0,64},{64,0},{1,65},{65,1},{2,66},{66,2},{3,67},{67,3},{4,68},{68... | collective-permute-start | bytes 3145736 | tf_op jit(solution)/shard_map/ppermute | solution.py:301
  289.1 24.1 %all-to-all-start.4 = ((bf16[8,512,128]{2,1,0:T(8,128)(2,1)}), bf16[8,512,128]{2,1,0:T(8,128)(2,1)S(1)}, u32[]{:S(2)}, u32[]{:S(2)}) async-start(bf16[8,512,128]{2,1,0:T(8,128)(2,1)} %fusion), calls=%async_computation.4 | async-start | bytes 2097152 | tf_op jit(solution)/shard_map/all_to_all | solution.py:303
  313.3 1.0 copy-start

commit v2 on v1

v2 whole, which is shorter than its diff:
```python
import functools
import math

import jax
import jax.numpy as jnp
import numpy as np
from jax import lax
from jax.experimental import pallas as pl
from jax.experimental.pallas import tpu as pltpu
from jax.sharding import PartitionSpec as P

INNER = 64
NPIX = 8192
LANES = 128
GROUP = 8
LAYERS_AXIS = 2
BLOCK = NPIX // GROUP
ROWS = BLOCK // GROUP
CELLS = NPIX // ROWS
HALF_ROOT = math.sqrt(0.5)
VMEM_LIMIT = 60 * 1024 * 1024


def power_terms(f):
    line = np.polynomial.Chebyshev.interpolate(lambda z: f(np.sqrt(z)), 4, domain=[0.0, 0.25])
    return [float(c) for c in line.convert(kind=np.polynomial.Polynomial).coef]


SIN_TERMS = power_terms(lambda t: np.pi * np.sinc(t))
COS_TERMS = power_terms(lambda t: np.cos(np.pi * t))


def unit(product, count):
    angle = 2.0 * np.pi / count * (product % count).astype(np.float64)
    return np.cos(angle), np.sin(angle)


def spread_tables():
    cell = np.arange(BLOCK) + BLOCK * np.arange(GROUP).reshape(GROUP, 1, 1)
    cosine, sine = unit(np.arange(GROUP)[:, None] * cell, NPIX)
    return cosine.astype(np.float32), sine.astype(np.float32)


def wide_table():
    cell = np.arange(BLOCK).reshape(GROUP, LANES, 1, 1)
    freq = np.arange(BLOCK).reshape(1, 1, GROUP, LANES)
    cosine, sine = unit(cell * freq, BLOCK)
    upper = np.stack([cosine, sine], axis=3)
    lower = np.stack([-sine, cosine], axis=3)
    return np.stack([upper, lower], axis=1).reshape(2 * BLOCK, 2 * BLOCK).astype(jnp.bfloat16)


def short_table():
    steps = np.arange(ROWS)
    cosine, sine = unit(steps[:, None] * steps[None, :], ROWS)
    upper = np.concatenate([cosine, -sine], axis=1)
    lower = np.concatenate([sine, cosine], axis=1)
    return np.concatenate([upper, lower], axis=0).astype(jnp.bfloat16)


def row_tables():
    start = np.arange(ROWS) + BLOCK * np.arange(GROUP)[:, None]
    cosine, sine = unit(start[:, :, None] * np.arange(CELLS), NPIX)
    return cosine.astype(np.float32), sine.astype(np.float32)


def eight(xr, xi):
    er = [xr[c] + xr[c + 4] for c in range(4)]
    ei = [xi[c] + xi[c + 4] for c in range(4)]
    dr = [xr[c] - xr[c + 4] for c in range(4)]
    di = [xi[c] - xi[c + 4] for c in range(4)]
    evr, evi, odr, odi = er[0] + er[2], ei[0] + ei[2], er[1] + er[3], ei[1] + ei[3]
    nr, ni = (dr[1] - dr[3]) * HALF_ROOT, (di[1] - di[3]) * HALF_ROOT
    fr, fi = (dr[1] + dr[3]) * HALF_ROOT, (di[1] + di[3]) * HALF_ROOT
    outr, outi = [None] * 8, [None] * 8
    outr[0], outi[0] = evr + odr, evi + odi
    outr[4], outi[4] = evr - odr, evi - odi
    pairs = (
        (2, er[0] - er[2], ei[0] - ei[2], er[1] - er[3], ei[1] - ei[3]),
        (1, dr[0] + nr, di[0] + ni, dr[2] + fr, di[2] + fi),
        (3, dr[0] - nr, di[0] - ni, fr - dr[2], fi - di[2]),
    )
    for j, pr, pi, qr, qi in pairs:
        outr[j], outi[j] = pr - qi, pi + qr
        outr[8 - j], outi[8 - j] = pr + qi, pi - qr
    return outr, outi


def part_planes(pair):
    one, two = pair[:, :LANES].astype(jnp.float32), pair[:, LANES:].astype(jnp.float32)
    low = lax.broadcasted_iota(jnp.int32, one.shape, 1) < INNER
    real = jnp.where(low, one, pltpu.roll(two, INNER, 1))
    imag = jnp.where(low, pltpu.roll(one, INNER, 1), two)
    return real, imag


def screened(real, imag, l, m, w_value):
    across = (l.astype(jnp.float32) - NPIX / 2) / NPIX
    down = (m.astype(jnp.float32) - NPIX / 2) / NPIX
    square = 1.0 - across * across - down * down
    turns = w_value * (square * lax.rsqrt(square) - 1.0)
    t = turns - jnp.floor(turns + 0.5)
    t2 = t * t
    sine, cosine = SIN_TERMS[-1], COS_TERMS[-1]
    for a, b in zip(SIN_TERMS[-2::-1], COS_TERMS[-2::-1]):
        sine, cosine = sine * t2 + a, cosine * t2 + b
    sine = sine * t
    return real - 2.0 * sine * (sine * real + cosine * imag)


def along_v_kernel(early, core_ref, place_ref, w_ref, _, *refs):
    cells, (cos_ref, sin_ref, table_ref, out_ref, spun) = refs[:-5], refs[-5:]
    step = pl.program_id(0)

    @pl.when(step == 0)
    def _():
        def one_tile(tile, carry):
            rows = pl.ds(pl.multiple_of(tile * 16, 16), 16)
            for part in range(GROUP):
                if early:
                    lanes = slice(2 * LANES * part, 2 * LANES * (part + 1))
                    pairs = [part_planes(ref[0, rows, lanes]) for ref in cells]
                    xr, xi = [p[0] for p in pairs], [p[1] for p in pairs]
                else:
                    xr = [cells[0][part, c, 0, rows].astype(jnp.float32) for c in range(GROUP)]
                    xi = [cells[0][part, c, 1, rows].astype(jnp.float32) for c in range(GROUP)]
                yr, yi = eight(xr, xi)
                lanes = slice(part * LANES, (part + 1) * LANES)
                for j in range(GROUP):
                    real, imag = yr[j], yi[j]
                    if j:
                        tc, ts = cos_ref[j : j + 1, lanes], sin_ref[j : j + 1, lanes]
                        real, imag = real * tc - imag * ts, real * ts + imag * tc
                    spun[j, rows, 2 * LANES * part : 2 * LANES * part + LANES] = real.astype(jnp.bfloat16)
                    spun[j, rows, 2 * LANES * part + LANES : 2 * LANES * (part + 1)] = imag.astype(jnp.bfloat16)
            return carry

        lax.fori_loop(0, ROWS // 16, one_tile, 0)

    shape = (ROWS, LANES)
    row = lax.broadcasted_iota(jnp.int32, shape, 0)
    q = lax.broadcasted_iota(jnp.int32, shape, 1)
    for j in range(GROUP):
        res = jnp.dot(spun[j], table_ref[...], preferred_element_type=jnp.float32)
        real, imag = res[:, :LANES], res[:, LANES:]
        if early:
            out_ref[0, j, 0] = real.astype(jnp.bfloat16)
            out_ref[0, j, 1] = imag.astype(jnp.bfloat16)
        else:
            l = row // CELLS * (NPIX // 2) + row % 8 * CELLS + row // 8 % 8 + place_ref[0]
            m = step * BLOCK + GROUP * q + j
            image = screened(real, imag, l, m, w_ref[0].astype(jnp.float32)).astype(jnp.bfloat16)
            out_ref[0, 0, j] = image[:CELLS]
            out_ref[1, 0, j] = image[CELLS:]


def along_v(early, cells, tw_cos, tw_sin, core, place, w_value, after):
    whole = lambda *shape: pl.BlockSpec(shape, lambda s, core: (0,) * len(shape))
    smem = pl.BlockSpec(memory_space=pltpu.SMEM)
    if early:
        shape, block, index = (GROUP, GROUP, 2, ROWS, LANES), (1, GROUP, 2, ROWS, LANES), lambda s, core: (s, 0, 0, 0, 0)
        pick = lambda k: pl.BlockSpec((1, ROWS, 2 * BLOCK), lambda s, core: (lax.rem(core[0] + k, 2), 0, 0))
        in_specs = [pick(k) for _ in range(GROUP // 2) for k in range(2)]
        cells = [pair for pair in cells for _ in range(2)]
    else:
        shape, block = (LAYERS_AXIS, GROUP, GROUP, CELLS, LANES), (LAYERS_AXIS, 1, GROUP, CELLS, LANES)
        index = lambda s, core: (0, s, 0, 0, 0)
        in_specs = [whole(GROUP, GROUP, 2, ROWS, LANES)]
    return pl.pallas_call(
        functools.partial(along_v_kernel, early),
        out_shape=jax.ShapeDtypeStruct(shape, jnp.bfloat16),
        grid_spec=pltpu.PrefetchScalarGridSpec(
            num_scalar_prefetch=1,
            grid=(GROUP,),
            in_specs=[
                smem,
                smem,
                pl.BlockSpec(memory_space=pl.ANY),
                *in_specs,
                whole(GROUP, BLOCK),
                whole(GROUP, BLOCK),
                pl.BlockSpec((2 * BLOCK, 2 * LANES), lambda s, core: (0, s)),
            ],
            out_specs=pl.BlockSpec(block, index),
            scratch_shapes=[pltpu.VMEM((GROUP, ROWS, 2 * BLOCK), jnp.bfloat16)],
        ),
        compiler_params=pltpu.CompilerParams(vmem_limit_bytes=VMEM_LIMIT),
        cost_estimate=pl.CostEstimate(flops=2 * 1024 * 2048 * 2048, bytes_accessed=16 << 20, transcendentals=0),
        name="v_first" if early else "v_last",
    )(core, place, w_value, after, *cells, tw_cos, tw_sin, jnp.asarray(wide_table()))


def along_u_kernel(early, place_ref, w_ref, _, *refs):
    cells, (cos_ref, sin_ref, table_ref, out_ref, mid, spun) = refs[:-6], refs[-6:]
    step = pl.program_id(0)
    tiles = ROWS // 16

    @pl.when(step < tiles)
    def _():
        for c in range(GROUP):
            if early:
                pairs = [part_planes(cells[r][c]) for r in range(GROUP)]
                xr, xi = [p[0] for p in pairs], [p[1] for p in pairs]
            else:
                xr = [cells[0][GROUP * r + c, 0].astype(jnp.float32) for r in range(GROUP)]
                xi = [cells[0][GROUP * r + c, 1].astype(jnp.float32) for r in range(GROUP)]
            yr, yi = eight(xr, xi)
            for i in range(GROUP):
                wr, wi = math.cos(2 * math.pi * c * i / CELLS), math.sin(2 * math.pi * c * i / CELLS)
                if c * i == 0:
                    mid[i, c, 0], mid[i, c, 1] = yr[i], yi[i]
                else:
                    mid[i, c, 0] = yr[i] * wr - yi[i] * wi
                    mid[i, c, 1] = yr[i] * wi + yi[i] * wr
        rows = pl.ds(pl.multiple_of(step * 16, 16), 16)
        lower = pl.ds(pl.multiple_of(ROWS + step * 16, 16), 16)
        for i1 in range(GROUP):
            yr, yi = eight([mid[i1, c, 0] for c in range(GROUP)], [mid[i1, c, 1] for c in range(GROUP)])
            for i2 in range(GROUP):
                i = i1 + GROUP * i2
                tc, ts = cos_ref[:, i : i + 1], sin_ref[:, i : i + 1]
                lanes = slice(i * LANES, (i + 1) * LANES)
                spun[rows, lanes] = (yr[i2] * tc - yi[i2] * ts).astype(jnp.bfloat16)
                spun[lower, lanes] = (yr[i2] * ts + yi[i2] * tc).astype(jnp.bfloat16)

    @pl.when(step >= tiles)
    def _():
        block = step - tiles
        lanes = pl.ds(pl.multiple_of(block * GROUP * LANES, LANES), GROUP * LANES)
        full = jnp.dot(table_ref[...], spun[:, lanes], preferred_element_type=jnp.float32)
        shape = (ROWS, LANES)
        g = lax.broadcasted_iota(jnp.int32, shape, 0)
        m = place_ref[0] + GROUP * lax.broadcasted_iota(jnp.int32, shape, 1)

        def by_tile(first, second):
            both = [z.reshape(ROWS // 8, 8, LANES) for z in (first, second)]
            return jnp.concatenate(both, axis=1).astype(jnp.bfloat16)

        for n in range(0, GROUP, 2):
            real = [full[:ROWS, k * LANES : (k + 1) * LANES] for k in (n, n + 1)]
            imag = [full[ROWS:, k * LANES : (k + 1) * LANES] for k in (n, n + 1)]
            if early:
                for p, pair in enumerate((real, imag)):
                    both = by_tile(*pair)
                    for group in range(LAYERS_AXIS):
                        out_ref[0, :, p, group, 8 * n : 8 * n + 16, :] = both[GROUP * group : GROUP * (group + 1)]
            else:
                images = [
                    screened(real[k], imag[k], CELLS * g + (block * GROUP + n + k), m, w_ref[0].astype(jnp.float32))
                    for k in range(2)
                ]
                out_ref[:, 8 * n : 8 * n + 16, :] = by_tile(*images)


def along_u(early, cells, tw_cos, tw_sin, place, w_value, after):
    tiles = ROWS // 16
    late = lambda s: jnp.maximum(s - tiles, 0)
    soon = lambda s: jnp.minimum(s, tiles - 1)
    smem = pl.BlockSpec(memory_space=pltpu.SMEM)
    if early:
        in_specs = [pl.BlockSpec((GROUP, 16, 2 * LANES), lambda s: (0, soon(s), 0))] * GROUP
        shape = (GROUP, GROUP, 2, LAYERS_AXIS, CELLS, LANES)
        out_spec = pl.BlockSpec((1,) + shape[1:], lambda s: (late(s), 0, 0, 0, 0, 0))
    else:
        in_specs = [pl.BlockSpec((CELLS, 2, 16, LANES), lambda s: (0, 0, soon(s), 0))]
        shape = (ROWS // 8, 8 * CELLS, LANES)
        out_spec = pl.BlockSpec((ROWS // 8, 8 * GROUP, LANES), lambda s: (0, late(s), 0))
    return pl.pallas_call(
        functools.partial(along_u_kernel, early),
        grid=(tiles + CELLS // GROUP,),
        out_shape=jax.ShapeDtypeStruct(shape, jnp.bfloat16),
        in_specs=[
            smem,
            smem,
            pl.BlockSpec(memory_space=pl.ANY),
            *in_specs,
            pl.BlockSpec((16, CELLS), lambda s: (soon(s), 0)),
            pl.BlockSpec((16, CELLS), lambda s: (soon(s), 0)),
            pl.BlockSpec((2 * ROWS, 2 * ROWS), lambda s: (0, 0)),
        ],
        out_specs=out_spec,
        scratch_shapes=[
            pltpu.VMEM((GROUP, GROUP, 2, 16, LANES), jnp.float32),
            pltpu.VMEM((2 * ROWS, CELLS * LANES), jnp.bfloat16),
        ],
        compiler_params=pltpu.CompilerParams(vmem_limit_bytes=VMEM_LIMIT),
        cost_estimate=pl.CostEstimate(flops=2 * 1024 * 2048 * 2048, bytes_accessed=8 << 20, transcendentals=0),
        name="u_first" if early else "u_last",
    )(place, w_value, after, *cells, tw_cos, tw_sin, jnp.asarray(short_table()))


def arrange_kernel(place_ref, *refs):
    one, (two_ref, rows_ref, cols_ref, out_ref, held) = refs[:-5], refs[-5:]
    q = lax.broadcasted_iota(jnp.int32, (LANES, BLOCK), 0)
    m = lax.broadcasted_iota(jnp.int32, (LANES, BLOCK), 1)
    total = None
    for shift in range(GROUP):
        j = lax.rem(place_ref[0] + GROUP - shift, GROUP)
        pick = jnp.where(m == GROUP * q + j, 1.0, 0.0).astype(jnp.bfloat16)
        other = [two_ref[0, r, j].astype(jnp.float32) + two_ref[1, r, j].astype(jnp.float32) for r in range(GROUP)]
        cells = (one[shift][...].astype(jnp.float32) + jnp.concatenate(other, axis=0)).astype(jnp.bfloat16)
        part = jnp.dot(cells, pick, preferred_element_type=jnp.float32)
        total = part if total is None else total + part
    total = total * (cols_ref[...] / NPIX)
    for part in range(GROUP):
        lanes = slice(part * LANES, (part + 1) * LANES)
        held[part] = total[:, lanes]
        for g in range(8):
            rows = slice(g * CELLS, (g + 1) * CELLS)
            out_ref[rows, lanes] = held[part, pl.ds(g, CELLS, 8), :] * rows_ref[rows, :]


def arrange(place, one, two, taper_rows, taper_cols):
    vmem = pl.BlockSpec(memory_space=pltpu.VMEM)
    return pl.pallas_call(
        arrange_kernel,
        out_shape=jax.ShapeDtypeStruct((8 * CELLS, BLOCK), jnp.float32),
        in_specs=[pl.BlockSpec(memory_space=pltpu.SMEM)] + [vmem] * (len(one) + 3),
        out_specs=vmem,
        scratch_shapes=[pltpu.VMEM((GROUP, 8 * CELLS, LANES), jnp.float32)],
        compiler_params=pltpu.CompilerParams(vmem_limit_bytes=VMEM_LIMIT),
        name="arrange",
    )(place, *one, two, taper_rows, taper_cols)


def columns_kernel(_, __, *refs):
    for cut, out in zip(refs[:GROUP], refs[GROUP:]):
        out[...] = cut[0]


def columns(grids, k, row, after):
    rows = 128
    cut = lambda n: pl.BlockSpec((1, rows, 2 * LANES), lambda s, place: (k, s, lax.rem(place[0] + n, GROUP)))
    return pl.pallas_call(
        columns_kernel,
        grid_spec=pltpu.PrefetchScalarGridSpec(
            num_scalar_prefetch=1,
            grid=(BLOCK // rows,),
            in_specs=[pl.BlockSpec(memory_space=pl.ANY)] + [cut(n) for n in range(GROUP)],
            out_specs=[pl.BlockSpec((rows, 2 * LANES), lambda s, place: (s, 0))] * GROUP,
        ),
        out_shape=[jax.ShapeDtypeStruct((BLOCK, 2 * LANES), grids.dtype)] * GROUP,
        name="columns",
    )(row, after, *[grids] * GROUP)


def around(blocks, axis, chains=()):
    before = {n: chain[i] for chain in chains for i, n in enumerate(chain[1:])}
    moved = {0: blocks[0]}
    for n in [n for chain in chains for n in chain] or range(1, GROUP):
        block = gate(blocks[n], moved[before[n]]) if n in before else blocks[n]
        moved[n] = lax.ppermute(block, axis, [(c, (c + n) % GROUP) for c in range(GROUP)])
    return [moved[-n % GROUP] for n in range(GROUP)]


def gate_kernel(*refs):
    del refs


def gate(value, *others):
    return pl.pallas_call(
        gate_kernel,
        out_shape=jax.ShapeDtypeStruct(value.shape, value.dtype),
        in_specs=[pl.BlockSpec(memory_space=pl.ANY)] * (1 + len(others)),
        out_specs=pl.BlockSpec(memory_space=pl.ANY),
        input_output_aliases={0: 0},
        name="gate",
    )(value, *others)


def swap(blocks, axes):
    return lax.all_to_all(blocks, axes, split_axis=0, concat_axis=0, tiled=True)


def on_device(grids, taper, w_steps):
    lay, row, col = lax.axis_index("layer"), lax.axis_index("row"), lax.axis_index("col")
    corner_u = (BLOCK * row + col).astype(jnp.int32).reshape(1)
    corner_v = (8 * CELLS * col + 8 * row).astype(jnp.int32).reshape(1)
    taper_cols = lax.dynamic_slice_in_dim(taper, BLOCK * row, BLOCK).reshape(1, BLOCK)
    taper_rows = lax.dynamic_slice_in_dim(taper, 8 * CELLS * (GROUP * lay + col), 8 * CELLS).reshape(8 * CELLS, 1)
    tables_u = [jnp.asarray(t) for t in row_tables()]
    tables_v = [jnp.asarray(t) for t in spread_tables()]
    own_u = [lax.dynamic_index_in_dim(t, row, 0, keepdims=False) for t in tables_u]
    own_v = [lax.dynamic_index_in_dim(t, col - col % 2, 0, keepdims=False) for t in tables_v]
    first_u, first_v = [t[0] for t in tables_u], [t[0] for t in tables_v]
    w_one, w_two = w_steps[:1], w_steps[1:]
    scalar = lambda value: value.astype(jnp.int32).reshape(1)

    side, place_y = col % 2, col // 2
    cells = grids.reshape(grids.shape[0], GROUP // 2, 2, ROWS, 2 * BLOCK)
    take = lambda k: lax.dynamic_slice(cells, (0, 0, k, 0, 0), (1, GROUP // 2, 1, ROWS, 2 * BLOCK))
    mine, give = (take(k).reshape(GROUP // 2, ROWS, 2 * BLOCK) for k in (side, 1 - side))
    got = lax.ppermute(give, "col", [(c, c ^ 1) for c in range(GROUP)])
    half = [None] * (GROUP // 2)
    for n in range(GROUP // 2):
        target = (place_y + n) % (GROUP // 2)
        block = jnp.stack([lax.dynamic_index_in_dim(t, target, 0, keepdims=False) for t in (mine, got)])
        last = block
        if n:
            block = lax.ppermute(block, "col", [(c, (c + 2 * n) % GROUP) for c in range(GROUP)])
        half[-n % (GROUP // 2)] = block
    other = around(columns(grids, 1, scalar(row), last), "row")
    half = along_v(True, half, *own_v, scalar(side), corner_v, w_one, w_one)
    half = gate(half, *other[1:])
    other = [block.reshape(GROUP, ROWS, 2 * LANES) for block in other]
    other = along_u(True, other, *own_u, corner_u, w_two, half)
    half = swap(half.reshape(CELLS, 2, ROWS, LANES), ("row", "col"))
    other = swap(other.reshape(CELLS, 2, ROWS, LANES), ("row", "col"))

    one = along_u(False, [half], *first_u, corner_u, w_one, w_one)
    two = along_v(False, [other.reshape(GROUP, GROUP, 2, ROWS, LANES)], *first_v, scalar(side), corner_v, w_two, one)
    one = one.reshape(LAYERS_AXIS, GROUP, 8 * CELLS, LANES)
    keep = lax.dynamic_index_in_dim(one, lay, 0, keepdims=False)
    send = lax.dynamic_index_in_dim(one, 1 - lay, 0, keepdims=False)
    send = lax.ppermute(send, "layer", [(0, 1), (1, 0)])
    one = (keep.astype(jnp.float32) + send.astype(jnp.float32)).astype(jnp.bfloat16)
    two = gate(two.reshape(LAYERS_AXIS * GROUP, GROUP, CELLS, LANES), one)
    two = swap(two, ("layer", "row")).reshape(LAYERS_AXIS, GROUP, GROUP, CELLS, LANES)
    one = [lax.dynamic_index_in_dim(one, (col + n) % GROUP, 0, keepdims=False) for n in range(GROUP)]
    one = around(one, "col")
    one = [one[-n % GROUP] for n in range(GROUP)]
    return arrange(scalar(col), one, two, taper_rows, taper_cols)


def solution(mesh):
    placed = (P("layer", "row", "col"), P(), P("layer"))
    return jax.shard_map(
        on_device, mesh=mesh, in_specs=placed, out_specs=P(("layer", "col"), "row"), check_vma=False
    )
```

time: 324 us -> 298 us (0.920)
  blocking collectives: 54.8 us -> 0 us
  starting transfers between devices: 40.7 us -> 82.2 us
  waiting for transfers between devices: 136 us -> 112 us
  Pallas kernels: 74.4 us -> 80.3 us
  local copies, waits for them, and re-layouts: 11.1 us -> 15.8 us
  other arithmetic: 2.47 us -> 5.78 us
    all_to_all x1 -> x0, blocking collectives: 54.8 us -> none  [on_device(): lax.all_to_all(grids[k].reshape(GROUP, ROWS, 2 * BLOCK), 'col', split_axi...]
    all_to_all x4 -> x3, waiting for transfers between devices: 113 us -> 76.7 us  [swap(): return lax.all_to_all(blocks, axes, split_axis=0, concat_axis=0, tiled=True)]
    ppermute x1 -> x19, starting transfers between devices: 5.13 us -> 38 us  [the longest x14 29.8 us: around(): lax.ppermute(block, axis, [(c, (c + n) % GROUP) for c in range(GROUP)])]
    ppermute x1 -> x19, waiting for transfers between devices: 23.1 us -> 35 us  [the longest x14 19.5 us: around(): lax.ppermute(block, axis, [(c, (c + n) % GROUP) for c in range(GROUP)])]
    all_to_all x4 -> x3, starting transfers between devices: 35.6 us -> 44.2 us  [swap(): return lax.all_to_all(blocks, axes, split_axis=0, concat_axis=0, tiled=True)]
    slice x2 -> x1, local copies, waits for them, and re-layouts: 5.96 us -> 0.59 us  [on_device(): w_one, w_two = (w_steps[:1], w_steps[1:])]
    pallas_call x4 -> x7, Pallas kernels: 68.9 us -> 74.2 us  [the longest x2 37.5 us: along_v(): pl.pallas_call(functools.partial(along_v_kernel, early), out_shape=jax.Sh...]
    squeeze x1 -> x4, local copies, waits for them, and re-layouts: 1.29 us -> 5.02 us  [the longest x1 1.54 us: on_device(): lax.dynamic_index_in_dim(t, row, 0, keepdims=False)]
  transfers between devices with their start and end apart: 5 -> 22, of which waited for: 5 -> 10; matrix products, arithmetic and copies ran while one was open for 1% -> 4% of each run, Pallas kernels for 16% -> 25%
where the time goes in v2:
time: 298 us; the launch traced here: 296 us
  waiting for transfers between devices  112 us (38%)
  starting transfers between devices  82.2 us (28%)
  Pallas kernels  80.3 us (27%)
  local copies, waits for them, and re-layouts  15.8 us (5%)
  other arithmetic  5.78 us (2%)
    all_to_all x3, waiting for transfers between devices, swap(): return lax.all_to_all(blocks, axes, split_axis=0, concat_axis=0, tiled=True)  76.7 us
    all_to_all x3, starting transfers between devices, swap(): return lax.all_to_all(blocks, axes, split_axis=0, concat_axis=0, tiled=True)  44.2 us
    pallas_call x2, Pallas kernels, along_v(): pl.pallas_call(functools.partial(along_v_kernel, early), out_shape=jax.Sh...  37.5 us
    pallas_call x2, Pallas kernels, along_u(): pl.pallas_call(functools.partial(along_u_kernel, early), grid=(tiles + CE...  30.1 us
    ppermute x14, starting transfers between devices, around(): lax.ppermute(block, axis, [(c, (c + n) % GROUP) for c in range(GROUP)])  29.8 us
    ppermute x14, waiting for transfers between devices, around(): lax.ppermute(block, axis, [(c, (c + n) % GROUP) for c in range(GROUP)])  19.5 us
    ppermute x3, waiting for transfers between devices, on_device(): lax.ppermute(block, 'col', [(c, (c + 2 * n) % GROUP) for c in range(GROUP)])  13 us
    pallas_call x1, Pallas kernels, columns(): pl.pallas_call(columns_kernel, grid_spec=pltpu.PrefetchScalarGridSpec(num...  6.62 us
  transfers between devices with their start and end apart: 22, of which 10 were waited for; matrix products, arithmetic and copies ran while one was open for 4% of the time, Pallas kernels for 25%

profile of v2, /device:TPU:0, one launch (start us, length us, event | category | flops | bytes accessed | tf_op | source)
XLA Modules:
  0.0 296.1 jit_solution(10904646150694043277)
XLA Ops:
  0.0 1.7 dynamic-slice_bitcast_fusion
  1.9 1.7 dynamic-slice_bitcast_fusion.2
  3.6 2.5 collective-permute-done
  6.1 1.7 constant_dynamic-slice_fusion
  8.9 1.7 collective-permute-start.3
  11.6 2.9 collective-permute-start.2
  16.0 6.6 %columns.1 = (bf16[1024,256]{1,0:T(8,128)(2,1)}, bf16[1024,256]{1,0:T(8,128)(2,1)}, bf16[1024,256]{1,0:T(8,128)(2,1)}, bf16[1024,256]{1,0:T(8,128)(2,1)}, bf16[1...) custom-call(s32[1]{0:T(128)} %bitcast.12._, ...), custom_call_target="tpu_custom_call" | custom-call | tf_op jit(solution)/shard_map/columns/pallas_call | solution.py:334
  22.7 2.0 collective-permute-start.10
  24.6 4.7 %collective-permute-start.4 = (bf16[1024,256]{1,0:T(8,128)(2,1)}, bf16[1024,256]{1,0:T(8,128)(2,1)S(1)}, u32[]{:S(2)}, u32[]{:S(2)}) collective-permute-start(bf16[1024,256]{1,0:T(8,128)(2,1)} %get-tuple-element.13), channel_id=1, source_target_pairs={{0,56},{8,0},{16,8},{24,16},{32,24},{40,32},{48,40},{56,48},{1,57}... | collective-permute-start | bytes 1572872 | tf_op jit(solution)/shard_map/ppermute | solution.py:352
  32.4 8.5 %collective-permute-done.10.refs_7_ = bf16[1024,256]{1,0:T(8,128)(2,1)S(1)} collective-permute-done((bf16[1024,256]{1,0:T(8,128)(2,1)}, bf16[1024,256]{1,0:T(8,128)(2,1)S(1)}, u32[]{:S(2)}, u32[]{:S(2)}) %collective-permute-start.10) | collective-permute-done | bytes 524320 | tf_op jit(solution)/shard_map/ppermute | solution.py:352
  43.4 3.0 %collective-permute-start.7 = (bf16[1024,256]{1,0:T(8,128)(2,1)}, bf16[1024,256]{1,0:T(8,128)(2,1)}, u32[]{:S(2)}, u32[]{:S(2)}) collective-permute-start(bf16[1024,256]{1,0:T(8,128)(2,1)} %get-tuple-element.16), channel_id=1, source_target_pairs={{0,32},{8,40},{16,48},{24,56},{32,0},{40,8},{48,16},{56,24},{1,33}... | collective-permute-start | bytes 1572872 | tf_op jit(solution)/shard_map/ppermute | solution.py:352
  46.4 13.0 %collective-permute-done.2.refs_4_.refs_5_ = bf16[2,128,2048]{2,1,0:T(8,128)(2,1)} collective-permute-done((bf16[2,128,2048]{2,1,0:T(8,128)(2,1)}, bf16[2,128,2048]{2,1,0:T(8,128)(2,1)}, u32[]{:S(2)}, u32[]{:S(2)}) %collective-permute-start.2) | collective-permute-done | bytes 1048608 | tf_op jit(solution)/shard_map/ppermute | solution.py:400
  59.4 4.0 %collective-permute-start.8 = (bf16[1024,256]{1,0:T(8,128)(2,1)}, bf16[1024,256]{1,0:T(8,128)(2,1)}, u32[]{:S(2)}, u32[]{:S(2)}) collective-permute-start(bf16[1024,256]{1,0:T(8,128)(2,1)} %get-tuple-element.17), channel_id=1, source_target_pairs={{0,24},{8,32},{16,40},{24,48},{32,56},{40,0},{48,8},{56,16},{1,25}... | collective-permute-start | bytes 1572872 | tf_op jit(solution)/shard_map/ppermute | solution.py:352
  63.4 2.4 collective-permute-start.9
  65.9 18.7 %v_first.1.refs_0_ = bf16[8,8,2,128,128]{4,3,2,1,0:T(8,128)(2,1)} custom-call(s32[1]{0:T(128)} %bitcast.2.core_ref, s32[1]{0:T(128)} %bitcast.3.place_ref, s32[1]{0:T(128)} %get-tuple-element.38.w_ref._, s32[1]{0:T(128)} %get-tuple-element.38.w_ref._, bf16[2,128,2048]{2,1,0:T(8,128)(2,1)} %pad_maximum_fusion.refs_0_.refs_1_, ...), custom_call_target="tpu_custom_call" | custom-call | flops 8589934592 | bytes 16777216 | tf_op jit(solution)/shard_map/v_first/pallas_call | solution.py:169
  84.7 3.8 %collective-permute-done.8.refs_5_ = bf16[1024,256]{1,0:T(8,128)(2,1)} collective-permute-done((bf16[1024,256]{1,0:T(8,128)(2,1)}, bf16[1024,256]{1,0:T(8,128)(2,1)}, u32[]{:S(2)}, u32[]{:S(2)}) %collective-permute-start.8) | collective-permute-done | bytes 524320 | tf_op jit(solution)/shard_map/ppermute | solution.py:352
  88.4 4.4 %collective-permute-done.9.refs_6_ = bf16[1024,256]{1,0:T(8,128)(2,1)S(1)} collective-permute-done((bf16[1024,256]{1,0:T(8,128)(2,1)S(1)}, bf16[1024,256]{1,0:T(8,128)(2,1)S(1)}, u32[]{:S(2)}, u32[]{:S(2)}) %collective-permute-start.9) | collective-permute-done | bytes 524320 | tf_op jit(solution)/shard_map/ppermute | solution.py:352
  93.7 13.3 %all-to-all-start = ((bf16[64,2,128,128]{3,2,1,0:T(8,128)(2,1)}), bf16[64,2,128,128]{3,2,1,0:T(8,128)(2,1)}, u32[]{:S(2)}, u32[]{:S(2)}) async-start(bf16[64,2,128,128]{3,2,1,0:T(8,128)(2,1)} %bitcast.63), calls=%async_computation | async-start | bytes 8388608 | tf_op jit(solution)/shard_map/all_to_all | solution.py:372
  108.5 14.0 %u_first.1 = bf16[8,8,2,2,64,128]{5,4,3,2,1,0:T(8,128)(2,1)} custom-call(s32[1]{0:T(128)} %bitcast.1.place_ref, s32[1]{0:T(128)} %get-tuple-element.37.w_ref, bf16[8,8,2,128,128]{4,3,2,1,0:T(8,128)(2,1)} %gate.2._, bf16[8,128,256]{2,1,0:T(8,128)(2,1)} %bitcast.76, bf16[8,128,256]{2,1,0:T(8,128)(2,1)} %bitcast.70, bf16[8,128,256]{2,1,0:T(8,128)(2,1)} %bitcast.71, ...), custom_call_target="tpu_custom_call" | custom-call | flops 8589934592 | bytes 8388608 | tf_op jit(solution)/shard_map/u_first/pallas_call | solution.py:268
  122.5 35.6 %all-to-all-done.refs_0_ = bf16[64,2,128,128]{3,2,1,0:T(8,128)(2,1)} async-done(((bf16[64,2,128,128]{3,2,1,0:T(8,128)(2,1)}), bf16[64,2,128,128]{3,2,1,0:T(8,128)(2,1)}, u32[]{:S(2)}, u32[]{:S(2)}) %all-to-all-start) | async-done | bytes 4194336 | tf_op jit(solution)/shard_map/all_to_all | solution.py:372
  158.1 13.0 %all-to-all-start.1 = ((bf16[64,2,128,128]{3,2,1,0:T(8,128)(2,1)}), bf16[64,2,128,128]{3,2,1,0:T(8,128)(2,1)}, u32[]{:S(2)}, u32[]{:S(2)}) async-start(bf16[64,2,128,128]{3,2,1,0:T(8,128)(2,1)} %bitcast.66), calls=%async_computation.1 | async-start | bytes 8388608 | tf_op jit(solution)/shard_map/all_to_all | solution.py:372
  171.1 16.1 %u_last.1._ = bf16[16,512,128]{2,1,0:T(8,128)(2,1)} custom-call(s32[1]{0:T(128)} %bitcast.1.place_ref, s32[1]{0:T(128)} %get-tuple-element.38.w_ref._, s32[1]{0:T(128)} %get-tuple-element.38.w_ref._, bf16[64,2,128,128]{3,2,1,0:T(8,128)(2,1)} %all-to-all-done.refs_0_, f32[128,64]{1,0:T(8,128)} %constant.298.refs_1_, f32[128,64]{1,0:T(8,128)} %constant.300.refs_2_, ...), custom_call_target="tpu_custom_call" | custom-call | flops 8589934592 | bytes 8388608 | tf_op jit(solution)/shard_map/u_last/pallas_call | solution.py:268
  188.5 2.1 collective-permute-start.11
  190.6 31.6 %all-to-all-done.1 = bf16[64,2,128,128]{3,2,1,0:T(8,128)(2,1)} async-done(((bf16[64,2,128,128]{3,2,1,0:T(8,128)(2,1)}), bf16[64,2,128,128]{3,2,1,0:T(8,128)(2,1)}, u32[]{:S(2)}, u32[]{:S(2)}) %all-to-all-start.1) | async-done | bytes 4194336 | tf_op jit(solution)/shard_map/all_to_all | solution.py:372
  222.3 18.8 %v_last.1 = bf16[2,8,8,64,128]{4,3,2,1,0:T(8,128)(2,1)} custom-call(s32[1]{0:T(128)} %bitcast.2.core_ref, s32[1]{0:T(128)} %bitcast.3.place_ref, s32[1]{0:T(128)} %get-tuple-element.37.w_ref, bf16[16,512,128]{2,1,0:T(8,128)(2,1)} %u_last.1._, bf16[8,8,2,128,128]{4,3,2,1,0:T(8,128)(2,1)} %bitcast.36.refs_0_, f32[8,1024]{1,0:T(8,128)} %constant.302.refs_1_, ...), custom_call_target="tpu_custom_call" | custom-call | flops 8589934592 | bytes 16777216 | tf_op jit(solution)/shard_map/v_last/pallas_call | solution.py:169
  241.1 2.5 fusion.refs_1_
  243.6 17.8 %all-to-all-start.2 = ((bf16[16,8,64,128]{3,2,1,0:T(8,128)(2,1)}), bf16[16,8,64,128]{3,2,1,0:T(8,128)(2,1)S(1)}, u32[]{:S(2)}, u32[]{:S(2)}) async-start(bf16[16,8,64,128]{3,2,1,0:T(8,128)(2,1)} %gate.3), calls=%async_computation.2 | async-start | bytes 4194304 | tf_op jit(solution)/shard_map/all_to_all | solution.py:372
  262.4 4.4 %collective-permute-start.15 = (bf16[512,128]{1,0:T(8,128)(2,1)}, bf16[512,128]{1,0:T(8,128)(2,1)S(1)}, u32[]{:S(2)}, u32[]{:S(2)}) collective-permute-start(bf16[512,128]{1,0:T(8,128)(2,1)} %get-tuple-element.32), channel_id=1, source_target_pairs={{0,4},{1,5},{2,6},{3,7},{4,0},{5,1},{6,2},{7,3},{8,12},{9,13},{10,... | collective-permute-start | bytes 393224 | tf_op jit(solution)/shard_map/ppermute | solution.py:352
  266.8 2.0 collective-permute-done.12.refs_1_
  270.0 6.3 %collective-permute-start.18 = (bf16[512,128]{1,0:T(8,128)(2,1)S(1)}, bf16[512,128]{1,0:T(8,128)(2,1)S(1)}, u32[]{:S(2)}, u32[]{:S(2)}) collective-permute-start(bf16[512,128]{1,0:T(8,128)(2,1)S(1)} %get-tuple-element.29), channel_id=1, source_target_pairs={{0,7},{1,0},{2,1},{3,2},{4,3},{5,4},{6,5},{7,6},{8,15},{9,8},{10,9... | collective-permute-start | bytes 393224 | tf_op jit(solution)/shard_map/ppermute | solution.py:352
  279.3 9.4 %all-to-all-done.2 = bf16[16,8,64,128]{3,2,1,0:T(8,128)(2,1)S(1)} async-done(((bf16[16,8,64,128]{3,2,1,0:T(8,128)(2,1)}), bf16[16,8,64,128]{3,2,1,0:T(8,128)(2,1)S(1)}, u32[]{:S(2)}, u32[]{:S(2)}) %all-to-all-start.2) | async-done | bytes 2097184 | tf_op jit(solution)/shard_map/all_to_all | solution.py:372
  290.1 6.1 %arrange.1 = f32[512,1024]{1,0:T(8,128)} custom-call(s32[1]{0:T(128)} %bitcast.place_ref, bf16[512,128]{1,0:T(8,128)(2,1)} %get-tuple-element.36.refs_0_, bf16[512,128]{1,0:T(8,128)(2,1)} %copy-done.9, bf16[512,128]{1,0:T(8,128)(2,1)} %copy-done.10, bf16[512,128]{1,0:T(8,128)(2,1)} %copy-done.11, bf16[512,128]{1,0:T(8,128)(2,1)} %copy-done.12, ...), custom_call_target="tpu_custom_call" | custom-call | tf_op jit(solution)/shard_map/arrange/pallas_call | solution.py:315
  (72 shorter events, 19.4 us)
Async XLA Ops:
  1.7 4.4 %collective-permute-start = (bf16[4,128,2048]{2,1,0:T(8,128)(2,1)S(1)}, bf16[4,128,2048]{2,1,0:T(8,128)(2,1)}, u32[]{:S(2)}, u32[]{:S(2)}) collective-permute-start(bf16[4,128,2048]{2,1,0:T(8,128)(2,1)S(1)} %dynamic-slice_bitcast_fusion), channel_id=1, source_target_pairs={{0,1},{1,0},{2,3},{3,2},{4,5},{5,4},{6,7},{7,6},{8,9},{9,8},{10,11... | collective-permute-start | bytes 6291464 | tf_op jit(solution)/shard_map/ppermute | solution.py:393
  8.9 34.5 %collective-permute-start.3 = (bf16[2,128,2048]{2,1,0:T(8,128)(2,1)}, bf16[2,128,2048]{2,1,0:T(8,128)(2,1)}, u32[]{:S(2)}, u32[]{:S(2)}) collective-permute-start(bf16[2,128,2048]{2,1,0:T(8,128)(2,1)} %pad_maximum_fusion.3), channel_id=1, source_target_pairs={{0,2},{1,3},{2,4},{3,5},{4,6},{5,7},{6,0},{7,1},{8,10},{9,11},{10,... | collective-permute-start | bytes 3145736 | tf_op jit(solution)/shard_map/ppermute | solution.py:400
  11.6 47.8 %collective-permute-start.2 = (bf16[2,128,2048]{2,1,0:T(8,128)(2,1)}, bf16[2,128,2048]{2,1,0:T(8,128)(2,1)}, u32[]{:S(2)}, u32[]{:S(2)}) collective-permute-start(bf16[2,128,2048]{2,1,0:T(8,128)(2,1)} %pad_maximum_fusion.2), channel_id=1, source_target_pairs={{0,4},{1,5},{2,6},{3,7},{4,0},{5,1},{6,2},{7,3},{8,12},{9,13},{10,... | collective-permute-start | bytes 3145736 | tf_op jit(solution)/shard_map/ppermute | solution.py:400
  14.6 48.8 %collective-permute-start.1 = (bf16[2,128,2048]{2,1,0:T(8,128)(2,1)S(1)}, bf16[2,128,2048]{2,1,0:T(8,128)(2,1)}, u32[]{:S(2)}, u32[]{:S(2)}) collective-permute-start(bf16[2,128,2048]{2,1,0:T(8,128)(2,1)S(1)} %pad_maximum_fusion.1.__), channel_id=1, source_target_pairs={{0,6},{1,7},{2,0},{3,1},{4,2},{5,3},{6,4},{7,5},{8,14},{9,15},{10,... | collective-permute-start | bytes 3145736 | tf_op jit(solution)/shard_map/ppermute | solution.py:400
  16.0 13.3 %copy-start.16 = (s32[2]{0:T(128)S(1)}, s32[2]{0:T(128)}, u32[]{:S(2)}) copy-start(s32[2]{0:T(128)} %param.13) | copy-start | bytes 28
  22.7 18.2 %collective-permute-start.10 = (bf16[1024,256]{1,0:T(8,128)(2,1)}, bf16[1024,256]{1,0:T(8,128)(2,1)S(1)}, u32[]{:S(2)}, u32[]{:S(2)}) collective-permute-start(bf16[1024,256]{1,0:T(8,128)(2,1)} %get-tuple-element.19), channel_id=1, source_target_pairs={{0,8},{8,16},{16,24},{24,32},{32,40},{40,48},{48,56},{56,0},{1,9},... | collective-permute-start | bytes 1572872 | tf_op jit(solution)/shard_map/ppermute | solution.py:352
  24.6 17.8 %collective-permute-start.4 = (bf16[1024,256]{1,0:T(8,128)(2,1)}, bf16[1024,256]{1,0:T(8,128)(2,1)S(1)}, u32[]{:S(2)}, u32[]{:S(2)}) collective-permute-start(bf16[1024,256]{1,0:T(8,128)(2,1)} %get-tuple-element.13), channel_id=1, source_target_pairs={{0,56},{8,0},{16,8},{24,16},{32,24},{40,32},{48,40},{56,48},{1,57}... | collective-permute-start | bytes 1572872 | tf_op jit(solution)/shard_map/ppermute | solution.py:352
  29.3 34.1 %copy-start.17 = (bf16[1024,256]{1,0:T(8,128)(2,1)S(1)}, bf16[1024,256]{1,0:T(8,128)(2,1)}, u32[]{:S(2)}) copy-start(bf16[1024,256]{1,0:T(8,128)(2,1)} %get-tuple-element.18) | copy-start | bytes 1572868
  40.8 43.8 %copy-start.4 = (bf16[1024,256]{1,0:T(8,128)(2,1)}, bf16[1024,256]{1,0:T(8,128)(2,1)S(1)}, u32[]{:S(2)}) copy-start(bf16[1024,256]{1,0:T(8,128)(2,1)S(1)} %collective-permute-done.10.refs_7_) | copy-start | bytes 1572868
  40.8 43.8 %collective-permute-start.5 = (bf16[1024,256]{1,0:T(8,128)(2,1)}, bf16[1024,256]{1,0:T(8,128)(2,1)S(1)}, u32[]{:S(2)}, u32[]{:S(2)}) collective-permute-start(bf16[1024,256]{1,0:T(8,128)(2,1)} %get-tuple-element.14), channel_id=1, source_target_pairs={{0,48},{8,56},{16,0},{24,8},{32,16},{40,24},{48,32},{56,40},{1,49}... | collective-permute-start | bytes 1572872 | tf_op jit(solution)/shard_map/ppermute | solution.py:352
  42.4 42.2 %copy-start.5 = (bf16[1024,256]{1,0:T(8,128)(2,1)}, bf16[1024,256]{1,0:T(8,128)(2,1)S(1)}, u32[]{:S(2)}) copy-start(bf16[1024,256]{1,0:T(8,128)(2,1)S(1)} %collective-permute-done.4.refs_1_) | copy-start | bytes 1572868
  42.4 42.2 %collective-permute-start.6 = (bf16[1024,256]{1,0:T(8,128)(2,1)}, bf16[1024,256]{1,0:T(8,128)(2,1)S(1)}, u32[]{:S(2)}, u32[]{:S(2)}) collective-permute-start(bf16[1024,256]{1,0:T(8,128)(2,1)} %get-tuple-element.15), channel_id=1, source_target_pairs={{0,40},{8,48},{16,56},{24,0},{32,8},{40,16},{48,24},{56,32},{1,41}... | collective-permute-start | bytes 1572872 | tf_op jit(solution)/shard_map/ppermute | solution.py:352
  43.4 41.3 %collective-permute-start.7 = (bf16[1024,256]{1,0:T(8,128)(2,1)}, bf16[1024,256]{1,0:T(8,128)(2,1)}, u32[]{:S(2)}, u32[]{:S(2)}) collective-permute-start(bf16[1024,256]{1,0:T(8,128)(2,1)} %get-tuple-element.16), channel_id=1, source_target_pairs={{0,32},{8,40},{16,48},{24,56},{32,0},{40,8},{48,16},{56,24},{1,33}... | collective-permute-start | bytes 1572872 | tf_op jit(solution)/shard_map/ppermute | solution.py:352
  59.4 29.0 %collective-permute-start.8 = (bf16[1024,256]{1,0:T(8,128)(2,1)}, bf16[1024,256]{1,0:T(8,128)(2,1)}, u32[]{:S(2)}, u32[]{:S(2)}) collective-permute-start(bf16[1024,256]{1,0:T(8,128)(2,1)} %get-tuple-element.17), channel_id=1, source_target_pairs={{0,24},{8,32},{16,40},{24,48},{32,56},{40,0},{48,8},{56,16},{1,25}... | collective-permute-start | bytes 1572872 | tf_op jit(solution)/shard_map/ppermute | solution.py:352
  63.4 29.4 %collective-permute-start.9 = (bf16[1024,256]{1,0:T(8,128)(2,1)S(1)}, bf16[1024,256]{1,0:T(8,128)(2,1)S(1)}, u32[]{:S(2)}, u32[]{:S(2)}) collective-permute-start(bf16[1024,256]{1,0:T(8,128)(2,1)S(1)} %copy-done.17), channel_id=1, source_target_pairs={{0,16},{8,24},{16,32},{24,40},{32,48},{40,56},{48,0},{56,8},{1,17}... | collective-permute-start | bytes 1572872 | tf_op jit(solution)/shard_map/ppermute | solution.py:352
  93.7 64.4 %all-to-all-start = ((bf16[64,2,128,128]{3,2,1,0:T(8,128)(2,1)}), bf16[64,2,128,128]{3,2,1,0:T(8,128)(2,1)}, u32[]{:S(2)}, u32[]{:S(2)}) async-start(bf16[64,2,128,128]{3,2,1,0:T(8,128)(2,1)} %bitcast.63), calls=%async_computation | async-start | bytes 8388608 | tf_op jit(solution)/shard_map/all_to_all | solution.py:372
  158.1 64.2 %all-to-all-start.1 = ((bf16[64,2,128,128]{3,2,1,0:T(8,128)(2,1)}), bf16[64,2,128,128]{3,2,1,0:T(8,128)(2,1)}, u32[]{:S(2)}, u32[]{:S(2)}) async-start(bf16[64,2,128,128]{3,2,1,0:T(8,128)(2,1)} %bitcast.66), calls=%async_computation.1 | async-start | bytes 8388608 | tf_op jit(solution)/shard_map/all_to_all | solution.py:372
  188.5 52.6 %collective-permute-start.11 = (bf16[8,512,128]{2,1,0:T(8,128)(2,1)S(1)}, bf16[8,512,128]{2,1,0:T(8,128)(2,1)}, u32[]{:S(2)}, u32[]{:S(2)}) collective-permute-start(bf16[8,512,128]{2,1,0:T(8,128)(2,1)S(1)} %dynamic-slice_bitcast_fusion.1), channel_id=1, source_target_pairs={{0,64},{64,0},{1,65},{65,1},{2,66},{66,2},{3,67},{67,3},{4,68},{68... | collective-permute-start | bytes 3145736 | tf_op jit(solution)/shard_map/ppermute | solution.py:415
  222.3 18.8 %copy-start.3 = (bf16[16,512,128]{2,1,0:T(8,128)(2,1)S(1)}, bf16[16,512,128]{2,1,0:T(8,128)(2,1)}, u32[]{:S(2)}) copy-start(bf16[16,512,128]{2,1,0:T(8,128)(2,1)} %u_last.1._) | copy-start | bytes 6291460
  243.6 17.9 %copy-start = (bf16[8,512,128]{2,1,0:T(8,128)(2,1)S(1)}, bf16[8,512,128]{2,1,0:T(8,128)(2,1)}, u32[]{:S(2)}) copy-start(bf16[8,512,128]{2,1,0:T(8,128)(2,1)} %fusion.refs_1_) | copy-start | bytes 3145732
  243.6 45.2 %all-to-all-start.2 = ((bf16[16,8,64,128]{3,2,1,0:T(8,128)(2,1)}), bf16[16,8,64,128]{3,2,1,0:T(8,128)(2,1)S(1)}, u32[]{:S(2)}, u32[]{:S(2)}) async-start(bf16[16,8,64,128]{3,2,1,0:T(8,128)(2,1)} %gate.3), calls=%async_computation.2 | async-start | bytes 4194304 | tf_op jit(solution)/shard_map/all_to_all | solution.py:372
  262.3 6.5 %collective-permute-start.12 = (bf16[512,128]{1,0:T(8,128)(2,1)S(1)}, bf16[512,128]{1,0:T(8,128)(2,1)S(1)}, u32[]{:S(2)}, u32[]{:S(2)}) collective-permute-start(bf16[512,128]{1,0:T(8,128)(2,1)S(1)} %get-tuple-element.35), channel_id=1, source_target_pairs={{0,1},{1,2},{2,3},{3,4},{4,5},{5,6},{6,7},{7,0},{8,9},{9,10},{10,1... | collective-permute-start | bytes 393224 | tf_op jit(solution)/shard_map/ppermute | solution.py:352
  262.3 7.7 %collective-permute-start.13 = (bf16[512,128]{1,0:T(8,128)(2,1)S(1)}, bf16[512,128]{1,0:T(8,128)(2,1)S(1)}, u32[]{:S(2)}, u32[]{:S(2)}) collective-permute-start(bf16[512,128]{1,0:T(8,128)(2,1)S(1)} %get-tuple-element.34), channel_id=1, source_target_pairs={{0,2},{1,3},{2,4},{3,5},{4,6},{5,7},{6,0},{7,1},{8,10},{9,11},{10,... | collective-permute-start | bytes 393224 | tf_op jit(solution)/shard_map/ppermute | solution.py:352
  262.3 16.9 %collective-permute-start.14 = (bf16[512,128]{1,0:T(8,128)(2,1)}, bf16[512,128]{1,0:T(8,128)(2,1)S(1)}, u32[]{:S(2)}, u32[]{:S(2)}) collective-permute-start(bf16[512,128]{1,0:T(8,128)(2,1)} %get-tuple-element.33), channel_id=1, source_target_pairs={{0,3},{1,4},{2,5},{3,6},{4,7},{5,0},{6,1},{7,2},{8,11},{9,12},{10,... | collective-permute-start | bytes 393224 | tf_op jit(solution)/shard_map/ppermute | solution.py:352
  262.4 16.9 %collective-permute-start.15 = (bf16[512,128]{1,0:T(8,128)(2,1)}, bf16[512,128]{1,0:T(8,128)(2,1)S(1)}, u32[]{:S(2)}, u32[]{:S(2)}) collective-permute-start(bf16[512,128]{1,0:T(8,128)(2,1)} %get-tuple-element.32), channel_id=1, source_target_pairs={{0,4},{1,5},{2,6},{3,7},{4,0},{5,1},{6,2},{7,3},{8,12},{9,13},{10,... | collective-permute-start | bytes 393224 | tf_op jit(solution)/shard_map/ppermute | solution.py:352
  266.8 12.5 %collective-permute-start.16 = (bf16[512,128]{1,0:T(8,128)(2,1)S(1)}, bf16[512,128]{1,0:T(8,128)(2,1)S(1)}, u32[]{:S(2)}, u32[]{:S(2)}) collective-permute-start(bf16[512,128]{1,0:T(8,128)(2,1)S(1)} %get-tuple-element.31), channel_id=1, source_target_pairs={{0,5},{1,6},{2,7},{3,0},{4,1},{5,2},{6,3},{7,4},{8,13},{9,14},{10,... | collective-permute-start | bytes 393224 | tf_op jit(solution)/shard_map/ppermute | solution.py:352
  268.8 20.0 %copy-start.9 = (bf16[512,128]{1,0:T(8,128)(2,1)}, bf16[512,128]{1,0:T(8,128)(2,1)S(1)}, u32[]{:S(2)}) copy-start(bf16[512,128]{1,0:T(8,128)(2,1)S(1)} %collective-permute-done.12.refs_1_) | copy-start | bytes 393220
  268.8 10.5 %collective-permute-start.17 = (bf16[512,128]{1,0:T(8,128)(2,1)S(1)}, bf16[512,128]{1,0:T(8,128)(2,1)S(1)}, u32[]{:S(2)}, u32[]{:S(2)}) collective-permute-start(bf16[512,128]{1,0:T(8,128)(2,1)S(1)} %get-tuple-element.30), channel_id=1, source_target_pairs={{0,6},{1,7},{2,0},{3,1},{4,2},{5,3},{6,4},{7,5},{8,14},{9,15},{10,... | collective-permute-start | bytes 393224 | tf_op jit(solution)/shard_map/ppermute | solution.py:352
  270.0 18.7 %copy-start.10 = (bf16[512,128]{1,0:T(8,128)(2,1)}, bf16[512,128]{1,0:T(8,128)(2,1)S(1)}, u32[]{:S(2)}) copy-start(bf16[512,128]{1,0:T(8,128)(2,1)S(1)} %collective-permute-done.13.refs_2_) | copy-start | bytes 393220
  270.0 9.3 %collective-permute-start.18 = (bf16[512,128]{1,0:T(8,128)(2,1)S(1)}, bf16[512,128]{1,0:T(8,128)(2,1)S(1)}, u32[]{:S(2)}, u32[]{:S(2)}) collective-permute-start(bf16[512,128]{1,0:T(8,128)(2,1)S(1)} %get-tuple-element.29), channel_id=1, source_target_pairs={{0,7},{1,0},{2,1},{3,2},{4,3},{5,4},{6,5},{7,6},{8,15},{9,8},{10,9... | collective-permute-start | bytes 393224 | tf_op jit(solution)/shard_map/ppermute | solution.py:352
  279.2 9.5 %copy-start.11 = (bf16[512,128]{1,0:T(8,128)(2,1)}, bf16[512,128]{1,0:T(8,128)(2,1)S(1)}, u32[]{:S(2)}) copy-start(bf16[512,128]{1,0:T(8,128)(2,1)S(1)} %collective-permute-done.14.refs_3_) | copy-start | bytes 393220
  279.2 9.5 %copy-start.12 = (bf16[512,128]{1,0:T(8,128)(2,1)}, bf16[512,128]{1,0:T(8,128)(2,1)S(1)}, u32[]{:S(2)}) copy-start(bf16[512,128]{1,0:T(8,128)(2,1)S(1)} %collective-permute-done.15.refs_4_) | copy-start | bytes 393220
  (8 other events, 48.4 us)

commit v3 on v2

--- a/solution.py
+++ b/solution.py
@@ -41,13 +41,10 @@
     return cosine.astype(np.float32), sine.astype(np.float32)
 
 
-def wide_table():
-    cell = np.arange(BLOCK).reshape(GROUP, LANES, 1, 1)
-    freq = np.arange(BLOCK).reshape(1, 1, GROUP, LANES)
-    cosine, sine = unit(cell * freq, BLOCK)
-    upper = np.stack([cosine, sine], axis=3)
-    lower = np.stack([-sine, cosine], axis=3)
-    return np.stack([upper, lower], axis=1).reshape(2 * BLOCK, 2 * BLOCK).astype(jnp.bfloat16)
+def wide_tables():
+    steps = np.arange(BLOCK)
+    tables = unit(steps[:, None] * steps[None, :], BLOCK)
+    return [np.ascontiguousarray(t.reshape(BLOCK, GROUP // 2, 2 * LANES).transpose(1, 0, 2)).astype(jnp.bfloat16) for t in tables]
 
 
 def short_table():
@@ -64,11 +61,13 @@
     return cosine.astype(np.float32), sine.astype(np.float32)
 
 
-def eight(xr, xi):
+def eight(xr, xi, signs=None):
     er = [xr[c] + xr[c + 4] for c in range(4)]
     ei = [xi[c] + xi[c + 4] for c in range(4)]
     dr = [xr[c] - xr[c + 4] for c in range(4)]
     di = [xi[c] - xi[c + 4] for c in range(4)]
+    if signs is not None:
+        dr[1:], di[1:] = ([z * s for z, s in zip(d[1:], signs)] for d in (dr, di))
     evr, evi, odr, odi = er[0] + er[2], ei[0] + ei[2], er[1] + er[3], ei[1] + ei[3]
     nr, ni = (dr[1] - dr[3]) * HALF_ROOT, (di[1] - di[3]) * HALF_ROOT
     fr, fi = (dr[1] + dr[3]) * HALF_ROOT, (di[1] + di[3]) * HALF_ROOT
@@ -109,7 +108,7 @@
 
 
 def along_v_kernel(early, core_ref, place_ref, w_ref, _, *refs):
-    cells, (cos_ref, sin_ref, table_ref, out_ref, spun) = refs[:-5], refs[-5:]
+    cells, (cos_ref, sin_ref, cos_table, sin_table, out_ref, spun) = refs[:-6], refs[-6:]
     step = pl.program_id(0)
 
     @pl.when(step == 0)
@@ -131,8 +130,8 @@
                     if j:
                         tc, ts = cos_ref[j : j + 1, lanes], sin_ref[j : j + 1, lanes]
                         real, imag = real * tc - imag * ts, real * ts + imag * tc
-                    spun[j, rows, 2 * LANES * part : 2 * LANES * part + LANES] = real.astype(jnp.bfloat16)
-                    spun[j, rows, 2 * LANES * part + LANES : 2 * LANES * (part + 1)] = imag.astype(jnp.bfloat16)
+                    spun[j, 0, rows, lanes] = real.astype(jnp.bfloat16)
+                    spun[j, 1, rows, lanes] = imag.astype(jnp.bfloat16)
             return carry
 
         lax.fori_loop(0, ROWS // 16, one_tile, 0)
@@ -140,30 +139,35 @@
     shape = (ROWS, LANES)
     row = lax.broadcasted_iota(jnp.int32, shape, 0)
     q = lax.broadcasted_iota(jnp.int32, shape, 1)
+    def section(one, two):
+        return jnp.dot(one, two[0], preferred_element_type=jnp.float32)
+
     for j in range(GROUP):
-        res = jnp.dot(spun[j], table_ref[...], preferred_element_type=jnp.float32)
-        real, imag = res[:, :LANES], res[:, LANES:]
-        if early:
-            out_ref[0, j, 0] = real.astype(jnp.bfloat16)
-            out_ref[0, j, 1] = imag.astype(jnp.bfloat16)
-        else:
-            l = row // CELLS * (NPIX // 2) + row % 8 * CELLS + row // 8 % 8 + place_ref[0]
-            m = step * BLOCK + GROUP * q + j
-            image = screened(real, imag, l, m, w_ref[0].astype(jnp.float32)).astype(jnp.bfloat16)
-            out_ref[0, 0, j] = image[:CELLS]
-            out_ref[1, 0, j] = image[CELLS:]
+        both_real = section(spun[j, 0], cos_table) - section(spun[j, 1], sin_table)
+        both_imag = section(spun[j, 0], sin_table) + section(spun[j, 1], cos_table)
+        for half in range(2):
+            real, imag = (z[:, half * LANES : (half + 1) * LANES] for z in (both_real, both_imag))
+            if early:
+                out_ref[half, j, 0] = real.astype(jnp.bfloat16)
+                out_ref[half, j, 1] = imag.astype(jnp.bfloat16)
+            else:
+                l = row // CELLS * (NPIX // 2) + row % 8 * CELLS + row // 8 % 8 + place_ref[0]
+                m = (2 * step + half) * BLOCK + GROUP * q + j
+                image = screened(real, imag, l, m, w_ref[0].astype(jnp.float32)).astype(jnp.bfloat16)
+                out_ref[0, half, j] = image[:CELLS]
+                out_ref[1, half, j] = image[CELLS:]
 
 
 def along_v(early, cells, tw_cos, tw_sin, core, place, w_value, after):
     whole = lambda *shape: pl.BlockSpec(shape, lambda s, core: (0,) * len(shape))
     smem = pl.BlockSpec(memory_space=pltpu.SMEM)
     if early:
-        shape, block, index = (GROUP, GROUP, 2, ROWS, LANES), (1, GROUP, 2, ROWS, LANES), lambda s, core: (s, 0, 0, 0, 0)
+        shape, block, index = (GROUP, GROUP, 2, ROWS, LANES), (2, GROUP, 2, ROWS, LANES), lambda s, core: (s, 0, 0, 0, 0)
         pick = lambda k: pl.BlockSpec((1, ROWS, 2 * BLOCK), lambda s, core: (lax.rem(core[0] + k, 2), 0, 0))
         in_specs = [pick(k) for _ in range(GROUP // 2) for k in range(2)]
         cells = [pair for pair in cells for _ in range(2)]
     else:
-        shape, block = (LAYERS_AXIS, GROUP, GROUP, CELLS, LANES), (LAYERS_AXIS, 1, GROUP, CELLS, LANES)
+        shape, block = (LAYERS_AXIS, GROUP, GROUP, CELLS, LANES), (LAYERS_AXIS, 2, GROUP, CELLS, LANES)
         index = lambda s, core: (0, s, 0, 0, 0)
         in_specs = [whole(GROUP, GROUP, 2, ROWS, LANES)]
     return pl.pallas_call(
@@ -171,7 +175,7 @@
         out_shape=jax.ShapeDtypeStruct(shape, jnp.bfloat16),
         grid_spec=pltpu.PrefetchScalarGridSpec(
             num_scalar_prefetch=1,
-            grid=(GROUP,),
+            grid=(GROUP // 2,),
             in_specs=[
                 smem,
                 smem,
@@ -179,15 +183,15 @@
                 *in_specs,
                 whole(GROUP, BLOCK),
                 whole(GROUP, BLOCK),
-                pl.BlockSpec((2 * BLOCK, 2 * LANES), lambda s, core: (0, s)),
+                *[pl.BlockSpec((1, BLOCK, 2 * LANES), lambda s, core: (s, 0, 0))] * 2,
             ],
             out_specs=pl.BlockSpec(block, index),
-            scratch_shapes=[pltpu.VMEM((GROUP, ROWS, 2 * BLOCK), jnp.bfloat16)],
+            scratch_shapes=[pltpu.VMEM((GROUP, 2, ROWS, BLOCK), jnp.bfloat16)],
         ),
         compiler_params=pltpu.CompilerParams(vmem_limit_bytes=VMEM_LIMIT),
         cost_estimate=pl.CostEstimate(flops=2 * 1024 * 2048 * 2048, bytes_accessed=16 << 20, transcendentals=0),
         name="v_first" if early else "v_last",
-    )(core, place, w_value, after, *cells, tw_cos, tw_sin, jnp.asarray(wide_table()))
+    )(core, place, w_value, after, *cells, tw_cos, tw_sin, *[jnp.asarray(t) for t in wide_tables()])
 
 
 def along_u_kernel(early, place_ref, w_ref, _, *refs):
@@ -204,7 +208,8 @@
             else:
                 xr = [cells[0][GROUP * r + c, 0].astype(jnp.float32) for r in range(GROUP)]
                 xi = [cells[0][GROUP * r + c, 1].astype(jnp.float32) for r in range(GROUP)]
-            yr, yi = eight(xr, xi)
+            place = lax.rem(w_ref[0], 4)
+            yr, yi = eight(xr, xi, [jnp.where(place + n >= 4, -1.0, 1.0) for n in (1, 2, 3)] if early else None)
             for i in range(GROUP):
                 wr, wi = math.cos(2 * math.pi * c * i / CELLS), math.sin(2 * math.pi * c * i / CELLS)
                 if c * i == 0:
@@ -295,7 +300,7 @@
     m = lax.broadcasted_iota(jnp.int32, (LANES, BLOCK), 1)
     total = None
     for shift in range(GROUP):
-        j = lax.rem(place_ref[0] + GROUP - shift, GROUP)
+        j = lax.rem(place_ref[0] // 2 + 4 - shift // 2, 4) * 2 + lax.rem(place_ref[0] + shift, 2)
         pick = jnp.where(m == GROUP * q + j, 1.0, 0.0).astype(jnp.bfloat16)
         other = [two_ref[0, r, j].astype(jnp.float32) + two_ref[1, r, j].astype(jnp.float32) for r in range(GROUP)]
         cells = (one[shift][...].astype(jnp.float32) + jnp.concatenate(other, axis=0)).astype(jnp.bfloat16)
@@ -328,9 +333,17 @@
         out[...] = cut[0]
 
 
+def across_row(place, n):
+    return (place // 4 + n // 4) % 2 * 4 + (place + n) % 4
+
+
+def across_col(place, n):
+    return (place // 2 + n // 2) % 4 * 2 + (place + n) % 2
+
+
 def columns(grids, k, row, after):
-    rows = 128
-    cut = lambda n: pl.BlockSpec((1, rows, 2 * LANES), lambda s, place: (k, s, lax.rem(place[0] + n, GROUP)))
+    rows = 256
+    cut = lambda n: pl.BlockSpec((1, rows, 2 * LANES), lambda s, place: (k, s, across_row(place[0], n)))
     return pl.pallas_call(
         columns_kernel,
         grid_spec=pltpu.PrefetchScalarGridSpec(
@@ -340,17 +353,16 @@
             out_specs=[pl.BlockSpec((rows, 2 * LANES), lambda s, place: (s, 0))] * GROUP,
         ),
         out_shape=[jax.ShapeDtypeStruct((BLOCK, 2 * LANES), grids.dtype)] * GROUP,
+        compiler_params=pltpu.CompilerParams(vmem_limit_bytes=VMEM_LIMIT),
         name="columns",
     )(row, after, *[grids] * GROUP)
 
 
-def around(blocks, axis, chains=()):
-    before = {n: chain[i] for chain in chains for i, n in enumerate(chain[1:])}
+def around(blocks, axis, across, order):
     moved = {0: blocks[0]}
-    for n in [n for chain in chains for n in chain] or range(1, GROUP):
-        block = gate(blocks[n], moved[before[n]]) if n in before else blocks[n]
-        moved[n] = lax.ppermute(block, axis, [(c, (c + n) % GROUP) for c in range(GROUP)])
-    return [moved[-n % GROUP] for n in range(GROUP)]
+    for n in order:
+        moved[n] = lax.ppermute(blocks[n], axis, [(c, across(c, n)) for c in range(GROUP)])
+    return [moved[n] for n in range(GROUP)]
 
 
 def gate_kernel(*refs):
@@ -399,11 +411,11 @@
         if n:
             block = lax.ppermute(block, "col", [(c, (c + 2 * n) % GROUP) for c in range(GROUP)])
         half[-n % (GROUP // 2)] = block
-    other = around(columns(grids, 1, scalar(row), last), "row")
+    other = around(columns(grids, 1, scalar(row), last), "row", across_row, (3, 4, 5, 7, 6, 2, 1))
     half = along_v(True, half, *own_v, scalar(side), corner_v, w_one, w_one)
     half = gate(half, *other[1:])
-    other = [block.reshape(GROUP, ROWS, 2 * LANES) for block in other]
-    other = along_u(True, other, *own_u, corner_u, w_two, half)
+    other = [other[n // 4 * 4 + -n % 4].reshape(GROUP, ROWS, 2 * LANES) for n in range(GROUP)]
+    other = along_u(True, other, *own_u, corner_u, scalar(row), half)
     half = swap(half.reshape(CELLS, 2, ROWS, LANES), ("row", "col"))
     other = swap(other.reshape(CELLS, 2, ROWS, LANES), ("row", "col"))
 
@@ -416,9 +428,8 @@
     one = (keep.astype(jnp.float32) + send.astype(jnp.float32)).astype(jnp.bfloat16)
     two = gate(two.reshape(LAYERS_AXIS * GROUP, GROUP, CELLS, LANES), one)
     two = swap(two, ("layer", "row")).reshape(LAYERS_AXIS, GROUP, GROUP, CELLS, LANES)
-    one = [lax.dynamic_index_in_dim(one, (col + n) % GROUP, 0, keepdims=False) for n in range(GROUP)]
-    one = around(one, "col")
-    one = [one[-n % GROUP] for n in range(GROUP)]
+    one = [lax.dynamic_index_in_dim(one, across_col(col, n), 0, keepdims=False) for n in range(GROUP)]
+    one = around(one, "col", across_col, (2, 3, 6, 7, 4, 5, 1))
     return arrange(scalar(col), one, two, taper_rows, taper_cols)
 
 

time: 298 us -> 294 us (0.987)
  starting transfers between devices: 82.2 us -> 75.7 us
  waiting for transfers between devices: 112 us -> 118 us
  Pallas kernels: 80.3 us -> 77.2 us
    ppermute x14, waiting for transfers between devices: 19.5 us -> 30.1 us  [around(): lax.ppermute(blocks[n], axis, [(c, across(c, n)) for c in range(GROUP)])]
    ppermute x3, waiting for transfers between devices: 13 us -> 6.27 us  [on_device(): lax.ppermute(block, 'col', [(c, (c + 2 * n) % GROUP) for c in range(GROUP)])]
    ppermute x14, starting transfers between devices: 29.8 us -> 23.6 us  [around(): lax.ppermute(blocks[n], axis, [(c, across(c, n)) for c in range(GROUP)])]
  transfers between devices with their start and end apart: 22 -> 22, of which waited for: 10 -> 12; matrix products, arithmetic and copies ran while one was open for 4% -> 4% of each run, Pallas kernels for 25% -> 24%
where the time goes in v3:
time: 294 us; the launch traced here: 293 us
  waiting for transfers between devices  118 us (40%)
  Pallas kernels  77.2 us (26%)
  starting transfers between devices  75.7 us (26%)
  local copies, waits for them, and re-layouts  15.8 us (5%)
  other arithmetic  5.78 us (2%)
    all_to_all x3, waiting for transfers between devices, swap(): return lax.all_to_all(blocks, axes, split_axis=0, concat_axis=0, tiled=True)  76.7 us
    all_to_all x3, starting transfers between devices, swap(): return lax.all_to_all(blocks, axes, split_axis=0, concat_axis=0, tiled=True)  42.1 us
    pallas_call x2, Pallas kernels, along_v(): pl.pallas_call(functools.partial(along_v_kernel, early), out_shape=jax.Sh...  36.7 us
    ppermute x14, waiting for transfers between devices, around(): lax.ppermute(blocks[n], axis, [(c, across(c, n)) for c in range(GROUP)])  30.1 us
    pallas_call x2, Pallas kernels, along_u(): pl.pallas_call(functools.partial(along_u_kernel, early), grid=(tiles + CE...  29.6 us
    ppermute x14, starting transfers between devices, around(): lax.ppermute(blocks[n], axis, [(c, across(c, n)) for c in range(GROUP)])  23.6 us
    ppermute x3, waiting for transfers between devices, on_device(): lax.ppermute(block, 'col', [(c, (c + 2 * n) % GROUP) for c in range(GROUP)])  6.27 us
    pallas_call x1, Pallas kernels, arrange(): pl.pallas_call(arrange_kernel, out_shape=jax.ShapeDtypeStruct((8 * CELLS,...  6.07 us
  transfers between devices with their start and end apart: 22, of which 12 were waited for; matrix products, arithmetic and copies ran while one was open for 4% of the time, Pallas kernels for 24%

profile of v3, /device:TPU:0, one launch (start us, length us, event | category | flops | bytes accessed | tf_op | source)
XLA Modules:
  0.0 292.8 jit_solution(1256587818928000468)
XLA Ops:
  0.0 1.7 dynamic-slice_bitcast_fusion
  1.9 1.7 dynamic-slice_bitcast_fusion.2
  3.6 2.5 collective-permute-done
  6.1 1.7 constant_dynamic-slice_fusion
  8.9 1.7 collective-permute-start.3
  11.6 2.9 collective-permute-start.2
  16.0 4.9 %columns.1 = (bf16[1024,256]{1,0:T(8,128)(2,1)}, bf16[1024,256]{1,0:T(8,128)(2,1)}, bf16[1024,256]{1,0:T(8,128)(2,1)}, bf16[1024,256]{1,0:T(8,128)(2,1)}, bf16[1...) custom-call(s32[1]{0:T(128)} %bitcast.12._.w_ref, ...), custom_call_target="tpu_custom_call" | custom-call | tf_op jit(solution)/shard_map/columns/pallas_call | solution.py:347
  21.0 6.6 %collective-permute-start.10 = (bf16[1024,256]{1,0:T(8,128)(2,1)}, bf16[1024,256]{1,0:T(8,128)(2,1)S(1)}, u32[]{:S(2)}, u32[]{:S(2)}) collective-permute-start(bf16[1024,256]{1,0:T(8,128)(2,1)} %get-tuple-element.19), channel_id=1, source_target_pairs={{0,56},{8,32},{16,40},{24,48},{32,24},{40,0},{48,8},{56,16},{1,57}... | collective-permute-start | bytes 1572872 | tf_op jit(solution)/shard_map/ppermute | solution.py:364
  30.6 7.9 %collective-permute-done.10.refs_7_ = bf16[1024,256]{1,0:T(8,128)(2,1)S(1)} collective-permute-done((bf16[1024,256]{1,0:T(8,128)(2,1)}, bf16[1024,256]{1,0:T(8,128)(2,1)S(1)}, u32[]{:S(2)}, u32[]{:S(2)}) %collective-permute-start.10) | collective-permute-done | bytes 524320 | tf_op jit(solution)/shard_map/ppermute | solution.py:364
  38.5 2.2 collective-permute-start.5
  40.7 12.4 %collective-permute-done.4.refs_1_ = bf16[1024,256]{1,0:T(8,128)(2,1)S(1)} collective-permute-done((bf16[1024,256]{1,0:T(8,128)(2,1)}, bf16[1024,256]{1,0:T(8,128)(2,1)S(1)}, u32[]{:S(2)}, u32[]{:S(2)}) %collective-permute-start.4) | collective-permute-done | bytes 524320 | tf_op jit(solution)/shard_map/ppermute | solution.py:364
  53.1 6.3 %collective-permute-done.2.refs_4_.refs_5_ = bf16[2,128,2048]{2,1,0:T(8,128)(2,1)} collective-permute-done((bf16[2,128,2048]{2,1,0:T(8,128)(2,1)}, bf16[2,128,2048]{2,1,0:T(8,128)(2,1)}, u32[]{:S(2)}, u32[]{:S(2)}) %collective-permute-start.2) | collective-permute-done | bytes 1048608 | tf_op jit(solution)/shard_map/ppermute | solution.py:412
  59.4 4.4 %collective-permute-start.8 = (bf16[1024,256]{1,0:T(8,128)(2,1)}, bf16[1024,256]{1,0:T(8,128)(2,1)}, u32[]{:S(2)}, u32[]{:S(2)}) collective-permute-start(bf16[1024,256]{1,0:T(8,128)(2,1)} %get-tuple-element.17), channel_id=1, source_target_pairs={{0,40},{8,48},{16,56},{24,32},{32,8},{40,16},{48,24},{56,0},{1,41}... | collective-permute-start | bytes 1572872 | tf_op jit(solution)/shard_map/ppermute | solution.py:364
  63.8 3.5 %collective-permute-start.9 = (bf16[1024,256]{1,0:T(8,128)(2,1)S(1)}, bf16[1024,256]{1,0:T(8,128)(2,1)S(1)}, u32[]{:S(2)}, u32[]{:S(2)}) collective-permute-start(bf16[1024,256]{1,0:T(8,128)(2,1)S(1)} %copy-done.17), channel_id=1, source_target_pairs={{0,48},{8,56},{16,32},{24,40},{32,16},{40,24},{48,0},{56,8},{1,49}... | collective-permute-start | bytes 1572872 | tf_op jit(solution)/shard_map/ppermute | solution.py:364
  67.3 18.3 %v_first.1.refs_0_ = bf16[8,8,2,128,128]{4,3,2,1,0:T(8,128)(2,1)} custom-call(s32[1]{0:T(128)} %bitcast.2.core_ref, s32[1]{0:T(128)} %bitcast.3.place_ref, s32[1]{0:T(128)} %get-tuple-element.38.w_ref._, s32[1]{0:T(128)} %get-tuple-element.38.w_ref._, bf16[2,128,2048]{2,1,0:T(8,128)(2,1)} %pad_maximum_fusion.refs_0_.refs_1_, ...), custom_call_target="tpu_custom_call" | custom-call | flops 8589934592 | bytes 16777216 | tf_op jit(solution)/shard_map/v_first/pallas_call | solution.py:173
  85.7 4.2 %collective-permute-done.9.refs_6_ = bf16[1024,256]{1,0:T(8,128)(2,1)S(1)} collective-permute-done((bf16[1024,256]{1,0:T(8,128)(2,1)S(1)}, bf16[1024,256]{1,0:T(8,128)(2,1)S(1)}, u32[]{:S(2)}, u32[]{:S(2)}) %collective-permute-start.9) | collective-permute-done | bytes 524320 | tf_op jit(solution)/shard_map/ppermute | solution.py:364
  90.7 11.7 %all-to-all-start = ((bf16[64,2,128,128]{3,2,1,0:T(8,128)(2,1)}), bf16[64,2,128,128]{3,2,1,0:T(8,128)(2,1)}, u32[]{:S(2)}, u32[]{:S(2)}) async-start(bf16[64,2,128,128]{3,2,1,0:T(8,128)(2,1)} %bitcast.63), calls=%async_computation | async-start | bytes 8388608 | tf_op jit(solution)/shard_map/all_to_all | solution.py:384
  104.0 13.5 %u_first.1 = bf16[8,8,2,2,64,128]{5,4,3,2,1,0:T(8,128)(2,1)} custom-call(s32[1]{0:T(128)} %bitcast.1.place_ref, s32[1]{0:T(128)} %bitcast.12._.w_ref, bf16[8,8,2,128,128]{4,3,2,1,0:T(8,128)(2,1)} %gate.2._, bf16[8,128,256]{2,1,0:T(8,128)(2,1)} %bitcast.76, bf16[8,128,256]{2,1,0:T(8,128)(2,1)} %bitcast.72, bf16[8,128,256]{2,1,0:T(8,128)(2,1)} %bitcast.71, ...), custom_call_target="tpu_custom_call" | custom-call | flops 8589934592 | bytes 8388608 | tf_op jit(solution)/shard_map/u_first/pallas_call | solution.py:273
  117.5 36.1 %all-to-all-done.refs_0_ = bf16[64,2,128,128]{3,2,1,0:T(8,128)(2,1)} async-done(((bf16[64,2,128,128]{3,2,1,0:T(8,128)(2,1)}), bf16[64,2,128,128]{3,2,1,0:T(8,128)(2,1)}, u32[]{:S(2)}, u32[]{:S(2)}) %all-to-all-start) | async-done | bytes 4194336 | tf_op jit(solution)/shard_map/all_to_all | solution.py:384
  153.6 13.2 %all-to-all-start.1 = ((bf16[64,2,128,128]{3,2,1,0:T(8,128)(2,1)}), bf16[64,2,128,128]{3,2,1,0:T(8,128)(2,1)}, u32[]{:S(2)}, u32[]{:S(2)}) async-start(bf16[64,2,128,128]{3,2,1,0:T(8,128)(2,1)} %bitcast.66), calls=%async_computation.1 | async-start | bytes 8388608 | tf_op jit(solution)/shard_map/all_to_all | solution.py:384
  166.8 16.1 %u_last.1._ = bf16[16,512,128]{2,1,0:T(8,128)(2,1)} custom-call(s32[1]{0:T(128)} %bitcast.1.place_ref, s32[1]{0:T(128)} %get-tuple-element.38.w_ref._, s32[1]{0:T(128)} %get-tuple-element.38.w_ref._, bf16[64,2,128,128]{3,2,1,0:T(8,128)(2,1)} %all-to-all-done.refs_0_, f32[128,64]{1,0:T(8,128)} %constant.328.refs_1_, f32[128,64]{1,0:T(8,128)} %constant.330.refs_2_, ...), custom_call_target="tpu_custom_call" | custom-call | flops 8589934592 | bytes 8388608 | tf_op jit(solution)/shard_map/u_last/pallas_call | solution.py:273
  184.2 4.0 %collective-permute-start.11 = (bf16[8,512,128]{2,1,0:T(8,128)(2,1)S(1)}, bf16[8,512,128]{2,1,0:T(8,128)(2,1)}, u32[]{:S(2)}, u32[]{:S(2)}) collective-permute-start(bf16[8,512,128]{2,1,0:T(8,128)(2,1)S(1)} %dynamic-slice_bitcast_fusion.1), channel_id=1, source_target_pairs={{0,64},{64,0},{1,65},{65,1},{2,66},{66,2},{3,67},{67,3},{4,68},{68... | collective-permute-start | bytes 3145736 | tf_op jit(solution)/shard_map/ppermute | solution.py:427
  188.1 29.6 %all-to-all-done.1 = bf16[64,2,128,128]{3,2,1,0:T(8,128)(2,1)} async-done(((bf16[64,2,128,128]{3,2,1,0:T(8,128)(2,1)}), bf16[64,2,128,128]{3,2,1,0:T(8,128)(2,1)}, u32[]{:S(2)}, u32[]{:S(2)}) %all-to-all-start.1) | async-done | bytes 4194336 | tf_op jit(solution)/shard_map/all_to_all | solution.py:384
  217.8 18.4 %v_last.1 = bf16[2,8,8,64,128]{4,3,2,1,0:T(8,128)(2,1)} custom-call(s32[1]{0:T(128)} %bitcast.2.core_ref, s32[1]{0:T(128)} %bitcast.3.place_ref, s32[1]{0:T(128)} %get-tuple-element.37.w_ref, bf16[16,512,128]{2,1,0:T(8,128)(2,1)} %u_last.1._, bf16[8,8,2,128,128]{4,3,2,1,0:T(8,128)(2,1)} %bitcast.36.refs_0_, f32[8,1024]{1,0:T(8,128)} %constant.332.refs_1_, ...), custom_call_target="tpu_custom_call" | custom-call | flops 8589934592 | bytes 16777216 | tf_op jit(solution)/shard_map/v_last/pallas_call | solution.py:173
  236.2 2.3 collective-permute-done.11
  238.5 2.5 fusion.refs_1_
  241.0 17.1 %all-to-all-start.2 = ((bf16[16,8,64,128]{3,2,1,0:T(8,128)(2,1)}), bf16[16,8,64,128]{3,2,1,0:T(8,128)(2,1)S(1)}, u32[]{:S(2)}, u32[]{:S(2)}) async-start(bf16[16,8,64,128]{3,2,1,0:T(8,128)(2,1)} %gate.3), calls=%async_computation.2 | async-start | bytes 4194304 | tf_op jit(solution)/shard_map/all_to_all | solution.py:384
  259.1 4.5 %collective-permute-start.15 = (bf16[512,128]{1,0:T(8,128)(2,1)}, bf16[512,128]{1,0:T(8,128)(2,1)S(1)}, u32[]{:S(2)}, u32[]{:S(2)}) collective-permute-start(bf16[512,128]{1,0:T(8,128)(2,1)} %get-tuple-element.32), channel_id=1, source_target_pairs={{0,4},{1,5},{2,6},{3,7},{4,0},{5,1},{6,2},{7,3},{8,12},{9,13},{10,... | collective-permute-start | bytes 393224 | tf_op jit(solution)/shard_map/ppermute | solution.py:364
  263.6 1.8 collective-permute-start.17
  270.0 4.1 %collective-permute-done.14.refs_3_ = bf16[512,128]{1,0:T(8,128)(2,1)S(1)} collective-permute-done((bf16[512,128]{1,0:T(8,128)(2,1)}, bf16[512,128]{1,0:T(8,128)(2,1)S(1)}, u32[]{:S(2)}, u32[]{:S(2)}) %collective-permute-start.14) | collective-permute-done | bytes 131104 | tf_op jit(solution)/shard_map/ppermute | solution.py:364
  274.5 10.9 %all-to-all-done.2 = bf16[16,8,64,128]{3,2,1,0:T(8,128)(2,1)S(1)} async-done(((bf16[16,8,64,128]{3,2,1,0:T(8,128)(2,1)}), bf16[16,8,64,128]{3,2,1,0:T(8,128)(2,1)S(1)}, u32[]{:S(2)}, u32[]{:S(2)}) %all-to-all-start.2) | async-done | bytes 2097184 | tf_op jit(solution)/shard_map/all_to_all | solution.py:384
  286.8 6.1 %arrange.1 = f32[512,1024]{1,0:T(8,128)} custom-call(s32[1]{0:T(128)} %bitcast.place_ref, bf16[512,128]{1,0:T(8,128)(2,1)} %get-tuple-element.36.refs_0_, bf16[512,128]{1,0:T(8,128)(2,1)} %copy-done.9, bf16[512,128]{1,0:T(8,128)(2,1)} %copy-done.10, bf16[512,128]{1,0:T(8,128)(2,1)} %copy-done.11, bf16[512,128]{1,0:T(8,128)(2,1)} %copy-done.12, ...), custom_call_target="tpu_custom_call" | custom-call | tf_op jit(solution)/shard_map/arrange/pallas_call | solution.py:320
  (72 shorter events, 17.7 us)
Async XLA Ops:
  1.7 4.4 %collective-permute-start = (bf16[4,128,2048]{2,1,0:T(8,128)(2,1)S(1)}, bf16[4,128,2048]{2,1,0:T(8,128)(2,1)}, u32[]{:S(2)}, u32[]{:S(2)}) collective-permute-start(bf16[4,128,2048]{2,1,0:T(8,128)(2,1)S(1)} %dynamic-slice_bitcast_fusion), channel_id=1, source_target_pairs={{0,1},{1,0},{2,3},{3,2},{4,5},{5,4},{6,7},{7,6},{8,9},{9,8},{10,11... | collective-permute-start | bytes 6291464 | tf_op jit(solution)/shard_map/ppermute | solution.py:405
  8.9 44.2 %collective-permute-start.3 = (bf16[2,128,2048]{2,1,0:T(8,128)(2,1)}, bf16[2,128,2048]{2,1,0:T(8,128)(2,1)}, u32[]{:S(2)}, u32[]{:S(2)}) collective-permute-start(bf16[2,128,2048]{2,1,0:T(8,128)(2,1)} %pad_maximum_fusion.3), channel_id=1, source_target_pairs={{0,2},{1,3},{2,4},{3,5},{4,6},{5,7},{6,0},{7,1},{8,10},{9,11},{10,... | collective-permute-start | bytes 3145736 | tf_op jit(solution)/shard_map/ppermute | solution.py:412
  11.6 47.8 %collective-permute-start.2 = (bf16[2,128,2048]{2,1,0:T(8,128)(2,1)}, bf16[2,128,2048]{2,1,0:T(8,128)(2,1)}, u32[]{:S(2)}, u32[]{:S(2)}) collective-permute-start(bf16[2,128,2048]{2,1,0:T(8,128)(2,1)} %pad_maximum_fusion.2), channel_id=1, source_target_pairs={{0,4},{1,5},{2,6},{3,7},{4,0},{5,1},{6,2},{7,3},{8,12},{9,13},{10,... | collective-permute-start | bytes 3145736 | tf_op jit(solution)/shard_map/ppermute | solution.py:412
  14.6 49.2 %collective-permute-start.1 = (bf16[2,128,2048]{2,1,0:T(8,128)(2,1)S(1)}, bf16[2,128,2048]{2,1,0:T(8,128)(2,1)}, u32[]{:S(2)}, u32[]{:S(2)}) collective-permute-start(bf16[2,128,2048]{2,1,0:T(8,128)(2,1)S(1)} %pad_maximum_fusion.1.__), channel_id=1, source_target_pairs={{0,6},{1,7},{2,0},{3,1},{4,2},{5,3},{6,4},{7,5},{8,14},{9,15},{10,... | collective-permute-start | bytes 3145736 | tf_op jit(solution)/shard_map/ppermute | solution.py:412
  16.0 11.5 %copy-start.16 = (s32[2]{0:T(128)S(1)}, s32[2]{0:T(128)}, u32[]{:S(2)}) copy-start(s32[2]{0:T(128)} %param.15) | copy-start | bytes 28
  21.0 17.5 %collective-permute-start.10 = (bf16[1024,256]{1,0:T(8,128)(2,1)}, bf16[1024,256]{1,0:T(8,128)(2,1)S(1)}, u32[]{:S(2)}, u32[]{:S(2)}) collective-permute-start(bf16[1024,256]{1,0:T(8,128)(2,1)} %get-tuple-element.19), channel_id=1, source_target_pairs={{0,56},{8,32},{16,40},{24,48},{32,24},{40,0},{48,8},{56,16},{1,57}... | collective-permute-start | bytes 1572872 | tf_op jit(solution)/shard_map/ppermute | solution.py:364
  27.5 25.5 %collective-permute-start.4 = (bf16[1024,256]{1,0:T(8,128)(2,1)}, bf16[1024,256]{1,0:T(8,128)(2,1)S(1)}, u32[]{:S(2)}, u32[]{:S(2)}) collective-permute-start(bf16[1024,256]{1,0:T(8,128)(2,1)} %get-tuple-element.13), channel_id=1, source_target_pairs={{0,8},{8,16},{16,24},{24,0},{32,40},{40,48},{48,56},{56,32},{1,9},... | collective-permute-start | bytes 1572872 | tf_op jit(solution)/shard_map/ppermute | solution.py:364
  27.5 36.2 %copy-start.17 = (bf16[1024,256]{1,0:T(8,128)(2,1)S(1)}, bf16[1024,256]{1,0:T(8,128)(2,1)}, u32[]{:S(2)}) copy-start(bf16[1024,256]{1,0:T(8,128)(2,1)} %get-tuple-element.18) | copy-start | bytes 1572868
  38.5 47.1 %copy-start.4 = (bf16[1024,256]{1,0:T(8,128)(2,1)}, bf16[1024,256]{1,0:T(8,128)(2,1)S(1)}, u32[]{:S(2)}) copy-start(bf16[1024,256]{1,0:T(8,128)(2,1)S(1)} %collective-permute-done.10.refs_7_) | copy-start | bytes 1572868
  38.5 47.1 %collective-permute-start.5 = (bf16[1024,256]{1,0:T(8,128)(2,1)}, bf16[1024,256]{1,0:T(8,128)(2,1)S(1)}, u32[]{:S(2)}, u32[]{:S(2)}) collective-permute-start(bf16[1024,256]{1,0:T(8,128)(2,1)} %get-tuple-element.14), channel_id=1, source_target_pairs={{0,16},{8,24},{16,0},{24,8},{32,48},{40,56},{48,32},{56,40},{1,17}... | collective-permute-start | bytes 1572872 | tf_op jit(solution)/shard_map/ppermute | solution.py:364
  53.0 32.6 %copy-start.5 = (bf16[1024,256]{1,0:T(8,128)(2,1)}, bf16[1024,256]{1,0:T(8,128)(2,1)S(1)}, u32[]{:S(2)}) copy-start(bf16[1024,256]{1,0:T(8,128)(2,1)S(1)} %collective-permute-done.4.refs_1_) | copy-start | bytes 1572868
  53.0 32.6 %collective-permute-start.6 = (bf16[1024,256]{1,0:T(8,128)(2,1)}, bf16[1024,256]{1,0:T(8,128)(2,1)S(1)}, u32[]{:S(2)}, u32[]{:S(2)}) collective-permute-start(bf16[1024,256]{1,0:T(8,128)(2,1)} %get-tuple-element.15), channel_id=1, source_target_pairs={{0,24},{8,0},{16,8},{24,16},{32,56},{40,32},{48,40},{56,48},{1,25}... | collective-permute-start | bytes 1572872 | tf_op jit(solution)/shard_map/ppermute | solution.py:364
  53.0 32.6 %collective-permute-start.7 = (bf16[1024,256]{1,0:T(8,128)(2,1)}, bf16[1024,256]{1,0:T(8,128)(2,1)}, u32[]{:S(2)}, u32[]{:S(2)}) collective-permute-start(bf16[1024,256]{1,0:T(8,128)(2,1)} %get-tuple-element.16), channel_id=1, source_target_pairs={{0,32},{8,40},{16,48},{24,56},{32,0},{40,8},{48,16},{56,24},{1,33}... | collective-permute-start | bytes 1572872 | tf_op jit(solution)/shard_map/ppermute | solution.py:364
  59.4 26.3 %collective-permute-start.8 = (bf16[1024,256]{1,0:T(8,128)(2,1)}, bf16[1024,256]{1,0:T(8,128)(2,1)}, u32[]{:S(2)}, u32[]{:S(2)}) collective-permute-start(bf16[1024,256]{1,0:T(8,128)(2,1)} %get-tuple-element.17), channel_id=1, source_target_pairs={{0,40},{8,48},{16,56},{24,32},{32,8},{40,16},{48,24},{56,0},{1,41}... | collective-permute-start | bytes 1572872 | tf_op jit(solution)/shard_map/ppermute | solution.py:364
  63.8 26.1 %collective-permute-start.9 = (bf16[1024,256]{1,0:T(8,128)(2,1)S(1)}, bf16[1024,256]{1,0:T(8,128)(2,1)S(1)}, u32[]{:S(2)}, u32[]{:S(2)}) collective-permute-start(bf16[1024,256]{1,0:T(8,128)(2,1)S(1)} %copy-done.17), channel_id=1, source_target_pairs={{0,48},{8,56},{16,32},{24,40},{32,16},{40,24},{48,0},{56,8},{1,49}... | collective-permute-start | bytes 1572872 | tf_op jit(solution)/shard_map/ppermute | solution.py:364
  90.7 62.9 %all-to-all-start = ((bf16[64,2,128,128]{3,2,1,0:T(8,128)(2,1)}), bf16[64,2,128,128]{3,2,1,0:T(8,128)(2,1)}, u32[]{:S(2)}, u32[]{:S(2)}) async-start(bf16[64,2,128,128]{3,2,1,0:T(8,128)(2,1)} %bitcast.63), calls=%async_computation | async-start | bytes 8388608 | tf_op jit(solution)/shard_map/all_to_all | solution.py:384
  153.6 64.2 %all-to-all-start.1 = ((bf16[64,2,128,128]{3,2,1,0:T(8,128)(2,1)}), bf16[64,2,128,128]{3,2,1,0:T(8,128)(2,1)}, u32[]{:S(2)}, u32[]{:S(2)}) async-start(bf16[64,2,128,128]{3,2,1,0:T(8,128)(2,1)} %bitcast.66), calls=%async_computation.1 | async-start | bytes 8388608 | tf_op jit(solution)/shard_map/all_to_all | solution.py:384
  184.2 54.4 %collective-permute-start.11 = (bf16[8,512,128]{2,1,0:T(8,128)(2,1)S(1)}, bf16[8,512,128]{2,1,0:T(8,128)(2,1)}, u32[]{:S(2)}, u32[]{:S(2)}) collective-permute-start(bf16[8,512,128]{2,1,0:T(8,128)(2,1)S(1)} %dynamic-slice_bitcast_fusion.1), channel_id=1, source_target_pairs={{0,64},{64,0},{1,65},{65,1},{2,66},{66,2},{3,67},{67,3},{4,68},{68... | collective-permute-start | bytes 3145736 | tf_op jit(solution)/shard_map/ppermute | solution.py:427
  217.8 20.8 %copy-start.3 = (bf16[16,512,128]{2,1,0:T(8,128)(2,1)S(1)}, bf16[16,512,128]{2,1,0:T(8,128)(2,1)}, u32[]{:S(2)}) copy-start(bf16[16,512,128]{2,1,0:T(8,128)(2,1)} %u_last.1._) | copy-start | bytes 6291460
  241.0 17.2 %copy-start = (bf16[8,512,128]{2,1,0:T(8,128)(2,1)S(1)}, bf16[8,512,128]{2,1,0:T(8,128)(2,1)}, u32[]{:S(2)}) copy-start(bf16[8,512,128]{2,1,0:T(8,128)(2,1)} %fusion.refs_1_) | copy-start | bytes 3145732
  241.0 44.4 %all-to-all-start.2 = ((bf16[16,8,64,128]{3,2,1,0:T(8,128)(2,1)}), bf16[16,8,64,128]{3,2,1,0:T(8,128)(2,1)S(1)}, u32[]{:S(2)}, u32[]{:S(2)}) async-start(bf16[16,8,64,128]{3,2,1,0:T(8,128)(2,1)} %gate.3), calls=%async_computation.2 | async-start | bytes 4194304 | tf_op jit(solution)/shard_map/all_to_all | solution.py:384
  259.0 4.5 %collective-permute-start.12 = (bf16[512,128]{1,0:T(8,128)(2,1)S(1)}, bf16[512,128]{1,0:T(8,128)(2,1)S(1)}, u32[]{:S(2)}, u32[]{:S(2)}) collective-permute-start(bf16[512,128]{1,0:T(8,128)(2,1)S(1)} %get-tuple-element.35), channel_id=1, source_target_pairs={{0,1},{1,0},{2,3},{3,2},{4,5},{5,4},{6,7},{7,6},{8,9},{9,8},{10,11... | collective-permute-start | bytes 393224 | tf_op jit(solution)/shard_map/ppermute | solution.py:364
  259.0 7.5 %collective-permute-start.13 = (bf16[512,128]{1,0:T(8,128)(2,1)S(1)}, bf16[512,128]{1,0:T(8,128)(2,1)S(1)}, u32[]{:S(2)}, u32[]{:S(2)}) collective-permute-start(bf16[512,128]{1,0:T(8,128)(2,1)S(1)} %get-tuple-element.34), channel_id=1, source_target_pairs={{0,2},{1,3},{2,4},{3,5},{4,6},{5,7},{6,0},{7,1},{8,10},{9,11},{10,... | collective-permute-start | bytes 393224 | tf_op jit(solution)/shard_map/ppermute | solution.py:364
  259.0 15.2 %collective-permute-start.14 = (bf16[512,128]{1,0:T(8,128)(2,1)}, bf16[512,128]{1,0:T(8,128)(2,1)S(1)}, u32[]{:S(2)}, u32[]{:S(2)}) collective-permute-start(bf16[512,128]{1,0:T(8,128)(2,1)} %get-tuple-element.33), channel_id=1, source_target_pairs={{0,3},{1,2},{2,5},{3,4},{4,7},{5,6},{6,1},{7,0},{8,11},{9,10},{10,... | collective-permute-start | bytes 393224 | tf_op jit(solution)/shard_map/ppermute | solution.py:364
  259.1 15.1 %collective-permute-start.15 = (bf16[512,128]{1,0:T(8,128)(2,1)}, bf16[512,128]{1,0:T(8,128)(2,1)S(1)}, u32[]{:S(2)}, u32[]{:S(2)}) collective-permute-start(bf16[512,128]{1,0:T(8,128)(2,1)} %get-tuple-element.32), channel_id=1, source_target_pairs={{0,4},{1,5},{2,6},{3,7},{4,0},{5,1},{6,2},{7,3},{8,12},{9,13},{10,... | collective-permute-start | bytes 393224 | tf_op jit(solution)/shard_map/ppermute | solution.py:364
  263.6 10.6 %collective-permute-start.16 = (bf16[512,128]{1,0:T(8,128)(2,1)S(1)}, bf16[512,128]{1,0:T(8,128)(2,1)S(1)}, u32[]{:S(2)}, u32[]{:S(2)}) collective-permute-start(bf16[512,128]{1,0:T(8,128)(2,1)S(1)} %get-tuple-element.31), channel_id=1, source_target_pairs={{0,5},{1,4},{2,7},{3,6},{4,1},{5,0},{6,3},{7,2},{8,13},{9,12},{10,... | collective-permute-start | bytes 393224 | tf_op jit(solution)/shard_map/ppermute | solution.py:364
  263.6 21.9 %copy-start.9 = (bf16[512,128]{1,0:T(8,128)(2,1)}, bf16[512,128]{1,0:T(8,128)(2,1)S(1)}, u32[]{:S(2)}) copy-start(bf16[512,128]{1,0:T(8,128)(2,1)S(1)} %collective-permute-done.12.refs_1_) | copy-start | bytes 393220
  263.6 10.6 %collective-permute-start.17 = (bf16[512,128]{1,0:T(8,128)(2,1)S(1)}, bf16[512,128]{1,0:T(8,128)(2,1)S(1)}, u32[]{:S(2)}, u32[]{:S(2)}) collective-permute-start(bf16[512,128]{1,0:T(8,128)(2,1)S(1)} %get-tuple-element.30), channel_id=1, source_target_pairs={{0,6},{1,7},{2,0},{3,1},{4,2},{5,3},{6,4},{7,5},{8,14},{9,15},{10,... | collective-permute-start | bytes 393224 | tf_op jit(solution)/shard_map/ppermute | solution.py:364
  266.5 18.9 %copy-start.10 = (bf16[512,128]{1,0:T(8,128)(2,1)}, bf16[512,128]{1,0:T(8,128)(2,1)S(1)}, u32[]{:S(2)}) copy-start(bf16[512,128]{1,0:T(8,128)(2,1)S(1)} %collective-permute-done.13.refs_2_) | copy-start | bytes 393220
  266.5 8.0 %collective-permute-start.18 = (bf16[512,128]{1,0:T(8,128)(2,1)S(1)}, bf16[512,128]{1,0:T(8,128)(2,1)S(1)}, u32[]{:S(2)}, u32[]{:S(2)}) collective-permute-start(bf16[512,128]{1,0:T(8,128)(2,1)S(1)} %get-tuple-element.29), channel_id=1, source_target_pairs={{0,7},{1,6},{2,1},{3,0},{4,3},{5,2},{6,5},{7,4},{8,15},{9,14},{10,... | collective-permute-start | bytes 393224 | tf_op jit(solution)/shard_map/ppermute | solution.py:364
  274.2 11.3 %copy-start.12 = (bf16[512,128]{1,0:T(8,128)(2,1)}, bf16[512,128]{1,0:T(8,128)(2,1)S(1)}, u32[]{:S(2)}) copy-start(bf16[512,128]{1,0:T(8,128)(2,1)S(1)} %collective-permute-done.15.refs_4_) | copy-start | bytes 393220
  274.2 11.3 %copy-start.13 = (bf16[512,128]{1,0:T(8,128)(2,1)}, bf16[512,128]{1,0:T(8,128)(2,1)S(1)}, u32[]{:S(2)}) copy-start(bf16[512,128]{1,0:T(8,128)(2,1)S(1)} %collective-permute-done.16.refs_5_) | copy-start | bytes 393220
  (8 other events, 45.6 us)

commit v4 on v3

--- a/solution.py
+++ b/solution.py
@@ -403,15 +403,23 @@
     take = lambda k: lax.dynamic_slice(cells, (0, 0, k, 0, 0), (1, GROUP // 2, 1, ROWS, 2 * BLOCK))
     mine, give = (take(k).reshape(GROUP // 2, ROWS, 2 * BLOCK) for k in (side, 1 - side))
     got = lax.ppermute(give, "col", [(c, c ^ 1) for c in range(GROUP)])
-    half = [None] * (GROUP // 2)
-    for n in range(GROUP // 2):
+    half = {}
+
+    def along_y(n, *earlier):
         target = (place_y + n) % (GROUP // 2)
         block = jnp.stack([lax.dynamic_index_in_dim(t, target, 0, keepdims=False) for t in (mine, got)])
-        last = block
-        if n:
-            block = lax.ppermute(block, "col", [(c, (c + 2 * n) % GROUP) for c in range(GROUP)])
-        half[-n % (GROUP // 2)] = block
-    other = around(columns(grids, 1, scalar(row), last), "row", across_row, (3, 4, 5, 7, 6, 2, 1))
+        if earlier:
+            block = gate(block, *earlier)
+        moved = lax.ppermute(block, "col", [(c, (c + 2 * n) % GROUP) for c in range(GROUP)]) if n else block
+        half[-n % (GROUP // 2)] = moved
+        return block
+
+    along_y(1)
+    begun = along_y(3)
+    other = around(columns(grids, 1, scalar(row), begun), "row", across_row, (1, 3, 4, 5, 7, 2, 6))
+    along_y(2, half[1], half[3], other[1], other[3], other[4])
+    along_y(0)
+    half = [half[n] for n in range(GROUP // 2)]
     half = along_v(True, half, *own_v, scalar(side), corner_v, w_one, w_one)
     half = gate(half, *other[1:])
     other = [other[n // 4 * 4 + -n % 4].reshape(GROUP, ROWS, 2 * LANES) for n in range(GROUP)]

time: 294 us -> 286 us (0.973)
  waiting for transfers between devices: 118 us -> 107 us
  local copies, waits for them, and re-layouts: 15.8 us -> 19.3 us
    ppermute x14, waiting for transfers between devices: 30.1 us -> 18.2 us  [around(): lax.ppermute(blocks[n], axis, [(c, across(c, n)) for c in range(GROUP)])]
    all_to_all x3, starting transfers between devices: 42.1 us -> 38.3 us  [swap(): return lax.all_to_all(blocks, axes, split_axis=0, concat_axis=0, tiled=True)]
  transfers between devices with their start and end apart: 22 -> 22, of which waited for: 12 -> 12; matrix products, arithmetic and copies ran while one was open for 4% -> 5% of each run, Pallas kernels for 24% -> 25%
where the time goes in v4:
time: 286 us; the launch traced here: 285 us
  waiting for transfers between devices  107 us (37%)
  Pallas kernels  77.6 us (27%)
  starting transfers between devices  73.2 us (26%)
  local copies, waits for them, and re-layouts  19.3 us (7%)
  other arithmetic  7.85 us (3%)
    all_to_all x3, waiting for transfers between devices, swap(): return lax.all_to_all(blocks, axes, split_axis=0, concat_axis=0, tiled=True)  76.5 us
    all_to_all x3, starting transfers between devices, swap(): return lax.all_to_all(blocks, axes, split_axis=0, concat_axis=0, tiled=True)  38.3 us
    pallas_call x2, Pallas kernels, along_v(): pl.pallas_call(functools.partial(along_v_kernel, early), out_shape=jax.Sh...  36.8 us
    pallas_call x2, Pallas kernels, along_u(): pl.pallas_call(functools.partial(along_u_kernel, early), grid=(tiles + CE...  29.7 us
    ppermute x14, starting transfers between devices, around(): lax.ppermute(blocks[n], axis, [(c, across(c, n)) for c in range(GROUP)])  25.2 us
    ppermute x14, waiting for transfers between devices, around(): lax.ppermute(blocks[n], axis, [(c, across(c, n)) for c in range(GROUP)])  18.2 us
    ppermute x3, waiting for transfers between devices, along_y(): lax.ppermute(block, 'col', [(c, (c + 2 * n) % GROUP) for c in range(GROUP)])  7.86 us
    pallas_call x1, Pallas kernels, arrange(): pl.pallas_call(arrange_kernel, out_shape=jax.ShapeDtypeStruct((8 * CELLS,...  6.07 us
  transfers between devices with their start and end apart: 22, of which 12 were waited for; matrix products, arithmetic and copies ran while one was open for 5% of the time, Pallas kernels for 25%

profile of v4, /device:TPU:0, one launch (start us, length us, event | category | flops | bytes accessed | tf_op | source)
XLA Modules:
  0.0 285.0 jit_solution(1704287884826102517)
XLA Ops:
  1.9 2.5 dynamic-slice_bitcast_fusion.2
  6.1 2.7 constant_dynamic-slice_fusion
  13.3 5.0 %columns.1 = (bf16[1024,256]{1,0:T(8,128)(2,1)}, bf16[1024,256]{1,0:T(8,128)(2,1)}, bf16[1024,256]{1,0:T(8,128)(2,1)}, bf16[1024,256]{1,0:T(8,128)(2,1)}, bf16[1...) custom-call(s32[1]{0:T(128)} %bitcast.10._.w_ref, ...), custom_call_target="tpu_custom_call" | custom-call | tf_op jit(solution)/shard_map/columns/pallas_call | solution.py:347
  18.3 2.1 collective-permute-start.3
  20.3 2.2 collective-permute-start.4
  22.5 3.0 %collective-permute-start.5 = (bf16[1024,256]{1,0:T(8,128)(2,1)}, bf16[1024,256]{1,0:T(8,128)(2,1)S(1)}, u32[]{:S(2)}, u32[]{:S(2)}) collective-permute-start(bf16[1024,256]{1,0:T(8,128)(2,1)} %get-tuple-element.15), channel_id=1, source_target_pairs={{0,32},{8,40},{16,48},{24,56},{32,0},{40,8},{48,16},{56,24},{1,33}... | collective-permute-start | bytes 1572872 | tf_op jit(solution)/shard_map/ppermute | solution.py:364
  25.6 2.1 pad_maximum_fusion.2.refs_0_
  27.7 6.7 %collective-permute-done.3.refs_3_.refs_1_ = bf16[1024,256]{1,0:T(8,128)(2,1)S(1)} collective-permute-done((bf16[1024,256]{1,0:T(8,128)(2,1)}, bf16[1024,256]{1,0:T(8,128)(2,1)S(1)}, u32[]{:S(2)}, u32[]{:S(2)}) %collective-permute-start.3) | collective-permute-done | bytes 524320 | tf_op jit(solution)/shard_map/ppermute | solution.py:364
  34.4 3.0 %collective-permute-done.5.refs_5_.refs_4_ = bf16[1024,256]{1,0:T(8,128)(2,1)S(1)} collective-permute-done((bf16[1024,256]{1,0:T(8,128)(2,1)}, bf16[1024,256]{1,0:T(8,128)(2,1)S(1)}, u32[]{:S(2)}, u32[]{:S(2)}) %collective-permute-start.5) | collective-permute-done | bytes 524320 | tf_op jit(solution)/shard_map/ppermute | solution.py:364
  38.2 2.3 collective-permute-start.6
  42.6 5.7 %collective-permute-start.10 = (bf16[1024,256]{1,0:T(8,128)(2,1)}, bf16[1024,256]{1,0:T(8,128)(2,1)S(1)}, u32[]{:S(2)}, u32[]{:S(2)}) collective-permute-start(bf16[1024,256]{1,0:T(8,128)(2,1)} %get-tuple-element.19), channel_id=1, source_target_pairs={{0,56},{8,32},{16,40},{24,48},{32,24},{40,0},{48,8},{56,16},{1,57}... | collective-permute-start | bytes 1572872 | tf_op jit(solution)/shard_map/ppermute | solution.py:364
  49.4 4.1 %collective-permute-start.9 = (bf16[1024,256]{1,0:T(8,128)(2,1)}, bf16[1024,256]{1,0:T(8,128)(2,1)S(1)}, u32[]{:S(2)}, u32[]{:S(2)}) collective-permute-start(bf16[1024,256]{1,0:T(8,128)(2,1)} %get-tuple-element.18), channel_id=1, source_target_pairs={{0,48},{8,56},{16,32},{24,40},{32,16},{40,24},{48,0},{56,8},{1,49}... | collective-permute-start | bytes 1572872 | tf_op jit(solution)/shard_map/ppermute | solution.py:364
  53.6 2.1 pad_maximum_fusion.refs_0_.refs_1_
  55.7 7.9 %collective-permute-done.6.refs_4_.refs_5_ = bf16[2,128,2048]{2,1,0:T(8,128)(2,1)} collective-permute-done((bf16[2,128,2048]{2,1,0:T(8,128)(2,1)}, bf16[2,128,2048]{2,1,0:T(8,128)(2,1)}, u32[]{:S(2)}, u32[]{:S(2)}) %collective-permute-start.6) | collective-permute-done | bytes 1048608 | tf_op jit(solution)/shard_map/ppermute | solution.py:413
  63.6 18.5 %v_first.1.refs_0_ = bf16[8,8,2,128,128]{4,3,2,1,0:T(8,128)(2,1)} custom-call(s32[1]{0:T(128)} %bitcast.2.core_ref, s32[1]{0:T(128)} %bitcast.3.place_ref, s32[1]{0:T(128)} %get-tuple-element.38.w_ref._, s32[1]{0:T(128)} %get-tuple-element.38.w_ref._, bf16[2,128,2048]{2,1,0:T(8,128)(2,1)} %pad_maximum_fusion.refs_0_.refs_1_, ...), custom_call_target="tpu_custom_call" | custom-call | flops 8589934592 | bytes 16777216 | tf_op jit(solution)/shard_map/v_first/pallas_call | solution.py:173
  82.0 2.8 collective-permute-done.7.refs_2_
  86.7 8.0 %all-to-all-start = ((bf16[64,2,128,128]{3,2,1,0:T(8,128)(2,1)}), bf16[64,2,128,128]{3,2,1,0:T(8,128)(2,1)}, u32[]{:S(2)}, u32[]{:S(2)}) async-start(bf16[64,2,128,128]{3,2,1,0:T(8,128)(2,1)} %bitcast.63), calls=%async_computation | async-start | bytes 8388608 | tf_op jit(solution)/shard_map/all_to_all | solution.py:384
  96.2 13.5 %u_first.1 = bf16[8,8,2,2,64,128]{5,4,3,2,1,0:T(8,128)(2,1)} custom-call(s32[1]{0:T(128)} %bitcast.1.place_ref, s32[1]{0:T(128)} %bitcast.10._.w_ref, bf16[8,8,2,128,128]{4,3,2,1,0:T(8,128)(2,1)} %gate.4._, bf16[8,128,256]{2,1,0:T(8,128)(2,1)} %bitcast.78, bf16[8,128,256]{2,1,0:T(8,128)(2,1)} %bitcast.70, bf16[8,128,256]{2,1,0:T(8,128)(2,1)} %bitcast.73, ...), custom_call_target="tpu_custom_call" | custom-call | flops 8589934592 | bytes 8388608 | tf_op jit(solution)/shard_map/u_first/pallas_call | solution.py:273
  109.7 36.1 %all-to-all-done.refs_0_ = bf16[64,2,128,128]{3,2,1,0:T(8,128)(2,1)} async-done(((bf16[64,2,128,128]{3,2,1,0:T(8,128)(2,1)}), bf16[64,2,128,128]{3,2,1,0:T(8,128)(2,1)}, u32[]{:S(2)}, u32[]{:S(2)}) %all-to-all-start) | async-done | bytes 4194336 | tf_op jit(solution)/shard_map/all_to_all | solution.py:384
  145.8 13.2 %all-to-all-start.1 = ((bf16[64,2,128,128]{3,2,1,0:T(8,128)(2,1)}), bf16[64,2,128,128]{3,2,1,0:T(8,128)(2,1)}, u32[]{:S(2)}, u32[]{:S(2)}) async-start(bf16[64,2,128,128]{3,2,1,0:T(8,128)(2,1)} %bitcast.66), calls=%async_computation.1 | async-start | bytes 8388608 | tf_op jit(solution)/shard_map/all_to_all | solution.py:384
  159.0 16.2 %u_last.1._ = bf16[16,512,128]{2,1,0:T(8,128)(2,1)} custom-call(s32[1]{0:T(128)} %bitcast.1.place_ref, s32[1]{0:T(128)} %get-tuple-element.38.w_ref._, s32[1]{0:T(128)} %get-tuple-element.38.w_ref._, bf16[64,2,128,128]{3,2,1,0:T(8,128)(2,1)} %all-to-all-done.refs_0_, f32[128,64]{1,0:T(8,128)} %constant.328.refs_1_, f32[128,64]{1,0:T(8,128)} %constant.330.refs_2_, ...), custom_call_target="tpu_custom_call" | custom-call | flops 8589934592 | bytes 8388608 | tf_op jit(solution)/shard_map/u_last/pallas_call | solution.py:273
  176.6 3.9 %collective-permute-start.11 = (bf16[8,512,128]{2,1,0:T(8,128)(2,1)S(1)}, bf16[8,512,128]{2,1,0:T(8,128)(2,1)}, u32[]{:S(2)}, u32[]{:S(2)}) collective-permute-start(bf16[8,512,128]{2,1,0:T(8,128)(2,1)S(1)} %dynamic-slice_bitcast_fusion.1), channel_id=1, source_target_pairs={{0,64},{64,0},{1,65},{65,1},{2,66},{66,2},{3,67},{67,3},{4,68},{68... | collective-permute-start | bytes 3145736 | tf_op jit(solution)/shard_map/ppermute | solution.py:435
  180.5 29.5 %all-to-all-done.1 = bf16[64,2,128,128]{3,2,1,0:T(8,128)(2,1)} async-done(((bf16[64,2,128,128]{3,2,1,0:T(8,128)(2,1)}), bf16[64,2,128,128]{3,2,1,0:T(8,128)(2,1)}, u32[]{:S(2)}, u32[]{:S(2)}) %all-to-all-start.1) | async-done | bytes 4194336 | tf_op jit(solution)/shard_map/all_to_all | solution.py:384
  210.0 18.4 %v_last.1 = bf16[2,8,8,64,128]{4,3,2,1,0:T(8,128)(2,1)} custom-call(s32[1]{0:T(128)} %bitcast.2.core_ref, s32[1]{0:T(128)} %bitcast.3.place_ref, s32[1]{0:T(128)} %get-tuple-element.37.w_ref, bf16[16,512,128]{2,1,0:T(8,128)(2,1)} %u_last.1._, bf16[8,8,2,128,128]{4,3,2,1,0:T(8,128)(2,1)} %bitcast.36.refs_0_, f32[8,1024]{1,0:T(8,128)} %constant.332.refs_1_, ...), custom_call_target="tpu_custom_call" | custom-call | flops 8589934592 | bytes 16777216 | tf_op jit(solution)/shard_map/v_last/pallas_call | solution.py:173
  228.4 2.4 collective-permute-done.11
  230.7 2.5 fusion.refs_1_
  233.2 17.1 %all-to-all-start.2 = ((bf16[16,8,64,128]{3,2,1,0:T(8,128)(2,1)}), bf16[16,8,64,128]{3,2,1,0:T(8,128)(2,1)S(1)}, u32[]{:S(2)}, u32[]{:S(2)}) async-start(bf16[16,8,64,128]{3,2,1,0:T(8,128)(2,1)} %gate.5), calls=%async_computation.2 | async-start | bytes 4194304 | tf_op jit(solution)/shard_map/all_to_all | solution.py:384
  251.3 4.5 %collective-permute-start.15 = (bf16[512,128]{1,0:T(8,128)(2,1)}, bf16[512,128]{1,0:T(8,128)(2,1)S(1)}, u32[]{:S(2)}, u32[]{:S(2)}) collective-permute-start(bf16[512,128]{1,0:T(8,128)(2,1)} %get-tuple-element.32), channel_id=1, source_target_pairs={{0,4},{1,5},{2,6},{3,7},{4,0},{5,1},{6,2},{7,3},{8,12},{9,13},{10,... | collective-permute-start | bytes 393224 | tf_op jit(solution)/shard_map/ppermute | solution.py:364
  255.8 1.8 collective-permute-start.17
  262.2 4.1 %collective-permute-done.14.refs_3_ = bf16[512,128]{1,0:T(8,128)(2,1)S(1)} collective-permute-done((bf16[512,128]{1,0:T(8,128)(2,1)}, bf16[512,128]{1,0:T(8,128)(2,1)S(1)}, u32[]{:S(2)}, u32[]{:S(2)}) %collective-permute-start.14) | collective-permute-done | bytes 131104 | tf_op jit(solution)/shard_map/ppermute | solution.py:364
  266.7 10.9 %all-to-all-done.2 = bf16[16,8,64,128]{3,2,1,0:T(8,128)(2,1)S(1)} async-done(((bf16[16,8,64,128]{3,2,1,0:T(8,128)(2,1)}), bf16[16,8,64,128]{3,2,1,0:T(8,128)(2,1)S(1)}, u32[]{:S(2)}, u32[]{:S(2)}) %all-to-all-start.2) | async-done | bytes 2097184 | tf_op jit(solution)/shard_map/all_to_all | solution.py:384
  279.0 6.1 %arrange.1 = f32[512,1024]{1,0:T(8,128)} custom-call(s32[1]{0:T(128)} %bitcast.place_ref, bf16[512,128]{1,0:T(8,128)(2,1)} %get-tuple-element.36.refs_0_, bf16[512,128]{1,0:T(8,128)(2,1)} %copy-done.12, bf16[512,128]{1,0:T(8,128)(2,1)} %copy-done.13, bf16[512,128]{1,0:T(8,128)(2,1)} %copy-done.14, bf16[512,128]{1,0:T(8,128)(2,1)} %copy-done.15, ...), custom_call_target="tpu_custom_call" | custom-call | tf_op jit(solution)/shard_map/arrange/pallas_call | solution.py:320
  (77 shorter events, 23.7 us)
Async XLA Ops:
  1.7 4.4 %collective-permute-start = (bf16[4,128,2048]{2,1,0:T(8,128)(2,1)S(1)}, bf16[4,128,2048]{2,1,0:T(8,128)(2,1)}, u32[]{:S(2)}, u32[]{:S(2)}) collective-permute-start(bf16[4,128,2048]{2,1,0:T(8,128)(2,1)S(1)} %dynamic-slice_bitcast_fusion), channel_id=1, source_target_pairs={{0,1},{1,0},{2,3},{3,2},{4,5},{5,4},{6,7},{7,6},{8,9},{9,8},{10,11... | collective-permute-start | bytes 6291464 | tf_op jit(solution)/shard_map/ppermute | solution.py:405
  9.9 27.6 %collective-permute-start.2 = (bf16[2,128,2048]{2,1,0:T(8,128)(2,1)}, bf16[2,128,2048]{2,1,0:T(8,128)(2,1)}, u32[]{:S(2)}, u32[]{:S(2)}) collective-permute-start(bf16[2,128,2048]{2,1,0:T(8,128)(2,1)} %pad_maximum_fusion.3), channel_id=1, source_target_pairs={{0,2},{1,3},{2,4},{3,5},{4,6},{5,7},{6,0},{7,1},{8,10},{9,11},{10,... | collective-permute-start | bytes 3145736 | tf_op jit(solution)/shard_map/ppermute | solution.py:413
  11.7 25.8 %collective-permute-start.1 = (bf16[2,128,2048]{2,1,0:T(8,128)(2,1)S(1)}, bf16[2,128,2048]{2,1,0:T(8,128)(2,1)}, u32[]{:S(2)}, u32[]{:S(2)}) collective-permute-start(bf16[2,128,2048]{2,1,0:T(8,128)(2,1)S(1)} %pad_maximum_fusion.1.__), channel_id=1, source_target_pairs={{0,6},{1,7},{2,0},{3,1},{4,2},{5,3},{6,4},{7,5},{8,14},{9,15},{10,... | collective-permute-start | bytes 3145736 | tf_op jit(solution)/shard_map/ppermute | solution.py:413
  13.3 12.3 %copy-start.7 = (bf16[1,128,2048]{2,1,0:T(8,128)(2,1)S(1)}, bf16[1,128,2048]{2,1,0:T(8,128)(2,1)}, u32[]{:S(2)}) copy-start(bf16[1,128,2048]{2,1,0:T(8,128)(2,1)} %get-tuple-element.22) | copy-start | bytes 1572868
  18.3 16.1 %collective-permute-start.3 = (bf16[1024,256]{1,0:T(8,128)(2,1)}, bf16[1024,256]{1,0:T(8,128)(2,1)S(1)}, u32[]{:S(2)}, u32[]{:S(2)}) collective-permute-start(bf16[1024,256]{1,0:T(8,128)(2,1)} %get-tuple-element.13), channel_id=1, source_target_pairs={{0,8},{8,16},{16,24},{24,0},{32,40},{40,48},{48,56},{56,32},{1,9},... | collective-permute-start | bytes 1572872 | tf_op jit(solution)/shard_map/ppermute | solution.py:364
  20.3 14.1 %collective-permute-start.4 = (bf16[1024,256]{1,0:T(8,128)(2,1)}, bf16[1024,256]{1,0:T(8,128)(2,1)S(1)}, u32[]{:S(2)}, u32[]{:S(2)}) collective-permute-start(bf16[1024,256]{1,0:T(8,128)(2,1)} %get-tuple-element.14), channel_id=1, source_target_pairs={{0,24},{8,0},{16,8},{24,16},{32,56},{40,32},{48,40},{56,48},{1,25}... | collective-permute-start | bytes 1572872 | tf_op jit(solution)/shard_map/ppermute | solution.py:364
  22.5 14.9 %collective-permute-start.5 = (bf16[1024,256]{1,0:T(8,128)(2,1)}, bf16[1024,256]{1,0:T(8,128)(2,1)S(1)}, u32[]{:S(2)}, u32[]{:S(2)}) collective-permute-start(bf16[1024,256]{1,0:T(8,128)(2,1)} %get-tuple-element.15), channel_id=1, source_target_pairs={{0,32},{8,40},{16,48},{24,56},{32,0},{40,8},{48,16},{56,24},{1,33}... | collective-permute-start | bytes 1572872 | tf_op jit(solution)/shard_map/ppermute | solution.py:364
  27.7 12.9 %copy-start.19 = (s32[2]{0:T(128)S(1)}, s32[2]{0:T(128)}, u32[]{:S(2)}) copy-start(s32[2]{0:T(128)} %param.15) | copy-start | bytes 28
  38.2 25.3 %collective-permute-start.6 = (bf16[2,128,2048]{2,1,0:T(8,128)(2,1)}, bf16[2,128,2048]{2,1,0:T(8,128)(2,1)}, u32[]{:S(2)}, u32[]{:S(2)}) collective-permute-start(bf16[2,128,2048]{2,1,0:T(8,128)(2,1)} %gate.3), channel_id=1, source_target_pairs={{0,4},{1,5},{2,6},{3,7},{4,0},{5,1},{6,2},{7,3},{8,12},{9,13},{10,... | collective-permute-start | bytes 3145736 | tf_op jit(solution)/shard_map/ppermute | solution.py:413
  42.6 39.5 %collective-permute-start.10 = (bf16[1024,256]{1,0:T(8,128)(2,1)}, bf16[1024,256]{1,0:T(8,128)(2,1)S(1)}, u32[]{:S(2)}, u32[]{:S(2)}) collective-permute-start(bf16[1024,256]{1,0:T(8,128)(2,1)} %get-tuple-element.19), channel_id=1, source_target_pairs={{0,56},{8,32},{16,40},{24,48},{32,24},{40,0},{48,8},{56,16},{1,57}... | collective-permute-start | bytes 1572872 | tf_op jit(solution)/shard_map/ppermute | solution.py:364
  48.2 36.6 %collective-permute-start.7 = (bf16[1024,256]{1,0:T(8,128)(2,1)}, bf16[1024,256]{1,0:T(8,128)(2,1)S(1)}, u32[]{:S(2)}, u32[]{:S(2)}) collective-permute-start(bf16[1024,256]{1,0:T(8,128)(2,1)} %get-tuple-element.16), channel_id=1, source_target_pairs={{0,16},{8,24},{16,0},{24,8},{32,48},{40,56},{48,32},{56,40},{1,17}... | collective-permute-start | bytes 1572872 | tf_op jit(solution)/shard_map/ppermute | solution.py:364
  48.2 36.6 %collective-permute-start.8 = (bf16[1024,256]{1,0:T(8,128)(2,1)}, bf16[1024,256]{1,0:T(8,128)(2,1)S(1)}, u32[]{:S(2)}, u32[]{:S(2)}) collective-permute-start(bf16[1024,256]{1,0:T(8,128)(2,1)} %get-tuple-element.17), channel_id=1, source_target_pairs={{0,40},{8,48},{16,56},{24,32},{32,8},{40,16},{48,24},{56,0},{1,41}... | collective-permute-start | bytes 1572872 | tf_op jit(solution)/shard_map/ppermute | solution.py:364
  49.4 35.4 %collective-permute-start.9 = (bf16[1024,256]{1,0:T(8,128)(2,1)}, bf16[1024,256]{1,0:T(8,128)(2,1)S(1)}, u32[]{:S(2)}, u32[]{:S(2)}) collective-permute-start(bf16[1024,256]{1,0:T(8,128)(2,1)} %get-tuple-element.18), channel_id=1, source_target_pairs={{0,48},{8,56},{16,32},{24,40},{32,16},{40,24},{48,0},{56,8},{1,49}... | collective-permute-start | bytes 1572872 | tf_op jit(solution)/shard_map/ppermute | solution.py:364
  86.7 59.1 %all-to-all-start = ((bf16[64,2,128,128]{3,2,1,0:T(8,128)(2,1)}), bf16[64,2,128,128]{3,2,1,0:T(8,128)(2,1)}, u32[]{:S(2)}, u32[]{:S(2)}) async-start(bf16[64,2,128,128]{3,2,1,0:T(8,128)(2,1)} %bitcast.63), calls=%async_computation | async-start | bytes 8388608 | tf_op jit(solution)/shard_map/all_to_all | solution.py:384
  145.8 64.2 %all-to-all-start.1 = ((bf16[64,2,128,128]{3,2,1,0:T(8,128)(2,1)}), bf16[64,2,128,128]{3,2,1,0:T(8,128)(2,1)}, u32[]{:S(2)}, u32[]{:S(2)}) async-start(bf16[64,2,128,128]{3,2,1,0:T(8,128)(2,1)} %bitcast.66), calls=%async_computation.1 | async-start | bytes 8388608 | tf_op jit(solution)/shard_map/all_to_all | solution.py:384
  176.6 54.2 %collective-permute-start.11 = (bf16[8,512,128]{2,1,0:T(8,128)(2,1)S(1)}, bf16[8,512,128]{2,1,0:T(8,128)(2,1)}, u32[]{:S(2)}, u32[]{:S(2)}) collective-permute-start(bf16[8,512,128]{2,1,0:T(8,128)(2,1)S(1)} %dynamic-slice_bitcast_fusion.1), channel_id=1, source_target_pairs={{0,64},{64,0},{1,65},{65,1},{2,66},{66,2},{3,67},{67,3},{4,68},{68... | collective-permute-start | bytes 3145736 | tf_op jit(solution)/shard_map/ppermute | solution.py:435
  210.0 20.8 %copy-start.3 = (bf16[16,512,128]{2,1,0:T(8,128)(2,1)S(1)}, bf16[16,512,128]{2,1,0:T(8,128)(2,1)}, u32[]{:S(2)}) copy-start(bf16[16,512,128]{2,1,0:T(8,128)(2,1)} %u_last.1._) | copy-start | bytes 6291460
  233.2 17.2 %copy-start = (bf16[8,512,128]{2,1,0:T(8,128)(2,1)S(1)}, bf16[8,512,128]{2,1,0:T(8,128)(2,1)}, u32[]{:S(2)}) copy-start(bf16[8,512,128]{2,1,0:T(8,128)(2,1)} %fusion.refs_1_) | copy-start | bytes 3145732
  233.2 44.4 %all-to-all-start.2 = ((bf16[16,8,64,128]{3,2,1,0:T(8,128)(2,1)}), bf16[16,8,64,128]{3,2,1,0:T(8,128)(2,1)S(1)}, u32[]{:S(2)}, u32[]{:S(2)}) async-start(bf16[16,8,64,128]{3,2,1,0:T(8,128)(2,1)} %gate.5), calls=%async_computation.2 | async-start | bytes 4194304 | tf_op jit(solution)/shard_map/all_to_all | solution.py:384
  251.2 4.5 %collective-permute-start.12 = (bf16[512,128]{1,0:T(8,128)(2,1)S(1)}, bf16[512,128]{1,0:T(8,128)(2,1)S(1)}, u32[]{:S(2)}, u32[]{:S(2)}) collective-permute-start(bf16[512,128]{1,0:T(8,128)(2,1)S(1)} %get-tuple-element.35), channel_id=1, source_target_pairs={{0,1},{1,0},{2,3},{3,2},{4,5},{5,4},{6,7},{7,6},{8,9},{9,8},{10,11... | collective-permute-start | bytes 393224 | tf_op jit(solution)/shard_map/ppermute | solution.py:364
  251.2 7.5 %collective-permute-start.13 = (bf16[512,128]{1,0:T(8,128)(2,1)S(1)}, bf16[512,128]{1,0:T(8,128)(2,1)S(1)}, u32[]{:S(2)}, u32[]{:S(2)}) collective-permute-start(bf16[512,128]{1,0:T(8,128)(2,1)S(1)} %get-tuple-element.34), channel_id=1, source_target_pairs={{0,2},{1,3},{2,4},{3,5},{4,6},{5,7},{6,0},{7,1},{8,10},{9,11},{10,... | collective-permute-start | bytes 393224 | tf_op jit(solution)/shard_map/ppermute | solution.py:364
  251.2 15.2 %collective-permute-start.14 = (bf16[512,128]{1,0:T(8,128)(2,1)}, bf16[512,128]{1,0:T(8,128)(2,1)S(1)}, u32[]{:S(2)}, u32[]{:S(2)}) collective-permute-start(bf16[512,128]{1,0:T(8,128)(2,1)} %get-tuple-element.33), channel_id=1, source_target_pairs={{0,3},{1,2},{2,5},{3,4},{4,7},{5,6},{6,1},{7,0},{8,11},{9,10},{10,... | collective-permute-start | bytes 393224 | tf_op jit(solution)/shard_map/ppermute | solution.py:364
  251.3 15.1 %collective-permute-start.15 = (bf16[512,128]{1,0:T(8,128)(2,1)}, bf16[512,128]{1,0:T(8,128)(2,1)S(1)}, u32[]{:S(2)}, u32[]{:S(2)}) collective-permute-start(bf16[512,128]{1,0:T(8,128)(2,1)} %get-tuple-element.32), channel_id=1, source_target_pairs={{0,4},{1,5},{2,6},{3,7},{4,0},{5,1},{6,2},{7,3},{8,12},{9,13},{10,... | collective-permute-start | bytes 393224 | tf_op jit(solution)/shard_map/ppermute | solution.py:364
  255.7 10.6 %collective-permute-start.16 = (bf16[512,128]{1,0:T(8,128)(2,1)S(1)}, bf16[512,128]{1,0:T(8,128)(2,1)S(1)}, u32[]{:S(2)}, u32[]{:S(2)}) collective-permute-start(bf16[512,128]{1,0:T(8,128)(2,1)S(1)} %get-tuple-element.31), channel_id=1, source_target_pairs={{0,5},{1,4},{2,7},{3,6},{4,1},{5,0},{6,3},{7,2},{8,13},{9,12},{10,... | collective-permute-start | bytes 393224 | tf_op jit(solution)/shard_map/ppermute | solution.py:364
  255.8 21.9 %copy-start.12 = (bf16[512,128]{1,0:T(8,128)(2,1)}, bf16[512,128]{1,0:T(8,128)(2,1)S(1)}, u32[]{:S(2)}) copy-start(bf16[512,128]{1,0:T(8,128)(2,1)S(1)} %collective-permute-done.12.refs_1_) | copy-start | bytes 393220
  255.8 10.6 %collective-permute-start.17 = (bf16[512,128]{1,0:T(8,128)(2,1)S(1)}, bf16[512,128]{1,0:T(8,128)(2,1)S(1)}, u32[]{:S(2)}, u32[]{:S(2)}) collective-permute-start(bf16[512,128]{1,0:T(8,128)(2,1)S(1)} %get-tuple-element.30), channel_id=1, source_target_pairs={{0,6},{1,7},{2,0},{3,1},{4,2},{5,3},{6,4},{7,5},{8,14},{9,15},{10,... | collective-permute-start | bytes 393224 | tf_op jit(solution)/shard_map/ppermute | solution.py:364
  258.7 18.9 %copy-start.13 = (bf16[512,128]{1,0:T(8,128)(2,1)}, bf16[512,128]{1,0:T(8,128)(2,1)S(1)}, u32[]{:S(2)}) copy-start(bf16[512,128]{1,0:T(8,128)(2,1)S(1)} %collective-permute-done.13.refs_2_) | copy-start | bytes 393220
  258.7 8.0 %collective-permute-start.18 = (bf16[512,128]{1,0:T(8,128)(2,1)S(1)}, bf16[512,128]{1,0:T(8,128)(2,1)S(1)}, u32[]{:S(2)}, u32[]{:S(2)}) collective-permute-start(bf16[512,128]{1,0:T(8,128)(2,1)S(1)} %get-tuple-element.29), channel_id=1, source_target_pairs={{0,7},{1,6},{2,1},{3,0},{4,3},{5,2},{6,5},{7,4},{8,15},{9,14},{10,... | collective-permute-start | bytes 393224 | tf_op jit(solution)/shard_map/ppermute | solution.py:364
  266.4 11.3 %copy-start.14 = (bf16[512,128]{1,0:T(8,128)(2,1)}, bf16[512,128]{1,0:T(8,128)(2,1)S(1)}, u32[]{:S(2)}) copy-start(bf16[512,128]{1,0:T(8,128)(2,1)S(1)} %collective-permute-done.14.refs_3_) | copy-start | bytes 393220
  266.4 11.3 %copy-start.15 = (bf16[512,128]{1,0:T(8,128)(2,1)}, bf16[512,128]{1,0:T(8,128)(2,1)S(1)}, u32[]{:S(2)}) copy-start(bf16[512,128]{1,0:T(8,128)(2,1)S(1)} %collective-permute-done.15.refs_4_) | copy-start | bytes 393220
  266.4 11.3 %copy-start.16 = (bf16[512,128]{1,0:T(8,128)(2,1)}, bf16[512,128]{1,0:T(8,128)(2,1)S(1)}, u32[]{:S(2)}) copy-start(bf16[512,128]{1,0:T(8,128)(2,1)S(1)} %collective-permute-done.16.refs_5_) | copy-start | bytes 393220
  266.4 11.3 %copy-start.17 = (bf16[512,128]{1,0:T(8,128)(2,1)}, bf16[512,128]{1,0:T(8,128)(2,1)S(1)}, u32[]{:S(2)}) copy-start(bf16[512,128]{1,0:T(8,128)(2,1)S(1)} %collective-permute-done.17.refs_6_) | copy-start | bytes 393220
  (10 other events, 26.3 us)

commit v5 on v4

--- a/solution.py
+++ b/solution.py
@@ -433,8 +433,8 @@
     keep = lax.dynamic_index_in_dim(one, lay, 0, keepdims=False)
     send = lax.dynamic_index_in_dim(one, 1 - lay, 0, keepdims=False)
     send = lax.ppermute(send, "layer", [(0, 1), (1, 0)])
+    two = gate(two.reshape(LAYERS_AXIS * GROUP, GROUP, CELLS, LANES), send)
     one = (keep.astype(jnp.float32) + send.astype(jnp.float32)).astype(jnp.bfloat16)
-    two = gate(two.reshape(LAYERS_AXIS * GROUP, GROUP, CELLS, LANES), one)
     two = swap(two, ("layer", "row")).reshape(LAYERS_AXIS, GROUP, GROUP, CELLS, LANES)
     one = [lax.dynamic_index_in_dim(one, across_col(col, n), 0, keepdims=False) for n in range(GROUP)]
     one = around(one, "col", across_col, (2, 3, 6, 7, 4, 5, 1))

time: 286 us -> 285 us (level)
  transfers between devices with their start and end apart: 22 -> 22, of which waited for: 12 -> 12; matrix products, arithmetic and copies ran while one was open for 5% -> 6% of each run, Pallas kernels for 25% -> 25%
where the time goes in v5:
time: 285 us; the launch traced here: 283 us
  waiting for transfers between devices  106 us (37%)
  Pallas kernels  77 us (27%)
  starting transfers between devices  72.9 us (26%)
  local copies, waits for them, and re-layouts  20.3 us (7%)
  other arithmetic  6.89 us (2%)
    all_to_all x3, waiting for transfers between devices, swap(): return lax.all_to_all(blocks, axes, split_axis=0, concat_axis=0, tiled=True)  75.4 us
    all_to_all x3, starting transfers between devices, swap(): return lax.all_to_all(blocks, axes, split_axis=0, concat_axis=0, tiled=True)  38 us
    pallas_call x2, Pallas kernels, along_v(): pl.pallas_call(functools.partial(along_v_kernel, early), out_shape=jax.Sh...  36.5 us
    pallas_call x2, Pallas kernels, along_u(): pl.pallas_call(functools.partial(along_u_kernel, early), grid=(tiles + CE...  29.5 us
    ppermute x14, starting transfers between devices, around(): lax.ppermute(blocks[n], axis, [(c, across(c, n)) for c in range(GROUP)])  25.2 us
    ppermute x14, waiting for transfers between devices, around(): lax.ppermute(blocks[n], axis, [(c, across(c, n)) for c in range(GROUP)])  18.4 us
    ppermute x3, waiting for transfers between devices, along_y(): lax.ppermute(block, 'col', [(c, (c + 2 * n) % GROUP) for c in range(GROUP)])  7.83 us
    pallas_call x1, Pallas kernels, arrange(): pl.pallas_call(arrange_kernel, out_shape=jax.ShapeDtypeStruct((8 * CELLS,...  6.07 us
  transfers between devices with their start and end apart: 22, of which 12 were waited for; matrix products, arithmetic and copies ran while one was open for 6% of the time, Pallas kernels for 25%

profile of v5, /device:TPU:0, one launch (start us, length us, event | category | flops | bytes accessed | tf_op | source)
XLA Modules:
  0.0 283.2 jit_solution(16084849400448397090)
XLA Ops:
  0.0 1.7 dynamic-slice_bitcast_fusion
  1.9 2.5 dynamic-slice_bitcast_fusion.2
  6.1 2.7 constant_dynamic-slice_fusion
  13.3 4.9 %columns.1 = (bf16[1024,256]{1,0:T(8,128)(2,1)}, bf16[1024,256]{1,0:T(8,128)(2,1)}, bf16[1024,256]{1,0:T(8,128)(2,1)}, bf16[1024,256]{1,0:T(8,128)(2,1)}, bf16[1...) custom-call(s32[1]{0:T(128)} %bitcast.10._.w_ref, ...), custom_call_target="tpu_custom_call" | custom-call | tf_op jit(solution)/shard_map/columns/pallas_call | solution.py:347
  18.2 2.1 collective-permute-start.3
  20.3 2.2 collective-permute-start.4
  22.5 3.0 %collective-permute-start.5 = (bf16[1024,256]{1,0:T(8,128)(2,1)}, bf16[1024,256]{1,0:T(8,128)(2,1)S(1)}, u32[]{:S(2)}, u32[]{:S(2)}) collective-permute-start(bf16[1024,256]{1,0:T(8,128)(2,1)} %get-tuple-element.15), channel_id=1, source_target_pairs={{0,32},{8,40},{16,48},{24,56},{32,0},{40,8},{48,16},{56,24},{1,33}... | collective-permute-start | bytes 1572872 | tf_op jit(solution)/shard_map/ppermute | solution.py:364
  25.5 2.1 pad_maximum_fusion.2.refs_0_
  27.7 6.7 %collective-permute-done.3.refs_3_.refs_1_ = bf16[1024,256]{1,0:T(8,128)(2,1)S(1)} collective-permute-done((bf16[1024,256]{1,0:T(8,128)(2,1)}, bf16[1024,256]{1,0:T(8,128)(2,1)S(1)}, u32[]{:S(2)}, u32[]{:S(2)}) %collective-permute-start.3) | collective-permute-done | bytes 524320 | tf_op jit(solution)/shard_map/ppermute | solution.py:364
  34.4 3.0 %collective-permute-done.5.refs_5_.refs_4_ = bf16[1024,256]{1,0:T(8,128)(2,1)S(1)} collective-permute-done((bf16[1024,256]{1,0:T(8,128)(2,1)}, bf16[1024,256]{1,0:T(8,128)(2,1)S(1)}, u32[]{:S(2)}, u32[]{:S(2)}) %collective-permute-start.5) | collective-permute-done | bytes 524320 | tf_op jit(solution)/shard_map/ppermute | solution.py:364
  38.2 2.3 collective-permute-start.6
  42.6 5.7 %collective-permute-start.10 = (bf16[1024,256]{1,0:T(8,128)(2,1)}, bf16[1024,256]{1,0:T(8,128)(2,1)S(1)}, u32[]{:S(2)}, u32[]{:S(2)}) collective-permute-start(bf16[1024,256]{1,0:T(8,128)(2,1)} %get-tuple-element.19), channel_id=1, source_target_pairs={{0,56},{8,32},{16,40},{24,48},{32,24},{40,0},{48,8},{56,16},{1,57}... | collective-permute-start | bytes 1572872 | tf_op jit(solution)/shard_map/ppermute | solution.py:364
  49.5 4.1 %collective-permute-start.9 = (bf16[1024,256]{1,0:T(8,128)(2,1)}, bf16[1024,256]{1,0:T(8,128)(2,1)S(1)}, u32[]{:S(2)}, u32[]{:S(2)}) collective-permute-start(bf16[1024,256]{1,0:T(8,128)(2,1)} %get-tuple-element.18), channel_id=1, source_target_pairs={{0,48},{8,56},{16,32},{24,40},{32,16},{40,24},{48,0},{56,8},{1,49}... | collective-permute-start | bytes 1572872 | tf_op jit(solution)/shard_map/ppermute | solution.py:364
  53.6 2.1 pad_maximum_fusion.refs_0_.refs_1_
  55.7 7.8 %collective-permute-done.6.refs_4_.refs_5_ = bf16[2,128,2048]{2,1,0:T(8,128)(2,1)} collective-permute-done((bf16[2,128,2048]{2,1,0:T(8,128)(2,1)}, bf16[2,128,2048]{2,1,0:T(8,128)(2,1)}, u32[]{:S(2)}, u32[]{:S(2)}) %collective-permute-start.6) | collective-permute-done | bytes 1048608 | tf_op jit(solution)/shard_map/ppermute | solution.py:413
  63.5 18.2 %v_first.1.refs_0_ = bf16[8,8,2,128,128]{4,3,2,1,0:T(8,128)(2,1)} custom-call(s32[1]{0:T(128)} %bitcast.2.core_ref, s32[1]{0:T(128)} %bitcast.3.place_ref, s32[1]{0:T(128)} %get-tuple-element.38.w_ref._, s32[1]{0:T(128)} %get-tuple-element.38.w_ref._, bf16[2,128,2048]{2,1,0:T(8,128)(2,1)} %pad_maximum_fusion.refs_0_.refs_1_, ...), custom_call_target="tpu_custom_call" | custom-call | flops 8589934592 | bytes 16777216 | tf_op jit(solution)/shard_map/v_first/pallas_call | solution.py:173
  81.8 3.1 %collective-permute-done.7.refs_2_ = bf16[1024,256]{1,0:T(8,128)(2,1)S(1)} collective-permute-done((bf16[1024,256]{1,0:T(8,128)(2,1)}, bf16[1024,256]{1,0:T(8,128)(2,1)S(1)}, u32[]{:S(2)}, u32[]{:S(2)}) %collective-permute-start.7) | collective-permute-done | bytes 524320 | tf_op jit(solution)/shard_map/ppermute | solution.py:364
  86.7 7.7 %all-to-all-start = ((bf16[64,2,128,128]{3,2,1,0:T(8,128)(2,1)}), bf16[64,2,128,128]{3,2,1,0:T(8,128)(2,1)}, u32[]{:S(2)}, u32[]{:S(2)}) async-start(bf16[64,2,128,128]{3,2,1,0:T(8,128)(2,1)} %bitcast.63), calls=%async_computation | async-start | bytes 8388608 | tf_op jit(solution)/shard_map/all_to_all | solution.py:384
  96.0 13.5 %u_first.1 = bf16[8,8,2,2,64,128]{5,4,3,2,1,0:T(8,128)(2,1)} custom-call(s32[1]{0:T(128)} %bitcast.1.place_ref, s32[1]{0:T(128)} %bitcast.10._.w_ref, bf16[8,8,2,128,128]{4,3,2,1,0:T(8,128)(2,1)} %gate.4._, bf16[8,128,256]{2,1,0:T(8,128)(2,1)} %bitcast.78, bf16[8,128,256]{2,1,0:T(8,128)(2,1)} %bitcast.70, bf16[8,128,256]{2,1,0:T(8,128)(2,1)} %bitcast.73, ...), custom_call_target="tpu_custom_call" | custom-call | flops 8589934592 | bytes 8388608 | tf_op jit(solution)/shard_map/u_first/pallas_call | solution.py:273
  109.5 36.1 %all-to-all-done.refs_0_ = bf16[64,2,128,128]{3,2,1,0:T(8,128)(2,1)} async-done(((bf16[64,2,128,128]{3,2,1,0:T(8,128)(2,1)}), bf16[64,2,128,128]{3,2,1,0:T(8,128)(2,1)}, u32[]{:S(2)}, u32[]{:S(2)}) %all-to-all-start) | async-done | bytes 4194336 | tf_op jit(solution)/shard_map/all_to_all | solution.py:384
  145.6 13.2 %all-to-all-start.1 = ((bf16[64,2,128,128]{3,2,1,0:T(8,128)(2,1)}), bf16[64,2,128,128]{3,2,1,0:T(8,128)(2,1)}, u32[]{:S(2)}, u32[]{:S(2)}) async-start(bf16[64,2,128,128]{3,2,1,0:T(8,128)(2,1)} %bitcast.66), calls=%async_computation.1 | async-start | bytes 8388608 | tf_op jit(solution)/shard_map/all_to_all | solution.py:384
  158.8 16.0 %u_last.1._ = bf16[16,512,128]{2,1,0:T(8,128)(2,1)} custom-call(s32[1]{0:T(128)} %bitcast.1.place_ref, s32[1]{0:T(128)} %get-tuple-element.38.w_ref._, s32[1]{0:T(128)} %get-tuple-element.38.w_ref._, bf16[64,2,128,128]{3,2,1,0:T(8,128)(2,1)} %all-to-all-done.refs_0_, f32[128,64]{1,0:T(8,128)} %constant.328.refs_1_, f32[128,64]{1,0:T(8,128)} %constant.330.refs_2_, ...), custom_call_target="tpu_custom_call" | custom-call | flops 8589934592 | bytes 8388608 | tf_op jit(solution)/shard_map/u_last/pallas_call | solution.py:273
  176.1 3.9 %collective-permute-start.11 = (bf16[8,512,128]{2,1,0:T(8,128)(2,1)S(1)}, bf16[8,512,128]{2,1,0:T(8,128)(2,1)S(1)}, u32[]{:S(2)}, u32[]{:S(2)}) collective-permute-start(bf16[8,512,128]{2,1,0:T(8,128)(2,1)S(1)} %dynamic-slice_bitcast_fusion.1), channel_id=1, source_target_pairs={{0,64},{64,0},{1,65},{65,1},{2,66},{66,2},{3,67},{67,3},{4,68},{68... | collective-permute-start | bytes 3145736 | tf_op jit(solution)/shard_map/ppermute | solution.py:435
  180.0 29.7 %all-to-all-done.1 = bf16[64,2,128,128]{3,2,1,0:T(8,128)(2,1)} async-done(((bf16[64,2,128,128]{3,2,1,0:T(8,128)(2,1)}), bf16[64,2,128,128]{3,2,1,0:T(8,128)(2,1)}, u32[]{:S(2)}, u32[]{:S(2)}) %all-to-all-start.1) | async-done | bytes 4194336 | tf_op jit(solution)/shard_map/all_to_all | solution.py:384
  209.8 18.3 %v_last.1 = bf16[2,8,8,64,128]{4,3,2,1,0:T(8,128)(2,1)} custom-call(s32[1]{0:T(128)} %bitcast.2.core_ref, s32[1]{0:T(128)} %bitcast.3.place_ref, s32[1]{0:T(128)} %get-tuple-element.37.w_ref, bf16[16,512,128]{2,1,0:T(8,128)(2,1)} %u_last.1._, bf16[8,8,2,128,128]{4,3,2,1,0:T(8,128)(2,1)} %bitcast.36.refs_0_, f32[8,1024]{1,0:T(8,128)} %constant.332.refs_1_, ...), custom_call_target="tpu_custom_call" | custom-call | flops 8589934592 | bytes 16777216 | tf_op jit(solution)/shard_map/v_last/pallas_call | solution.py:173
  228.1 2.3 collective-permute-done.11.refs_1_
  231.4 17.1 %all-to-all-start.2 = ((bf16[16,8,64,128]{3,2,1,0:T(8,128)(2,1)}), bf16[16,8,64,128]{3,2,1,0:T(8,128)(2,1)S(1)}, u32[]{:S(2)}, u32[]{:S(2)}) async-start(bf16[16,8,64,128]{3,2,1,0:T(8,128)(2,1)} %gate.5), calls=%async_computation.2 | async-start | bytes 4194304 | tf_op jit(solution)/shard_map/all_to_all | solution.py:384
  250.9 4.5 %collective-permute-start.15 = (bf16[512,128]{1,0:T(8,128)(2,1)S(1)}, bf16[512,128]{1,0:T(8,128)(2,1)S(1)}, u32[]{:S(2)}, u32[]{:S(2)}) collective-permute-start(bf16[512,128]{1,0:T(8,128)(2,1)S(1)} %get-tuple-element.32), channel_id=1, source_target_pairs={{0,4},{1,5},{2,6},{3,7},{4,0},{5,1},{6,2},{7,3},{8,12},{9,13},{10,... | collective-permute-start | bytes 393224 | tf_op jit(solution)/shard_map/ppermute | solution.py:364
  255.4 1.8 collective-permute-start.17
  261.9 4.1 %collective-permute-done.14.refs_3_ = bf16[512,128]{1,0:T(8,128)(2,1)S(1)} collective-permute-done((bf16[512,128]{1,0:T(8,128)(2,1)S(1)}, bf16[512,128]{1,0:T(8,128)(2,1)S(1)}, u32[]{:S(2)}, u32[]{:S(2)}) %collective-permute-start.14) | collective-permute-done | bytes 131104 | tf_op jit(solution)/shard_map/ppermute | solution.py:364
  266.2 9.6 %all-to-all-done.2 = bf16[16,8,64,128]{3,2,1,0:T(8,128)(2,1)S(1)} async-done(((bf16[16,8,64,128]{3,2,1,0:T(8,128)(2,1)}), bf16[16,8,64,128]{3,2,1,0:T(8,128)(2,1)S(1)}, u32[]{:S(2)}, u32[]{:S(2)}) %all-to-all-start.2) | async-done | bytes 2097184 | tf_op jit(solution)/shard_map/all_to_all | solution.py:384
  277.1 6.1 %arrange.1 = f32[512,1024]{1,0:T(8,128)} custom-call(s32[1]{0:T(128)} %bitcast.place_ref, bf16[512,128]{1,0:T(8,128)(2,1)} %get-tuple-element.36.refs_0_, bf16[512,128]{1,0:T(8,128)(2,1)} %copy-done.12, bf16[512,128]{1,0:T(8,128)(2,1)} %copy-done.13, bf16[512,128]{1,0:T(8,128)(2,1)} %copy-done.14, bf16[512,128]{1,0:T(8,128)(2,1)} %copy-done.15, ...), custom_call_target="tpu_custom_call" | custom-call | tf_op jit(solution)/shard_map/arrange/pallas_call | solution.py:320
  (75 shorter events, 24.3 us)
Async XLA Ops:
  1.7 4.4 %collective-permute-start = (bf16[4,128,2048]{2,1,0:T(8,128)(2,1)S(1)}, bf16[4,128,2048]{2,1,0:T(8,128)(2,1)}, u32[]{:S(2)}, u32[]{:S(2)}) collective-permute-start(bf16[4,128,2048]{2,1,0:T(8,128)(2,1)S(1)} %dynamic-slice_bitcast_fusion), channel_id=1, source_target_pairs={{0,1},{1,0},{2,3},{3,2},{4,5},{5,4},{6,7},{7,6},{8,9},{9,8},{10,11... | collective-permute-start | bytes 6291464 | tf_op jit(solution)/shard_map/ppermute | solution.py:405
  9.9 27.5 %collective-permute-start.2 = (bf16[2,128,2048]{2,1,0:T(8,128)(2,1)}, bf16[2,128,2048]{2,1,0:T(8,128)(2,1)}, u32[]{:S(2)}, u32[]{:S(2)}) collective-permute-start(bf16[2,128,2048]{2,1,0:T(8,128)(2,1)} %pad_maximum_fusion.3), channel_id=1, source_target_pairs={{0,2},{1,3},{2,4},{3,5},{4,6},{5,7},{6,0},{7,1},{8,10},{9,11},{10,... | collective-permute-start | bytes 3145736 | tf_op jit(solution)/shard_map/ppermute | solution.py:413
  11.7 25.8 %collective-permute-start.1 = (bf16[2,128,2048]{2,1,0:T(8,128)(2,1)S(1)}, bf16[2,128,2048]{2,1,0:T(8,128)(2,1)}, u32[]{:S(2)}, u32[]{:S(2)}) collective-permute-start(bf16[2,128,2048]{2,1,0:T(8,128)(2,1)S(1)} %pad_maximum_fusion.1.__), channel_id=1, source_target_pairs={{0,6},{1,7},{2,0},{3,1},{4,2},{5,3},{6,4},{7,5},{8,14},{9,15},{10,... | collective-permute-start | bytes 3145736 | tf_op jit(solution)/shard_map/ppermute | solution.py:413
  13.3 12.2 %copy-start.7 = (bf16[1,128,2048]{2,1,0:T(8,128)(2,1)S(1)}, bf16[1,128,2048]{2,1,0:T(8,128)(2,1)}, u32[]{:S(2)}) copy-start(bf16[1,128,2048]{2,1,0:T(8,128)(2,1)} %get-tuple-element.22) | copy-start | bytes 1572868
  18.2 16.1 %collective-permute-start.3 = (bf16[1024,256]{1,0:T(8,128)(2,1)}, bf16[1024,256]{1,0:T(8,128)(2,1)S(1)}, u32[]{:S(2)}, u32[]{:S(2)}) collective-permute-start(bf16[1024,256]{1,0:T(8,128)(2,1)} %get-tuple-element.13), channel_id=1, source_target_pairs={{0,8},{8,16},{16,24},{24,0},{32,40},{40,48},{48,56},{56,32},{1,9},... | collective-permute-start | bytes 1572872 | tf_op jit(solution)/shard_map/ppermute | solution.py:364
  20.3 14.1 %collective-permute-start.4 = (bf16[1024,256]{1,0:T(8,128)(2,1)}, bf16[1024,256]{1,0:T(8,128)(2,1)S(1)}, u32[]{:S(2)}, u32[]{:S(2)}) collective-permute-start(bf16[1024,256]{1,0:T(8,128)(2,1)} %get-tuple-element.14), channel_id=1, source_target_pairs={{0,24},{8,0},{16,8},{24,16},{32,56},{40,32},{48,40},{56,48},{1,25}... | collective-permute-start | bytes 1572872 | tf_op jit(solution)/shard_map/ppermute | solution.py:364
  22.5 14.9 %collective-permute-start.5 = (bf16[1024,256]{1,0:T(8,128)(2,1)}, bf16[1024,256]{1,0:T(8,128)(2,1)S(1)}, u32[]{:S(2)}, u32[]{:S(2)}) collective-permute-start(bf16[1024,256]{1,0:T(8,128)(2,1)} %get-tuple-element.15), channel_id=1, source_target_pairs={{0,32},{8,40},{16,48},{24,56},{32,0},{40,8},{48,16},{56,24},{1,33}... | collective-permute-start | bytes 1572872 | tf_op jit(solution)/shard_map/ppermute | solution.py:364
  27.7 12.9 %copy-start.18 = (s32[2]{0:T(128)S(1)}, s32[2]{0:T(128)}, u32[]{:S(2)}) copy-start(s32[2]{0:T(128)} %param.15) | copy-start | bytes 28
  38.2 25.3 %collective-permute-start.6 = (bf16[2,128,2048]{2,1,0:T(8,128)(2,1)}, bf16[2,128,2048]{2,1,0:T(8,128)(2,1)}, u32[]{:S(2)}, u32[]{:S(2)}) collective-permute-start(bf16[2,128,2048]{2,1,0:T(8,128)(2,1)} %gate.3), channel_id=1, source_target_pairs={{0,4},{1,5},{2,6},{3,7},{4,0},{5,1},{6,2},{7,3},{8,12},{9,13},{10,... | collective-permute-start | bytes 3145736 | tf_op jit(solution)/shard_map/ppermute | solution.py:413
  42.6 39.2 %collective-permute-start.10 = (bf16[1024,256]{1,0:T(8,128)(2,1)}, bf16[1024,256]{1,0:T(8,128)(2,1)S(1)}, u32[]{:S(2)}, u32[]{:S(2)}) collective-permute-start(bf16[1024,256]{1,0:T(8,128)(2,1)} %get-tuple-element.19), channel_id=1, source_target_pairs={{0,56},{8,32},{16,40},{24,48},{32,24},{40,0},{48,8},{56,16},{1,57}... | collective-permute-start | bytes 1572872 | tf_op jit(solution)/shard_map/ppermute | solution.py:364
  48.3 36.6 %collective-permute-start.7 = (bf16[1024,256]{1,0:T(8,128)(2,1)}, bf16[1024,256]{1,0:T(8,128)(2,1)S(1)}, u32[]{:S(2)}, u32[]{:S(2)}) collective-permute-start(bf16[1024,256]{1,0:T(8,128)(2,1)} %get-tuple-element.16), channel_id=1, source_target_pairs={{0,16},{8,24},{16,0},{24,8},{32,48},{40,56},{48,32},{56,40},{1,17}... | collective-permute-start | bytes 1572872 | tf_op jit(solution)/shard_map/ppermute | solution.py:364
  48.3 36.6 %collective-permute-start.8 = (bf16[1024,256]{1,0:T(8,128)(2,1)}, bf16[1024,256]{1,0:T(8,128)(2,1)S(1)}, u32[]{:S(2)}, u32[]{:S(2)}) collective-permute-start(bf16[1024,256]{1,0:T(8,128)(2,1)} %get-tuple-element.17), channel_id=1, source_target_pairs={{0,40},{8,48},{16,56},{24,32},{32,8},{40,16},{48,24},{56,0},{1,41}... | collective-permute-start | bytes 1572872 | tf_op jit(solution)/shard_map/ppermute | solution.py:364
  49.5 35.4 %collective-permute-start.9 = (bf16[1024,256]{1,0:T(8,128)(2,1)}, bf16[1024,256]{1,0:T(8,128)(2,1)S(1)}, u32[]{:S(2)}, u32[]{:S(2)}) collective-permute-start(bf16[1024,256]{1,0:T(8,128)(2,1)} %get-tuple-element.18), channel_id=1, source_target_pairs={{0,48},{8,56},{16,32},{24,40},{32,16},{40,24},{48,0},{56,8},{1,49}... | collective-permute-start | bytes 1572872 | tf_op jit(solution)/shard_map/ppermute | solution.py:364
  81.8 3.1 %copy-start.8 = (bf16[1024,256]{1,0:T(8,128)(2,1)}, bf16[1024,256]{1,0:T(8,128)(2,1)S(1)}, u32[]{:S(2)}) copy-start(bf16[1024,256]{1,0:T(8,128)(2,1)S(1)} %collective-permute-done.10.refs_7_) | copy-start | bytes 1572868
  86.7 58.9 %all-to-all-start = ((bf16[64,2,128,128]{3,2,1,0:T(8,128)(2,1)}), bf16[64,2,128,128]{3,2,1,0:T(8,128)(2,1)}, u32[]{:S(2)}, u32[]{:S(2)}) async-start(bf16[64,2,128,128]{3,2,1,0:T(8,128)(2,1)} %bitcast.63), calls=%async_computation | async-start | bytes 8388608 | tf_op jit(solution)/shard_map/all_to_all | solution.py:384
  145.6 64.2 %all-to-all-start.1 = ((bf16[64,2,128,128]{3,2,1,0:T(8,128)(2,1)}), bf16[64,2,128,128]{3,2,1,0:T(8,128)(2,1)}, u32[]{:S(2)}, u32[]{:S(2)}) async-start(bf16[64,2,128,128]{3,2,1,0:T(8,128)(2,1)} %bitcast.66), calls=%async_computation.1 | async-start | bytes 8388608 | tf_op jit(solution)/shard_map/all_to_all | solution.py:384
  176.1 54.3 %collective-permute-start.11 = (bf16[8,512,128]{2,1,0:T(8,128)(2,1)S(1)}, bf16[8,512,128]{2,1,0:T(8,128)(2,1)S(1)}, u32[]{:S(2)}, u32[]{:S(2)}) collective-permute-start(bf16[8,512,128]{2,1,0:T(8,128)(2,1)S(1)} %dynamic-slice_bitcast_fusion.1), channel_id=1, source_target_pairs={{0,64},{64,0},{1,65},{65,1},{2,66},{66,2},{3,67},{67,3},{4,68},{68... | collective-permute-start | bytes 3145736 | tf_op jit(solution)/shard_map/ppermute | solution.py:435
  231.4 17.2 %copy-start.3 = (bf16[8,512,128]{2,1,0:T(8,128)(2,1)S(1)}, bf16[8,512,128]{2,1,0:T(8,128)(2,1)}, u32[]{:S(2)}) copy-start(bf16[8,512,128]{2,1,0:T(8,128)(2,1)} %copy-done.2) | copy-start | bytes 3145732
  231.4 44.4 %all-to-all-start.2 = ((bf16[16,8,64,128]{3,2,1,0:T(8,128)(2,1)}), bf16[16,8,64,128]{3,2,1,0:T(8,128)(2,1)S(1)}, u32[]{:S(2)}, u32[]{:S(2)}) async-start(bf16[16,8,64,128]{3,2,1,0:T(8,128)(2,1)} %gate.5), calls=%async_computation.2 | async-start | bytes 4194304 | tf_op jit(solution)/shard_map/all_to_all | solution.py:384
  250.8 4.5 %collective-permute-start.12 = (bf16[512,128]{1,0:T(8,128)(2,1)S(1)}, bf16[512,128]{1,0:T(8,128)(2,1)S(1)}, u32[]{:S(2)}, u32[]{:S(2)}) collective-permute-start(bf16[512,128]{1,0:T(8,128)(2,1)S(1)} %get-tuple-element.35), channel_id=1, source_target_pairs={{0,1},{1,0},{2,3},{3,2},{4,5},{5,4},{6,7},{7,6},{8,9},{9,8},{10,11... | collective-permute-start | bytes 393224 | tf_op jit(solution)/shard_map/ppermute | solution.py:364
  250.9 7.5 %collective-permute-start.13 = (bf16[512,128]{1,0:T(8,128)(2,1)S(1)}, bf16[512,128]{1,0:T(8,128)(2,1)S(1)}, u32[]{:S(2)}, u32[]{:S(2)}) collective-permute-start(bf16[512,128]{1,0:T(8,128)(2,1)S(1)} %get-tuple-element.34), channel_id=1, source_target_pairs={{0,2},{1,3},{2,4},{3,5},{4,6},{5,7},{6,0},{7,1},{8,10},{9,11},{10,... | collective-permute-start | bytes 393224 | tf_op jit(solution)/shard_map/ppermute | solution.py:364
  250.9 15.2 %collective-permute-start.14 = (bf16[512,128]{1,0:T(8,128)(2,1)S(1)}, bf16[512,128]{1,0:T(8,128)(2,1)S(1)}, u32[]{:S(2)}, u32[]{:S(2)}) collective-permute-start(bf16[512,128]{1,0:T(8,128)(2,1)S(1)} %get-tuple-element.33), channel_id=1, source_target_pairs={{0,3},{1,2},{2,5},{3,4},{4,7},{5,6},{6,1},{7,0},{8,11},{9,10},{10,... | collective-permute-start | bytes 393224 | tf_op jit(solution)/shard_map/ppermute | solution.py:364
  250.9 15.2 %collective-permute-start.15 = (bf16[512,128]{1,0:T(8,128)(2,1)S(1)}, bf16[512,128]{1,0:T(8,128)(2,1)S(1)}, u32[]{:S(2)}, u32[]{:S(2)}) collective-permute-start(bf16[512,128]{1,0:T(8,128)(2,1)S(1)} %get-tuple-element.32), channel_id=1, source_target_pairs={{0,4},{1,5},{2,6},{3,7},{4,0},{5,1},{6,2},{7,3},{8,12},{9,13},{10,... | collective-permute-start | bytes 393224 | tf_op jit(solution)/shard_map/ppermute | solution.py:364
  255.4 10.6 %collective-permute-start.16 = (bf16[512,128]{1,0:T(8,128)(2,1)S(1)}, bf16[512,128]{1,0:T(8,128)(2,1)S(1)}, u32[]{:S(2)}, u32[]{:S(2)}) collective-permute-start(bf16[512,128]{1,0:T(8,128)(2,1)S(1)} %get-tuple-element.31), channel_id=1, source_target_pairs={{0,5},{1,4},{2,7},{3,6},{4,1},{5,0},{6,3},{7,2},{8,13},{9,12},{10,... | collective-permute-start | bytes 393224 | tf_op jit(solution)/shard_map/ppermute | solution.py:364
  255.4 20.4 %copy-start.12 = (bf16[512,128]{1,0:T(8,128)(2,1)}, bf16[512,128]{1,0:T(8,128)(2,1)S(1)}, u32[]{:S(2)}) copy-start(bf16[512,128]{1,0:T(8,128)(2,1)S(1)} %collective-permute-done.12.refs_1_) | copy-start | bytes 393220
  255.4 10.6 %collective-permute-start.17 = (bf16[512,128]{1,0:T(8,128)(2,1)S(1)}, bf16[512,128]{1,0:T(8,128)(2,1)S(1)}, u32[]{:S(2)}, u32[]{:S(2)}) collective-permute-start(bf16[512,128]{1,0:T(8,128)(2,1)S(1)} %get-tuple-element.30), channel_id=1, source_target_pairs={{0,6},{1,7},{2,0},{3,1},{4,2},{5,3},{6,4},{7,5},{8,14},{9,15},{10,... | collective-permute-start | bytes 393224 | tf_op jit(solution)/shard_map/ppermute | solution.py:364
  258.4 17.4 %copy-start.13 = (bf16[512,128]{1,0:T(8,128)(2,1)}, bf16[512,128]{1,0:T(8,128)(2,1)S(1)}, u32[]{:S(2)}) copy-start(bf16[512,128]{1,0:T(8,128)(2,1)S(1)} %collective-permute-done.13.refs_2_) | copy-start | bytes 393220
  258.4 7.9 %collective-permute-start.18 = (bf16[512,128]{1,0:T(8,128)(2,1)S(1)}, bf16[512,128]{1,0:T(8,128)(2,1)}, u32[]{:S(2)}, u32[]{:S(2)}) collective-permute-start(bf16[512,128]{1,0:T(8,128)(2,1)S(1)} %get-tuple-element.29), channel_id=1, source_target_pairs={{0,7},{1,6},{2,1},{3,0},{4,3},{5,2},{6,5},{7,4},{8,15},{9,14},{10,... | collective-permute-start | bytes 393224 | tf_op jit(solution)/shard_map/ppermute | solution.py:364
  266.0 9.8 %copy-start.14 = (bf16[512,128]{1,0:T(8,128)(2,1)}, bf16[512,128]{1,0:T(8,128)(2,1)S(1)}, u32[]{:S(2)}) copy-start(bf16[512,128]{1,0:T(8,128)(2,1)S(1)} %collective-permute-done.14.refs_3_) | copy-start | bytes 393220
  266.0 9.8 %copy-start.15 = (bf16[512,128]{1,0:T(8,128)(2,1)}, bf16[512,128]{1,0:T(8,128)(2,1)S(1)}, u32[]{:S(2)}) copy-start(bf16[512,128]{1,0:T(8,128)(2,1)S(1)} %collective-permute-done.15.refs_4_) | copy-start | bytes 393220
  266.0 9.8 %copy-start.16 = (bf16[512,128]{1,0:T(8,128)(2,1)}, bf16[512,128]{1,0:T(8,128)(2,1)S(1)}, u32[]{:S(2)}) copy-start(bf16[512,128]{1,0:T(8,128)(2,1)S(1)} %collective-permute-done.16.refs_5_) | copy-start | bytes 393220
  266.0 9.8 %copy-start.17 = (bf16[512,128]{1,0:T(8,128)(2,1)}, bf16[512,128]{1,0:T(8,128)(2,1)S(1)}, u32[]{:S(2)}) copy-start(bf16[512,128]{1,0:T(8,128)(2,1)S(1)} %collective-permute-done.17.refs_6_) | copy-start | bytes 393220
  (9 other events, 13.5 us)

commit v6 on v5

--- a/solution.py
+++ b/solution.py
@@ -294,38 +294,52 @@
     )(place, w_value, after, *cells, tw_cos, tw_sin, jnp.asarray(short_table()))
 
 
-def arrange_kernel(place_ref, *refs):
-    one, (two_ref, rows_ref, cols_ref, out_ref, held) = refs[:-5], refs[-5:]
-    q = lax.broadcasted_iota(jnp.int32, (LANES, BLOCK), 0)
-    m = lax.broadcasted_iota(jnp.int32, (LANES, BLOCK), 1)
+def arrange_kernel(col_ref, *refs):
+    one, (two_ref, rows_ref, cols_ref, out_ref, picks, held) = refs[:GROUP], refs[GROUP:]
+    places = [lax.rem(col_ref[0] // 2 + 4 - n // 2, 4) * 2 + lax.rem(col_ref[0] + n, 2) for n in range(GROUP)]
+
+    @pl.when(pl.program_id(0) == 0)
+    def _():
+        q = lax.broadcasted_iota(jnp.int32, (LANES, BLOCK), 0)
+        m = lax.broadcasted_iota(jnp.int32, (LANES, BLOCK), 1)
+        for n, j in enumerate(places):
+            picks[n] = jnp.where(m == GROUP * q + j, 1.0, 0.0).astype(jnp.bfloat16)
+
     total = None
-    for shift in range(GROUP):
-        j = lax.rem(place_ref[0] // 2 + 4 - shift // 2, 4) * 2 + lax.rem(place_ref[0] + shift, 2)
-        pick = jnp.where(m == GROUP * q + j, 1.0, 0.0).astype(jnp.bfloat16)
-        other = [two_ref[0, r, j].astype(jnp.float32) + two_ref[1, r, j].astype(jnp.float32) for r in range(GROUP)]
-        cells = (one[shift][...].astype(jnp.float32) + jnp.concatenate(other, axis=0)).astype(jnp.bfloat16)
-        part = jnp.dot(cells, pick, preferred_element_type=jnp.float32)
+    for n, j in enumerate(places):
+        other = [two_ref[0, r, j].astype(jnp.float32) + two_ref[1, r, j].astype(jnp.float32) for r in range(2)]
+        cells = (one[n][...].astype(jnp.float32) + jnp.concatenate(other, axis=0)).astype(jnp.bfloat16)
+        part = jnp.dot(cells, picks[n], preferred_element_type=jnp.float32)
         total = part if total is None else total + part
     total = total * (cols_ref[...] / NPIX)
     for part in range(GROUP):
         lanes = slice(part * LANES, (part + 1) * LANES)
         held[part] = total[:, lanes]
         for g in range(8):
-            rows = slice(g * CELLS, (g + 1) * CELLS)
-            out_ref[rows, lanes] = held[part, pl.ds(g, CELLS, 8), :] * rows_ref[rows, :]
-
-
-def arrange(place, one, two, taper_rows, taper_cols):
-    vmem = pl.BlockSpec(memory_space=pltpu.VMEM)
+            out_ref[g, :, lanes] = held[part, pl.ds(g, 16, 8), :] * rows_ref[g]
+
+
+def arrange(col, one, two, taper_rows, taper_cols):
+    tile = pl.BlockSpec((8, 16, 1), lambda s: (0, s, 0))
     return pl.pallas_call(
         arrange_kernel,
-        out_shape=jax.ShapeDtypeStruct((8 * CELLS, BLOCK), jnp.float32),
-        in_specs=[pl.BlockSpec(memory_space=pltpu.SMEM)] + [vmem] * (len(one) + 3),
-        out_specs=vmem,
-        scratch_shapes=[pltpu.VMEM((GROUP, 8 * CELLS, LANES), jnp.float32)],
+        grid=(CELLS // 16,),
+        out_shape=jax.ShapeDtypeStruct((8, CELLS, BLOCK), jnp.float32),
+        in_specs=[pl.BlockSpec(memory_space=pltpu.SMEM)]
+        + [pl.BlockSpec((LANES, LANES), lambda s: (s, 0))] * GROUP
+        + [
+            pl.BlockSpec((LAYERS_AXIS, 2, GROUP, CELLS, LANES), lambda s: (0, s, 0, 0, 0)),
+            tile,
+            pl.BlockSpec((1, BLOCK), lambda s: (0, 0)),
+        ],
+        out_specs=pl.BlockSpec((8, 16, BLOCK), lambda s: (0, s, 0)),
+        scratch_shapes=[
+            pltpu.VMEM((GROUP, LANES, BLOCK), jnp.bfloat16),
+            pltpu.VMEM((GROUP, LANES, LANES), jnp.float32),
+        ],
         compiler_params=pltpu.CompilerParams(vmem_limit_bytes=VMEM_LIMIT),
         name="arrange",
-    )(place, *one, two, taper_rows, taper_cols)
+    )(col, *one, two, taper_rows.reshape(8, CELLS, 1), taper_cols).reshape(8 * CELLS, BLOCK)
 
 
 def columns_kernel(_, __, *refs):

time: 285 us -> 285 us (level)
  no operation moved by 1% of the time
where the time goes in v6:
time: 285 us; the launch traced here: 283 us
  waiting for transfers between devices  106 us (37%)
  Pallas kernels  77.2 us (27%)
  starting transfers between devices  72.9 us (26%)
  local copies, waits for them, and re-layouts  20.4 us (7%)
  other arithmetic  6.89 us (2%)
    all_to_all x3, waiting for transfers between devices, swap(): return lax.all_to_all(blocks, axes, split_axis=0, concat_axis=0, tiled=True)  75.4 us
    all_to_all x3, starting transfers between devices, swap(): return lax.all_to_all(blocks, axes, split_axis=0, concat_axis=0, tiled=True)  38 us
    pallas_call x2, Pallas kernels, along_v(): pl.pallas_call(functools.partial(along_v_kernel, early), out_shape=jax.Sh...  36.5 us
    pallas_call x2, Pallas kernels, along_u(): pl.pallas_call(functools.partial(along_u_kernel, early), grid=(tiles + CE...  29.5 us
    ppermute x14, starting transfers between devices, around(): lax.ppermute(blocks[n], axis, [(c, across(c, n)) for c in range(GROUP)])  25.2 us
    ppermute x14, waiting for transfers between devices, around(): lax.ppermute(blocks[n], axis, [(c, across(c, n)) for c in range(GROUP)])  18.3 us
    ppermute x3, waiting for transfers between devices, along_y(): lax.ppermute(block, 'col', [(c, (c + 2 * n) % GROUP) for c in range(GROUP)])  7.83 us
    pallas_call x1, Pallas kernels, arrange(): pl.pallas_call(arrange_kernel, grid=(CELLS // 16,), out_shape=jax.ShapeDt...  6.26 us
  transfers between devices with their start and end apart: 22, of which 12 were waited for; matrix products, arithmetic and copies ran while one was open for 6% of the time, Pallas kernels for 25%

profile of v6, /device:TPU:0, one launch (start us, length us, event | category | flops | bytes accessed | tf_op | source)
XLA Modules:
  0.0 283.4 jit_solution(9471547108022775812)
XLA Ops:
  0.0 1.7 dynamic-slice_bitcast_fusion
  1.9 2.5 dynamic-slice_bitcast_fusion.2
  6.1 2.7 constant_dynamic-slice_fusion
  13.3 4.9 %columns.1 = (bf16[1024,256]{1,0:T(8,128)(2,1)}, bf16[1024,256]{1,0:T(8,128)(2,1)}, bf16[1024,256]{1,0:T(8,128)(2,1)}, bf16[1024,256]{1,0:T(8,128)(2,1)}, bf16[1...) custom-call(s32[1]{0:T(128)} %bitcast.10._.w_ref, ...), custom_call_target="tpu_custom_call" | custom-call | tf_op jit(solution)/shard_map/columns/pallas_call | solution.py:361
  18.2 2.1 collective-permute-start.3
  20.3 2.2 collective-permute-start.4
  22.5 3.0 %collective-permute-start.5 = (bf16[1024,256]{1,0:T(8,128)(2,1)}, bf16[1024,256]{1,0:T(8,128)(2,1)S(1)}, u32[]{:S(2)}, u32[]{:S(2)}) collective-permute-start(bf16[1024,256]{1,0:T(8,128)(2,1)} %get-tuple-element.15), channel_id=1, source_target_pairs={{0,32},{8,40},{16,48},{24,56},{32,0},{40,8},{48,16},{56,24},{1,33}... | collective-permute-start | bytes 1572872 | tf_op jit(solution)/shard_map/ppermute | solution.py:378
  25.5 2.1 pad_maximum_fusion.2.refs_0_
  27.7 6.7 %collective-permute-done.3.refs_3_.refs_1_ = bf16[1024,256]{1,0:T(8,128)(2,1)S(1)} collective-permute-done((bf16[1024,256]{1,0:T(8,128)(2,1)}, bf16[1024,256]{1,0:T(8,128)(2,1)S(1)}, u32[]{:S(2)}, u32[]{:S(2)}) %collective-permute-start.3) | collective-permute-done | bytes 524320 | tf_op jit(solution)/shard_map/ppermute | solution.py:378
  34.4 3.0 %collective-permute-done.5.refs_5_.refs_4_ = bf16[1024,256]{1,0:T(8,128)(2,1)S(1)} collective-permute-done((bf16[1024,256]{1,0:T(8,128)(2,1)}, bf16[1024,256]{1,0:T(8,128)(2,1)S(1)}, u32[]{:S(2)}, u32[]{:S(2)}) %collective-permute-start.5) | collective-permute-done | bytes 524320 | tf_op jit(solution)/shard_map/ppermute | solution.py:378
  38.2 2.3 collective-permute-start.6
  42.6 5.7 %collective-permute-start.10 = (bf16[1024,256]{1,0:T(8,128)(2,1)}, bf16[1024,256]{1,0:T(8,128)(2,1)S(1)}, u32[]{:S(2)}, u32[]{:S(2)}) collective-permute-start(bf16[1024,256]{1,0:T(8,128)(2,1)} %get-tuple-element.19), channel_id=1, source_target_pairs={{0,56},{8,32},{16,40},{24,48},{32,24},{40,0},{48,8},{56,16},{1,57}... | collective-permute-start | bytes 1572872 | tf_op jit(solution)/shard_map/ppermute | solution.py:378
  49.5 4.1 %collective-permute-start.9 = (bf16[1024,256]{1,0:T(8,128)(2,1)}, bf16[1024,256]{1,0:T(8,128)(2,1)S(1)}, u32[]{:S(2)}, u32[]{:S(2)}) collective-permute-start(bf16[1024,256]{1,0:T(8,128)(2,1)} %get-tuple-element.18), channel_id=1, source_target_pairs={{0,48},{8,56},{16,32},{24,40},{32,16},{40,24},{48,0},{56,8},{1,49}... | collective-permute-start | bytes 1572872 | tf_op jit(solution)/shard_map/ppermute | solution.py:378
  53.6 2.1 pad_maximum_fusion.refs_0_.refs_1_
  55.7 7.8 %collective-permute-done.6.refs_4_.refs_5_ = bf16[2,128,2048]{2,1,0:T(8,128)(2,1)} collective-permute-done((bf16[2,128,2048]{2,1,0:T(8,128)(2,1)}, bf16[2,128,2048]{2,1,0:T(8,128)(2,1)}, u32[]{:S(2)}, u32[]{:S(2)}) %collective-permute-start.6) | collective-permute-done | bytes 1048608 | tf_op jit(solution)/shard_map/ppermute | solution.py:427
  63.5 18.2 %v_first.1.refs_0_ = bf16[8,8,2,128,128]{4,3,2,1,0:T(8,128)(2,1)} custom-call(s32[1]{0:T(128)} %bitcast.2.core_ref, s32[1]{0:T(128)} %bitcast.3.place_ref, s32[1]{0:T(128)} %get-tuple-element.38.w_ref._, s32[1]{0:T(128)} %get-tuple-element.38.w_ref._, bf16[2,128,2048]{2,1,0:T(8,128)(2,1)} %pad_maximum_fusion.refs_0_.refs_1_, ...), custom_call_target="tpu_custom_call" | custom-call | flops 8589934592 | bytes 16777216 | tf_op jit(solution)/shard_map/v_first/pallas_call | solution.py:173
  81.8 3.1 %collective-permute-done.7.refs_2_ = bf16[1024,256]{1,0:T(8,128)(2,1)S(1)} collective-permute-done((bf16[1024,256]{1,0:T(8,128)(2,1)}, bf16[1024,256]{1,0:T(8,128)(2,1)S(1)}, u32[]{:S(2)}, u32[]{:S(2)}) %collective-permute-start.7) | collective-permute-done | bytes 524320 | tf_op jit(solution)/shard_map/ppermute | solution.py:378
  86.7 7.7 %all-to-all-start = ((bf16[64,2,128,128]{3,2,1,0:T(8,128)(2,1)}), bf16[64,2,128,128]{3,2,1,0:T(8,128)(2,1)}, u32[]{:S(2)}, u32[]{:S(2)}) async-start(bf16[64,2,128,128]{3,2,1,0:T(8,128)(2,1)} %bitcast.63), calls=%async_computation | async-start | bytes 8388608 | tf_op jit(solution)/shard_map/all_to_all | solution.py:398
  96.0 13.5 %u_first.1 = bf16[8,8,2,2,64,128]{5,4,3,2,1,0:T(8,128)(2,1)} custom-call(s32[1]{0:T(128)} %bitcast.1.place_ref, s32[1]{0:T(128)} %bitcast.10._.w_ref, bf16[8,8,2,128,128]{4,3,2,1,0:T(8,128)(2,1)} %gate.4._, bf16[8,128,256]{2,1,0:T(8,128)(2,1)} %bitcast.77, bf16[8,128,256]{2,1,0:T(8,128)(2,1)} %bitcast.70, bf16[8,128,256]{2,1,0:T(8,128)(2,1)} %bitcast.73, ...), custom_call_target="tpu_custom_call" | custom-call | flops 8589934592 | bytes 8388608 | tf_op jit(solution)/shard_map/u_first/pallas_call | solution.py:273
  109.5 36.1 %all-to-all-done.refs_0_ = bf16[64,2,128,128]{3,2,1,0:T(8,128)(2,1)} async-done(((bf16[64,2,128,128]{3,2,1,0:T(8,128)(2,1)}), bf16[64,2,128,128]{3,2,1,0:T(8,128)(2,1)}, u32[]{:S(2)}, u32[]{:S(2)}) %all-to-all-start) | async-done | bytes 4194336 | tf_op jit(solution)/shard_map/all_to_all | solution.py:398
  145.6 13.2 %all-to-all-start.1 = ((bf16[64,2,128,128]{3,2,1,0:T(8,128)(2,1)}), bf16[64,2,128,128]{3,2,1,0:T(8,128)(2,1)}, u32[]{:S(2)}, u32[]{:S(2)}) async-start(bf16[64,2,128,128]{3,2,1,0:T(8,128)(2,1)} %bitcast.66), calls=%async_computation.1 | async-start | bytes 8388608 | tf_op jit(solution)/shard_map/all_to_all | solution.py:398
  158.8 16.0 %u_last.1._ = bf16[16,512,128]{2,1,0:T(8,128)(2,1)} custom-call(s32[1]{0:T(128)} %bitcast.1.place_ref, s32[1]{0:T(128)} %get-tuple-element.38.w_ref._, s32[1]{0:T(128)} %get-tuple-element.38.w_ref._, bf16[64,2,128,128]{3,2,1,0:T(8,128)(2,1)} %all-to-all-done.refs_0_, f32[128,64]{1,0:T(8,128)} %constant.328.refs_1_, f32[128,64]{1,0:T(8,128)} %constant.330.refs_2_, ...), custom_call_target="tpu_custom_call" | custom-call | flops 8589934592 | bytes 8388608 | tf_op jit(solution)/shard_map/u_last/pallas_call | solution.py:273
  176.1 3.9 %collective-permute-start.11 = (bf16[8,512,128]{2,1,0:T(8,128)(2,1)S(1)}, bf16[8,512,128]{2,1,0:T(8,128)(2,1)S(1)}, u32[]{:S(2)}, u32[]{:S(2)}) collective-permute-start(bf16[8,512,128]{2,1,0:T(8,128)(2,1)S(1)} %dynamic-slice_bitcast_fusion.1), channel_id=1, source_target_pairs={{0,64},{64,0},{1,65},{65,1},{2,66},{66,2},{3,67},{67,3},{4,68},{68... | collective-permute-start | bytes 3145736 | tf_op jit(solution)/shard_map/ppermute | solution.py:449
  180.0 29.7 %all-to-all-done.1 = bf16[64,2,128,128]{3,2,1,0:T(8,128)(2,1)} async-done(((bf16[64,2,128,128]{3,2,1,0:T(8,128)(2,1)}), bf16[64,2,128,128]{3,2,1,0:T(8,128)(2,1)}, u32[]{:S(2)}, u32[]{:S(2)}) %all-to-all-start.1) | async-done | bytes 4194336 | tf_op jit(solution)/shard_map/all_to_all | solution.py:398
  209.8 18.3 %v_last.1 = bf16[2,8,8,64,128]{4,3,2,1,0:T(8,128)(2,1)} custom-call(s32[1]{0:T(128)} %bitcast.2.core_ref, s32[1]{0:T(128)} %bitcast.3.place_ref, s32[1]{0:T(128)} %get-tuple-element.37.w_ref, bf16[16,512,128]{2,1,0:T(8,128)(2,1)} %u_last.1._, bf16[8,8,2,128,128]{4,3,2,1,0:T(8,128)(2,1)} %bitcast.36.refs_0_, f32[8,1024]{1,0:T(8,128)} %constant.332.refs_1_, ...), custom_call_target="tpu_custom_call" | custom-call | flops 8589934592 | bytes 16777216 | tf_op jit(solution)/shard_map/v_last/pallas_call | solution.py:173
  228.1 2.3 collective-permute-done.11.refs_1_
  231.4 17.1 %all-to-all-start.2 = ((bf16[16,8,64,128]{3,2,1,0:T(8,128)(2,1)}), bf16[16,8,64,128]{3,2,1,0:T(8,128)(2,1)S(1)}, u32[]{:S(2)}, u32[]{:S(2)}) async-start(bf16[16,8,64,128]{3,2,1,0:T(8,128)(2,1)} %gate.5), calls=%async_computation.2 | async-start | bytes 4194304 | tf_op jit(solution)/shard_map/all_to_all | solution.py:398
  250.9 4.5 %collective-permute-start.15 = (bf16[512,128]{1,0:T(8,128)(2,1)S(1)}, bf16[512,128]{1,0:T(8,128)(2,1)S(1)}, u32[]{:S(2)}, u32[]{:S(2)}) collective-permute-start(bf16[512,128]{1,0:T(8,128)(2,1)S(1)} %get-tuple-element.32), channel_id=1, source_target_pairs={{0,4},{1,5},{2,6},{3,7},{4,0},{5,1},{6,2},{7,3},{8,12},{9,13},{10,... | collective-permute-start | bytes 393224 | tf_op jit(solution)/shard_map/ppermute | solution.py:378
  255.4 1.8 collective-permute-start.17
  261.9 4.1 %collective-permute-done.14.refs_3_ = bf16[512,128]{1,0:T(8,128)(2,1)S(1)} collective-permute-done((bf16[512,128]{1,0:T(8,128)(2,1)S(1)}, bf16[512,128]{1,0:T(8,128)(2,1)S(1)}, u32[]{:S(2)}, u32[]{:S(2)}) %collective-permute-start.14) | collective-permute-done | bytes 131104 | tf_op jit(solution)/shard_map/ppermute | solution.py:378
  266.2 9.6 %all-to-all-done.2 = bf16[16,8,64,128]{3,2,1,0:T(8,128)(2,1)S(1)} async-done(((bf16[16,8,64,128]{3,2,1,0:T(8,128)(2,1)}), bf16[16,8,64,128]{3,2,1,0:T(8,128)(2,1)S(1)}, u32[]{:S(2)}, u32[]{:S(2)}) %all-to-all-start.2) | async-done | bytes 2097184 | tf_op jit(solution)/shard_map/all_to_all | solution.py:398
  277.1 6.3 %arrange.1 = f32[8,64,1024]{2,1,0:T(8,128)} custom-call(s32[1]{0:T(128)} %bitcast.col_ref, bf16[512,128]{1,0:T(8,128)(2,1)} %get-tuple-element.36.refs_0_, bf16[512,128]{1,0:T(8,128)(2,1)} %copy-done.12, bf16[512,128]{1,0:T(8,128)(2,1)} %copy-done.13, bf16[512,128]{1,0:T(8,128)(2,1)} %copy-done.14, bf16[512,128]{1,0:T(8,128)(2,1)} %copy-done.15, ...), custom_call_target="tpu_custom_call" | custom-call | tf_op jit(solution)/shard_map/arrange/pallas_call | solution.py:324
  (75 shorter events, 24.3 us)
Async XLA Ops:
  1.7 4.4 %collective-permute-start = (bf16[4,128,2048]{2,1,0:T(8,128)(2,1)S(1)}, bf16[4,128,2048]{2,1,0:T(8,128)(2,1)}, u32[]{:S(2)}, u32[]{:S(2)}) collective-permute-start(bf16[4,128,2048]{2,1,0:T(8,128)(2,1)S(1)} %dynamic-slice_bitcast_fusion), channel_id=1, source_target_pairs={{0,1},{1,0},{2,3},{3,2},{4,5},{5,4},{6,7},{7,6},{8,9},{9,8},{10,11... | collective-permute-start | bytes 6291464 | tf_op jit(solution)/shard_map/ppermute | solution.py:419
  9.9 27.5 %collective-permute-start.2 = (bf16[2,128,2048]{2,1,0:T(8,128)(2,1)}, bf16[2,128,2048]{2,1,0:T(8,128)(2,1)}, u32[]{:S(2)}, u32[]{:S(2)}) collective-permute-start(bf16[2,128,2048]{2,1,0:T(8,128)(2,1)} %pad_maximum_fusion.3), channel_id=1, source_target_pairs={{0,2},{1,3},{2,4},{3,5},{4,6},{5,7},{6,0},{7,1},{8,10},{9,11},{10,... | collective-permute-start | bytes 3145736 | tf_op jit(solution)/shard_map/ppermute | solution.py:427
  11.7 25.8 %collective-permute-start.1 = (bf16[2,128,2048]{2,1,0:T(8,128)(2,1)S(1)}, bf16[2,128,2048]{2,1,0:T(8,128)(2,1)}, u32[]{:S(2)}, u32[]{:S(2)}) collective-permute-start(bf16[2,128,2048]{2,1,0:T(8,128)(2,1)S(1)} %pad_maximum_fusion.1.__), channel_id=1, source_target_pairs={{0,6},{1,7},{2,0},{3,1},{4,2},{5,3},{6,4},{7,5},{8,14},{9,15},{10,... | collective-permute-start | bytes 3145736 | tf_op jit(solution)/shard_map/ppermute | solution.py:427
  13.3 12.2 %copy-start.7 = (bf16[1,128,2048]{2,1,0:T(8,128)(2,1)S(1)}, bf16[1,128,2048]{2,1,0:T(8,128)(2,1)}, u32[]{:S(2)}) copy-start(bf16[1,128,2048]{2,1,0:T(8,128)(2,1)} %get-tuple-element.22) | copy-start | bytes 1572868
  18.2 16.1 %collective-permute-start.3 = (bf16[1024,256]{1,0:T(8,128)(2,1)}, bf16[1024,256]{1,0:T(8,128)(2,1)S(1)}, u32[]{:S(2)}, u32[]{:S(2)}) collective-permute-start(bf16[1024,256]{1,0:T(8,128)(2,1)} %get-tuple-element.13), channel_id=1, source_target_pairs={{0,8},{8,16},{16,24},{24,0},{32,40},{40,48},{48,56},{56,32},{1,9},... | collective-permute-start | bytes 1572872 | tf_op jit(solution)/shard_map/ppermute | solution.py:378
  20.3 14.1 %collective-permute-start.4 = (bf16[1024,256]{1,0:T(8,128)(2,1)}, bf16[1024,256]{1,0:T(8,128)(2,1)S(1)}, u32[]{:S(2)}, u32[]{:S(2)}) collective-permute-start(bf16[1024,256]{1,0:T(8,128)(2,1)} %get-tuple-element.14), channel_id=1, source_target_pairs={{0,24},{8,0},{16,8},{24,16},{32,56},{40,32},{48,40},{56,48},{1,25}... | collective-permute-start | bytes 1572872 | tf_op jit(solution)/shard_map/ppermute | solution.py:378
  22.5 14.9 %collective-permute-start.5 = (bf16[1024,256]{1,0:T(8,128)(2,1)}, bf16[1024,256]{1,0:T(8,128)(2,1)S(1)}, u32[]{:S(2)}, u32[]{:S(2)}) collective-permute-start(bf16[1024,256]{1,0:T(8,128)(2,1)} %get-tuple-element.15), channel_id=1, source_target_pairs={{0,32},{8,40},{16,48},{24,56},{32,0},{40,8},{48,16},{56,24},{1,33}... | collective-permute-start | bytes 1572872 | tf_op jit(solution)/shard_map/ppermute | solution.py:378
  27.7 12.9 %copy-start.18 = (s32[2]{0:T(128)S(1)}, s32[2]{0:T(128)}, u32[]{:S(2)}) copy-start(s32[2]{0:T(128)} %param.15) | copy-start | bytes 28
  38.2 25.3 %collective-permute-start.6 = (bf16[2,128,2048]{2,1,0:T(8,128)(2,1)}, bf16[2,128,2048]{2,1,0:T(8,128)(2,1)}, u32[]{:S(2)}, u32[]{:S(2)}) collective-permute-start(bf16[2,128,2048]{2,1,0:T(8,128)(2,1)} %gate.3), channel_id=1, source_target_pairs={{0,4},{1,5},{2,6},{3,7},{4,0},{5,1},{6,2},{7,3},{8,12},{9,13},{10,... | collective-permute-start | bytes 3145736 | tf_op jit(solution)/shard_map/ppermute | solution.py:427
  42.6 39.2 %collective-permute-start.10 = (bf16[1024,256]{1,0:T(8,128)(2,1)}, bf16[1024,256]{1,0:T(8,128)(2,1)S(1)}, u32[]{:S(2)}, u32[]{:S(2)}) collective-permute-start(bf16[1024,256]{1,0:T(8,128)(2,1)} %get-tuple-element.19), channel_id=1, source_target_pairs={{0,56},{8,32},{16,40},{24,48},{32,24},{40,0},{48,8},{56,16},{1,57}... | collective-permute-start | bytes 1572872 | tf_op jit(solution)/shard_map/ppermute | solution.py:378
  48.3 36.6 %collective-permute-start.7 = (bf16[1024,256]{1,0:T(8,128)(2,1)}, bf16[1024,256]{1,0:T(8,128)(2,1)S(1)}, u32[]{:S(2)}, u32[]{:S(2)}) collective-permute-start(bf16[1024,256]{1,0:T(8,128)(2,1)} %get-tuple-element.16), channel_id=1, source_target_pairs={{0,16},{8,24},{16,0},{24,8},{32,48},{40,56},{48,32},{56,40},{1,17}... | collective-permute-start | bytes 1572872 | tf_op jit(solution)/shard_map/ppermute | solution.py:378
  48.3 36.6 %collective-permute-start.8 = (bf16[1024,256]{1,0:T(8,128)(2,1)}, bf16[1024,256]{1,0:T(8,128)(2,1)S(1)}, u32[]{:S(2)}, u32[]{:S(2)}) collective-permute-start(bf16[1024,256]{1,0:T(8,128)(2,1)} %get-tuple-element.17), channel_id=1, source_target_pairs={{0,40},{8,48},{16,56},{24,32},{32,8},{40,16},{48,24},{56,0},{1,41}... | collective-permute-start | bytes 1572872 | tf_op jit(solution)/shard_map/ppermute | solution.py:378
  49.5 35.4 %collective-permute-start.9 = (bf16[1024,256]{1,0:T(8,128)(2,1)}, bf16[1024,256]{1,0:T(8,128)(2,1)S(1)}, u32[]{:S(2)}, u32[]{:S(2)}) collective-permute-start(bf16[1024,256]{1,0:T(8,128)(2,1)} %get-tuple-element.18), channel_id=1, source_target_pairs={{0,48},{8,56},{16,32},{24,40},{32,16},{40,24},{48,0},{56,8},{1,49}... | collective-permute-start | bytes 1572872 | tf_op jit(solution)/shard_map/ppermute | solution.py:378
  81.8 3.1 %copy-start.8 = (bf16[1024,256]{1,0:T(8,128)(2,1)}, bf16[1024,256]{1,0:T(8,128)(2,1)S(1)}, u32[]{:S(2)}) copy-start(bf16[1024,256]{1,0:T(8,128)(2,1)S(1)} %collective-permute-done.10.refs_7_) | copy-start | bytes 1572868
  86.7 58.9 %all-to-all-start = ((bf16[64,2,128,128]{3,2,1,0:T(8,128)(2,1)}), bf16[64,2,128,128]{3,2,1,0:T(8,128)(2,1)}, u32[]{:S(2)}, u32[]{:S(2)}) async-start(bf16[64,2,128,128]{3,2,1,0:T(8,128)(2,1)} %bitcast.63), calls=%async_computation | async-start | bytes 8388608 | tf_op jit(solution)/shard_map/all_to_all | solution.py:398
  145.6 64.2 %all-to-all-start.1 = ((bf16[64,2,128,128]{3,2,1,0:T(8,128)(2,1)}), bf16[64,2,128,128]{3,2,1,0:T(8,128)(2,1)}, u32[]{:S(2)}, u32[]{:S(2)}) async-start(bf16[64,2,128,128]{3,2,1,0:T(8,128)(2,1)} %bitcast.66), calls=%async_computation.1 | async-start | bytes 8388608 | tf_op jit(solution)/shard_map/all_to_all | solution.py:398
  176.1 54.3 %collective-permute-start.11 = (bf16[8,512,128]{2,1,0:T(8,128)(2,1)S(1)}, bf16[8,512,128]{2,1,0:T(8,128)(2,1)S(1)}, u32[]{:S(2)}, u32[]{:S(2)}) collective-permute-start(bf16[8,512,128]{2,1,0:T(8,128)(2,1)S(1)} %dynamic-slice_bitcast_fusion.1), channel_id=1, source_target_pairs={{0,64},{64,0},{1,65},{65,1},{2,66},{66,2},{3,67},{67,3},{4,68},{68... | collective-permute-start | bytes 3145736 | tf_op jit(solution)/shard_map/ppermute | solution.py:449
  231.4 17.2 %copy-start.3 = (bf16[8,512,128]{2,1,0:T(8,128)(2,1)S(1)}, bf16[8,512,128]{2,1,0:T(8,128)(2,1)}, u32[]{:S(2)}) copy-start(bf16[8,512,128]{2,1,0:T(8,128)(2,1)} %copy-done.2) | copy-start | bytes 3145732
  231.4 44.4 %all-to-all-start.2 = ((bf16[16,8,64,128]{3,2,1,0:T(8,128)(2,1)}), bf16[16,8,64,128]{3,2,1,0:T(8,128)(2,1)S(1)}, u32[]{:S(2)}, u32[]{:S(2)}) async-start(bf16[16,8,64,128]{3,2,1,0:T(8,128)(2,1)} %gate.5), calls=%async_computation.2 | async-start | bytes 4194304 | tf_op jit(solution)/shard_map/all_to_all | solution.py:398
  250.8 4.5 %collective-permute-start.12 = (bf16[512,128]{1,0:T(8,128)(2,1)S(1)}, bf16[512,128]{1,0:T(8,128)(2,1)S(1)}, u32[]{:S(2)}, u32[]{:S(2)}) collective-permute-start(bf16[512,128]{1,0:T(8,128)(2,1)S(1)} %get-tuple-element.35), channel_id=1, source_target_pairs={{0,1},{1,0},{2,3},{3,2},{4,5},{5,4},{6,7},{7,6},{8,9},{9,8},{10,11... | collective-permute-start | bytes 393224 | tf_op jit(solution)/shard_map/ppermute | solution.py:378
  250.9 7.5 %collective-permute-start.13 = (bf16[512,128]{1,0:T(8,128)(2,1)S(1)}, bf16[512,128]{1,0:T(8,128)(2,1)S(1)}, u32[]{:S(2)}, u32[]{:S(2)}) collective-permute-start(bf16[512,128]{1,0:T(8,128)(2,1)S(1)} %get-tuple-element.34), channel_id=1, source_target_pairs={{0,2},{1,3},{2,4},{3,5},{4,6},{5,7},{6,0},{7,1},{8,10},{9,11},{10,... | collective-permute-start | bytes 393224 | tf_op jit(solution)/shard_map/ppermute | solution.py:378
  250.9 15.2 %collective-permute-start.14 = (bf16[512,128]{1,0:T(8,128)(2,1)S(1)}, bf16[512,128]{1,0:T(8,128)(2,1)S(1)}, u32[]{:S(2)}, u32[]{:S(2)}) collective-permute-start(bf16[512,128]{1,0:T(8,128)(2,1)S(1)} %get-tuple-element.33), channel_id=1, source_target_pairs={{0,3},{1,2},{2,5},{3,4},{4,7},{5,6},{6,1},{7,0},{8,11},{9,10},{10,... | collective-permute-start | bytes 393224 | tf_op jit(solution)/shard_map/ppermute | solution.py:378
  250.9 15.2 %collective-permute-start.15 = (bf16[512,128]{1,0:T(8,128)(2,1)S(1)}, bf16[512,128]{1,0:T(8,128)(2,1)S(1)}, u32[]{:S(2)}, u32[]{:S(2)}) collective-permute-start(bf16[512,128]{1,0:T(8,128)(2,1)S(1)} %get-tuple-element.32), channel_id=1, source_target_pairs={{0,4},{1,5},{2,6},{3,7},{4,0},{5,1},{6,2},{7,3},{8,12},{9,13},{10,... | collective-permute-start | bytes 393224 | tf_op jit(solution)/shard_map/ppermute | solution.py:378
  255.4 10.6 %collective-permute-start.16 = (bf16[512,128]{1,0:T(8,128)(2,1)S(1)}, bf16[512,128]{1,0:T(8,128)(2,1)S(1)}, u32[]{:S(2)}, u32[]{:S(2)}) collective-permute-start(bf16[512,128]{1,0:T(8,128)(2,1)S(1)} %get-tuple-element.31), channel_id=1, source_target_pairs={{0,5},{1,4},{2,7},{3,6},{4,1},{5,0},{6,3},{7,2},{8,13},{9,12},{10,... | collective-permute-start | bytes 393224 | tf_op jit(solution)/shard_map/ppermute | solution.py:378
  255.4 20.4 %copy-start.12 = (bf16[512,128]{1,0:T(8,128)(2,1)}, bf16[512,128]{1,0:T(8,128)(2,1)S(1)}, u32[]{:S(2)}) copy-start(bf16[512,128]{1,0:T(8,128)(2,1)S(1)} %collective-permute-done.12.refs_1_) | copy-start | bytes 393220
  255.4 10.6 %collective-permute-start.17 = (bf16[512,128]{1,0:T(8,128)(2,1)S(1)}, bf16[512,128]{1,0:T(8,128)(2,1)S(1)}, u32[]{:S(2)}, u32[]{:S(2)}) collective-permute-start(bf16[512,128]{1,0:T(8,128)(2,1)S(1)} %get-tuple-element.30), channel_id=1, source_target_pairs={{0,6},{1,7},{2,0},{3,1},{4,2},{5,3},{6,4},{7,5},{8,14},{9,15},{10,... | collective-permute-start | bytes 393224 | tf_op jit(solution)/shard_map/ppermute | solution.py:378
  258.4 17.4 %copy-start.13 = (bf16[512,128]{1,0:T(8,128)(2,1)}, bf16[512,128]{1,0:T(8,128)(2,1)S(1)}, u32[]{:S(2)}) copy-start(bf16[512,128]{1,0:T(8,128)(2,1)S(1)} %collective-permute-done.13.refs_2_) | copy-start | bytes 393220
  258.4 7.9 %collective-permute-start.18 = (bf16[512,128]{1,0:T(8,128)(2,1)S(1)}, bf16[512,128]{1,0:T(8,128)(2,1)}, u32[]{:S(2)}, u32[]{:S(2)}) collective-permute-start(bf16[512,128]{1,0:T(8,128)(2,1)S(1)} %get-tuple-element.29), channel_id=1, source_target_pairs={{0,7},{1,6},{2,1},{3,0},{4,3},{5,2},{6,5},{7,4},{8,15},{9,14},{10,... | collective-permute-start | bytes 393224 | tf_op jit(solution)/shard_map/ppermute | solution.py:378
  266.0 9.8 %copy-start.14 = (bf16[512,128]{1,0:T(8,128)(2,1)}, bf16[512,128]{1,0:T(8,128)(2,1)S(1)}, u32[]{:S(2)}) copy-start(bf16[512,128]{1,0:T(8,128)(2,1)S(1)} %collective-permute-done.14.refs_3_) | copy-start | bytes 393220
  266.0 9.8 %copy-start.15 = (bf16[512,128]{1,0:T(8,128)(2,1)}, bf16[512,128]{1,0:T(8,128)(2,1)S(1)}, u32[]{:S(2)}) copy-start(bf16[512,128]{1,0:T(8,128)(2,1)S(1)} %collective-permute-done.15.refs_4_) | copy-start | bytes 393220
  266.0 9.8 %copy-start.16 = (bf16[512,128]{1,0:T(8,128)(2,1)}, bf16[512,128]{1,0:T(8,128)(2,1)S(1)}, u32[]{:S(2)}) copy-start(bf16[512,128]{1,0:T(8,128)(2,1)S(1)} %collective-permute-done.16.refs_5_) | copy-start | bytes 393220
  266.0 9.8 %copy-start.17 = (bf16[512,128]{1,0:T(8,128)(2,1)}, bf16[512,128]{1,0:T(8,128)(2,1)S(1)}, u32[]{:S(2)}) copy-start(bf16[512,128]{1,0:T(8,128)(2,1)S(1)} %collective-permute-done.17.refs_6_) | copy-start | bytes 393220
  (9 other events, 13.5 us)
